TPU v7x, 128 devices: a whole 4x4x4 slice. The times are simulated.
128 devices in a mesh: space: 32 (over z, y, core), slab: 4 (over x).
Axes of the slice: x: 4, y: 4, z: 4, core: 2. Of those that a mesh axis runs over, the one named last changes fastest.
Arguments:
- features: float32 [512, 8, 8, 512], P(('space', 'slab')), may hold values from -6 to 6
- live: int32 [128], P(('space', 'slab')), may hold values from 1 to 4, as said below
- rim_slots: int32 [128, 2], P(('space', 'slab')), may hold values from 0 to 3, as said below
- neighbours: int32 [512, 26], P(('space', 'slab')), may hold values from 0 to 12, as said below
- weights: float32 [4, 27, 4096], replicated, may hold values from -0.15625 to 0.15625
- biases: float32 [4, 64], replicated, may hold values from -3 to 3
Outputs:
- output: float32 [512, 8, 8, 512], P(('space', 'slab'))
Inputs may be any that keep to these rules, and one draw needn't show every extreme that they name: `live`: devices whose space indices differ by 32 / 2 (same slab index) hold at most 6 occupied bricks together; in every draw some pair holds exactly that and some device holds 4. `rim_slots`: every entry is below its device's live count. `neighbours`: entries below 4 are below the device's live count.
All inputs are finite; a program needn't handle non-finite values.
Results may differ from a plain program's by a relative error of at most 0.0003.
Values sent between devices are 32-bit elements; how exact they have to be, the bound alone decides.
No kernel may reach another device: no remote copies, remote signals or barrier semaphores. Data moves between devices by JAX's collectives and lax.ppermute only.
A program may use at most 128 MiB of HBM per device.

v0:
```python
import jax
import jax.numpy as jnp
from jax import lax
from jax.sharding import PartitionSpec as P


def padded_2(array, sides, width):
    edges = {}
    for axis, dim in sides:
        size, length = (lax.axis_size(axis), array.shape[dim])
        up = [(i, (i + 1) % size) for i in range(size - 1)]
        last = lax.slice_in_dim(array, length - width, length, axis=dim)
        first = lax.slice_in_dim(array, 0, width, axis=dim)
        edges[dim] = (
            lax.ppermute(last, axis, up),
            lax.ppermute(first, axis, [(b, a) for a, b in up]),
        )
    done = []
    for _, dim in sides:
        low, high = edges[dim]
        around = [(width, width) if d in done else (0, 0) for d in range(array.ndim)]
        array = jnp.concatenate([jnp.pad(low, around), array, jnp.pad(high, around)], axis=dim)
        done.append(dim)
    return array


def direction_list():
    result = []
    for ddx in (-1, 0, 1):
        for ddy in (-1, 0, 1):
            for ddz in (-1, 0, 1):
                if (ddx, ddy, ddz) != (0, 0, 0):
                    result.append((ddx, ddy, ddz))
    return result


def source_index(step):
    if step == -1:
        return 7
    if step == 1:
        return 0
    return slice(0, 8)


def extent(step):
    return 8 if step == 0 else 1


def faces_of(field):
    count = field.shape[0]
    channels = field.shape[-1] // 8
    xfaces = jnp.stack([field[:, 0], field[:, 7]], 1)
    yfaces = jnp.stack([field[:, :, 0], field[:, :, 7]], 1)
    cube = field.reshape(count, 8, 8, 8, channels)
    zfaces = jnp.stack([cube[:, :, :, 0], cube[:, :, :, 7]], 1).reshape(count, 2, 8, 8 * channels)
    return jnp.stack([xfaces, yfaces, zfaces], 1)


def face_piece(facetab, direction):
    ddx, ddy, ddz = direction
    count = facetab.shape[0]
    channels = facetab.shape[-1] // 8
    if ddx != 0:
        plane = facetab[:, 0, 1 if ddx == -1 else 0].reshape(count, 8, 8, channels)
        return plane[:, source_index(ddy), source_index(ddz)]
    if ddy != 0:
        plane = facetab[:, 1, 1 if ddy == -1 else 0].reshape(count, 8, 8, channels)
        return plane[:, source_index(ddx), source_index(ddz)]
    plane = facetab[:, 2, 1 if ddz == -1 else 0].reshape(count, 8, 8, channels)
    return plane


def assemble(center, table, nbr, getter):
    count = center.shape[0]
    channels = center.shape[-1] // 8
    blocks = {(0, 0, 0): center.reshape(count, 8, 8, 8, channels)}
    for jdir, direction in enumerate(direction_list()):
        piece = getter(table, direction)[nbr[:, jdir]]
        blocks[direction] = piece.reshape(
            count, extent(direction[0]), extent(direction[1]), extent(direction[2]), channels
        )
    slabs = []
    for ddx in (-1, 0, 1):
        rows = []
        for ddy in (-1, 0, 1):
            rows.append(jnp.concatenate([blocks[ddx, ddy, ddz] for ddz in (-1, 0, 1)], 3))
        slabs.append(jnp.concatenate(rows, 2))
    return jnp.concatenate(slabs, 1)


def convolve(padded, kernel):
    count = padded.shape[0]
    channels = padded.shape[-1]
    taps = kernel.reshape(3, 3, 3, channels, channels)
    result = lax.conv_general_dilated(
        padded,
        taps,
        (1, 1, 1),
        "VALID",
        dimension_numbers=("NDHWC", "DHWIO", "NDHWC"),
        precision=lax.Precision.HIGHEST,
        preferred_element_type=jnp.float32,
    )
    return result.reshape(count, 8, 8, 8 * channels)


def gather_margins(field, slots, nbr):
    own_faces = faces_of(field)
    offered = own_faces[slots][None, None]
    arrived = padded_2(offered, (("space", 0), ("slab", 1)), 1)
    table = jnp.concatenate(
        [
            own_faces,
            arrived[0, 1],
            arrived[2, 1],
            arrived[1, 0],
            arrived[1, 2],
            jnp.zeros_like(own_faces[:1]),
        ],
        0,
    )
    return assemble(field, table, nbr, face_piece)


def shards(features, live, rim_slots, neighbours, weights, biases):
    slots_all = features.shape[0]
    count = live[0]
    mask = (jnp.arange(slots_all, dtype=jnp.int32) < count).astype(jnp.float32)[:, None, None, None]
    slots = rim_slots[0]

    def layer(field, kidx):
        padded = gather_margins(field, slots, neighbours)
        return convolve(padded, weights[kidx])

    field = features * mask
    for blk in range(weights.shape[0] // 2):
        first = 2 * blk
        hidden = jax.nn.relu(layer(field, first) + jnp.tile(biases[first], 8)) * mask
        field = (
            jax.nn.relu(field + layer(hidden, first + 1) + jnp.tile(biases[first + 1], 8)) * mask
        )
    return field


def solution(mesh):
    in_specs = (
        P(("space", "slab"), None, None, None),
        P(("space", "slab")),
        P(("space", "slab"), None),
        P(("space", "slab"), None),
        P(),
        P(),
    )
    out_specs = P(("space", "slab"), None, None, None)
    return jax.shard_map(shards, mesh=mesh, in_specs=in_specs, out_specs=out_specs, check_vma=False)
```

profile of v0, /device:TPU:96, one launch (start us, length us, event | category | flops | bytes accessed | tf_op | source)
XLA Modules:
  0.0 325.1 jit_solution(16543068948415808232)
XLA Ops:
  4.5 2.1 collective-permute-start
  6.6 5.8 %collective-permute-start.1 = (f32[1,1,2,3,2,8,512]{6,5,4,3,2,1,0:T(8,128)S(1)}, f32[1,1,2,3,2,8,512]{6,5,4,3,2,1,0:T(8,128)}, u32[]{:S(2)}, u32[]{:S(2)}) collective-permute-start(f32[1,1,2,3,2,8,512]{6,5,4,3,2,1,0:T(8,128)S(1)} %bitcast.711), channel_id=1, source_target_pairs={{4,0},{8,4},{12,8},{16,12},{20,16},{24,20},{28,24},{32,28},{36,32}... | collective-permute-start | bytes 589832 | tf_op jit(solution)/shard_map/ppermute | solution.py:16
  12.4 3.4 %collective-permute-start.2 = (f32[1,1,2,3,2,8,512]{6,5,4,3,2,1,0:T(8,128)S(1)}, f32[1,1,2,3,2,8,512]{6,5,4,3,2,1,0:T(8,128)S(1)}, u32[]{:S(2)}, u32[]{:S(2)}) collective-permute-start(f32[1,1,2,3,2,8,512]{6,5,4,3,2,1,0:T(8,128)S(1)} %bitcast.712), channel_id=1, source_target_pairs={{0,1},{1,2},{2,3},{4,5},{5,6},{6,7},{8,9},{9,10},{10,11},{12,13},{... | collective-permute-start | bytes 589832 | tf_op jit(solution)/shard_map/ppermute | solution.py:15
  18.0 1.7 copy.40
  20.3 5.6 %slice_reduce_fusion.1 = (f32[27,4096]{1,0:T(8,128)}, f32[27,4096]{1,0:T(8,128)S(1)}, f32[27,4096]{1,0:T(8,128)S(1)}, f32[27,4096]{1,0:T(8,128)}) fusion(f32[4,27,4096]{2,0,1:T(4,128)S(1)} %copy-done.5), kind=kLoop, calls=%fused_computation.332 | loop fusion | bytes 3538944 | tf_op jit(solution)/shard_map/slice | solution.py:133
  57.4 1.5 gather_fusion.2
  59.6 1.5 gather_fusion.6
  61.1 1.5 gather_fusion.4
  69.0 26.0 %maximum_multiply_fusion.1 = (f32[4,8,8,8,64]{4,0,3,2,1:T(4,128)}, f32[4,8,8,8,64]{4,0,3,2,1:T(4,128)S(1)}) fusion(f32[4]{0:T(128)S(1)} %compare_convert_fusion, f32[64]{0:T(128)} %copy-done.32, f32[3,3,3,64,64]{4,3,2,1,0:T(8,128)} %reshape_squeeze.62, f32[4,1,1,1,64]{4,0,3,2,1:T(4,128)S(1)} %bitcast.878, f32[4,1,1,8,64]{4,0,3,2,1:T(4,128)S(1)} %bitcast.825, ...), kind=kOutput, calls=%fused_computation.325 | convolution fusion | flops 2724958208 | bytes 2515216 | tf_op jit(solution)/shard_map/conv_general_dilated | solution.py:95
  98.1 1.9 collective-permute-start.4
  100.5 5.7 %collective-permute-start.5 = (f32[1,1,2,3,2,8,512]{6,5,2,4,3,1,0:T(8,128)S(1)}, f32[1,1,2,3,2,8,512]{6,5,2,4,3,1,0:T(8,128)S(1)}, u32[]{:S(2)}, u32[]{:S(2)}) collective-permute-start(f32[1,1,2,3,2,8,512]{6,5,2,4,3,1,0:T(8,128)S(1)} %bitcast.719), channel_id=1, source_target_pairs={{4,0},{8,4},{12,8},{16,12},{20,16},{24,20},{28,24},{32,28},{36,32}... | collective-permute-start | bytes 589832 | tf_op jit(solution)/shard_map/ppermute | solution.py:16
  106.2 4.6 %collective-permute-start.6 = (f32[1,1,2,3,2,8,512]{6,5,2,4,3,1,0:T(8,128)S(1)}, f32[1,1,2,3,2,8,512]{6,5,2,4,3,1,0:T(8,128)S(1)}, u32[]{:S(2)}, u32[]{:S(2)}) collective-permute-start(f32[1,1,2,3,2,8,512]{6,5,2,4,3,1,0:T(8,128)S(1)} %bitcast.720), channel_id=1, source_target_pairs={{0,1},{1,2},{2,3},{4,5},{5,6},{6,7},{8,9},{9,10},{10,11},{12,13},{... | collective-permute-start | bytes 589832 | tf_op jit(solution)/shard_map/ppermute | solution.py:15
  112.4 1.6 collective-permute-done.6
  114.0 4.4 %collective-permute-done.7 = f32[1,1,2,3,2,8,512]{6,5,2,4,3,1,0:T(8,128)S(1)} collective-permute-done((f32[1,1,2,3,2,8,512]{6,5,2,4,3,1,0:T(8,128)S(1)}, f32[1,1,2,3,2,8,512]{6,5,2,4,3,1,0:T(8,128)S(1)}, u32[]{:S(2)}, u32[]{:S(2)}) %collective-permute-start.7) | collective-permute-done | bytes 196640 | tf_op jit(solution)/shard_map/ppermute | solution.py:16
  138.2 25.0 %fusion.54 = f32[4,8,8,8,64]{4,0,3,2,1:T(4,128)S(1)} fusion(f32[3,3,3,64,64]{4,3,2,1,0:T(8,128)S(1)} %reshape_squeeze.69, f32[4,1,1,1,64]{4,0,3,2,1:T(4,128)S(1)} %bitcast.881, f32[4,1,1,8,64]{4,0,3,2,1:T(4,128)S(1)} %bitcast.845, f32[4,1,1,1,64]{4,0,3,2,1:T(4,128)S(1)} %bitcast.864, f32[4,1,8,1,64]{4,0,3,2,1:T(4,128)S(1)} %bitcast.816, ...), kind=kOutput, calls=%fused_computation.162 | convolution fusion | flops 2724564992 | bytes 1990656 | tf_op jit(solution)/shard_map/conv_general_dilated | solution.py:95
  168.5 1.9 collective-permute-start.8
  172.4 5.7 %collective-permute-start.9 = (f32[1,1,2,3,2,8,512]{6,5,2,4,3,1,0:T(8,128)}, f32[1,1,2,3,2,8,512]{6,5,2,4,3,1,0:T(8,128)S(1)}, u32[]{:S(2)}, u32[]{:S(2)}) collective-permute-start(f32[1,1,2,3,2,8,512]{6,5,2,4,3,1,0:T(8,128)} %bitcast.609), channel_id=1, source_target_pairs={{4,0},{8,4},{12,8},{16,12},{20,16},{24,20},{28,24},{32,28},{36,32}... | collective-permute-start | bytes 589832 | tf_op jit(solution)/shard_map/ppermute | solution.py:16
  178.1 3.4 %collective-permute-start.10 = (f32[1,1,2,3,2,8,512]{6,5,2,4,3,1,0:T(8,128)}, f32[1,1,2,3,2,8,512]{6,5,2,4,3,1,0:T(8,128)S(1)}, u32[]{:S(2)}, u32[]{:S(2)}) collective-permute-start(f32[1,1,2,3,2,8,512]{6,5,2,4,3,1,0:T(8,128)} %bitcast.609), channel_id=1, source_target_pairs={{0,1},{1,2},{2,3},{4,5},{5,6},{6,7},{8,9},{9,10},{10,11},{12,13},{... | collective-permute-start | bytes 589832 | tf_op jit(solution)/shard_map/ppermute | solution.py:15
  185.0 4.3 %collective-permute-done.11 = f32[1,1,2,3,2,8,512]{6,5,2,4,3,1,0:T(8,128)S(1)} collective-permute-done((f32[1,1,2,3,2,8,512]{6,5,2,4,3,1,0:T(8,128)}, f32[1,1,2,3,2,8,512]{6,5,2,4,3,1,0:T(8,128)S(1)}, u32[]{:S(2)}, u32[]{:S(2)}) %collective-permute-start.11) | collective-permute-done | bytes 196640 | tf_op jit(solution)/shard_map/ppermute | solution.py:16
  205.5 1.5 gather_fusion.75
  207.0 1.5 gather_fusion.73
  208.5 1.5 gather_fusion.71
  216.8 1.5 gather_fusion.62
  221.7 1.5 gather_fusion.60
  223.2 1.5 gather_fusion.58
  230.2 25.8 %maximum_multiply_fusion = (f32[4,8,8,8,64]{4,0,3,2,1:T(4,128)}, f32[4,8,8,8,64]{4,0,3,2,1:T(4,128)S(1)}) fusion(f32[64]{0:T(128)} %get-tuple-element.174, f32[4]{0:T(128)S(1)} %copy-done.23, f32[3,3,3,64,64]{4,3,2,1,0:T(8,128)S(1)} %copy-done.8, f32[4,1,1,1,64]{4,0,3,2,1:T(4,128)S(1)} %bitcast.879, f32[4,1,1,8,64]{4,0,3,2,1:T(4,128)S(1)} %bitcast.843, ...), kind=kOutput, calls=%fused_computation.324 | convolution fusion | flops 2724958208 | bytes 2515216 | tf_op jit(solution)/shard_map/conv_general_dilated | solution.py:95
  259.2 1.9 collective-permute-start.12
  261.5 5.7 %collective-permute-start.13 = (f32[1,1,2,3,2,8,512]{6,5,2,4,3,1,0:T(8,128)S(1)}, f32[1,1,2,3,2,8,512]{6,5,2,4,3,1,0:T(8,128)S(1)}, u32[]{:S(2)}, u32[]{:S(2)}) collective-permute-start(f32[1,1,2,3,2,8,512]{6,5,2,4,3,1,0:T(8,128)S(1)} %bitcast.715), channel_id=1, source_target_pairs={{4,0},{8,4},{12,8},{16,12},{20,16},{24,20},{28,24},{32,28},{36,32}... | collective-permute-start | bytes 589832 | tf_op jit(solution)/shard_map/ppermute | solution.py:16
  267.3 3.1 collective-permute-start.14
  271.8 1.8 collective-permute-done.14
  273.6 4.4 %collective-permute-done.15 = f32[1,1,2,3,2,8,512]{6,5,2,4,3,1,0:T(8,128)S(1)} collective-permute-done((f32[1,1,2,3,2,8,512]{6,5,2,4,3,1,0:T(8,128)S(1)}, f32[1,1,2,3,2,8,512]{6,5,2,4,3,1,0:T(8,128)S(1)}, u32[]{:S(2)}, u32[]{:S(2)}) %collective-permute-start.15) | collective-permute-done | bytes 196640 | tf_op jit(solution)/shard_map/ppermute | solution.py:16
  297.8 24.7 %fusion.162 = f32[4,8,8,8,64]{4,0,3,2,1:T(4,128)S(1)} fusion(f32[3,3,3,64,64]{4,3,2,1,0:T(8,128)S(1)} %reshape_squeeze.83, f32[4,1,1,1,64]{4,0,3,2,1:T(4,128)S(1)} %bitcast.880, f32[4,1,1,8,64]{4,0,3,2,1:T(4,128)S(1)} %bitcast.838, f32[4,1,1,1,64]{4,0,3,2,1:T(4,128)S(1)} %bitcast.866, f32[4,1,8,1,64]{4,0,3,2,1:T(4,128)S(1)} %bitcast.810, ...), kind=kOutput, calls=%fused_computation.270 | convolution fusion | flops 2724564992 | bytes 1990656 | tf_op jit(solution)/shard_map/conv_general_dilated | solution.py:95
  (467 shorter events, 137.6 us)
Async XLA Ops:
  0.7 163.0 %copy-start.22 = (f32[4]{0:T(128)}, f32[4]{0:T(128)S(1)}, u32[]{:S(2)}) copy-start(f32[4]{0:T(128)S(1)} %compare_convert_fusion) | copy-start | bytes 52
  2.9 14.4 %copy-start.6 = (s32[4,26]{1,0:T(4,128)S(1)}, s32[4,26]{1,0:T(4,128)}, u32[]{:S(2)}) copy-start(s32[4,26]{1,0:T(4,128)} %param.9) | copy-start | bytes 1252
  3.9 8.5 %copy-start.25 = (s32[1024]{0:T(1024)}, s32[1024]{0:T(1024)S(1)}, u32[]{:S(2)}) copy-start(s32[1024]{0:T(1024)S(1)} %pad_clamp_fusion.26) | copy-start | bytes 12292
  3.9 15.8 %copy-start.28 = (f32[4,64]{1,0:T(4,128)S(1)}, f32[4,64]{1,0:T(4,128)}, u32[]{:S(2)}) copy-start(f32[4,64]{1,0:T(4,128)} %param.11) | copy-start | bytes 3076
  4.5 15.8 %copy-start.5 = (f32[4,27,4096]{2,0,1:T(4,128)S(1)}, f32[4,27,4096]{2,0,1:T(4,128)}, u32[]{:S(2)}) copy-start(f32[4,27,4096]{2,0,1:T(4,128)} %param.10) | copy-start | bytes 5308420
  4.5 31.1 %collective-permute-start = (f32[1,1,2,3,2,8,512]{6,5,4,3,2,1,0:T(8,128)S(1)}, f32[1,1,2,3,2,8,512]{6,5,4,3,2,1,0:T(8,128)}, u32[]{:S(2)}, u32[]{:S(2)}) collective-permute-start(f32[1,1,2,3,2,8,512]{6,5,4,3,2,1,0:T(8,128)S(1)} %bitcast.710), channel_id=1, source_target_pairs={{0,4},{4,8},{8,12},{12,16},{16,20},{20,24},{24,28},{28,32},{32,36}... | collective-permute-start | bytes 589832 | tf_op jit(solution)/shard_map/ppermute | solution.py:15
  6.6 30.0 %collective-permute-start.1 = (f32[1,1,2,3,2,8,512]{6,5,4,3,2,1,0:T(8,128)S(1)}, f32[1,1,2,3,2,8,512]{6,5,4,3,2,1,0:T(8,128)}, u32[]{:S(2)}, u32[]{:S(2)}) collective-permute-start(f32[1,1,2,3,2,8,512]{6,5,4,3,2,1,0:T(8,128)S(1)} %bitcast.711), channel_id=1, source_target_pairs={{4,0},{8,4},{12,8},{16,12},{20,16},{24,20},{28,24},{32,28},{36,32}... | collective-permute-start | bytes 589832 | tf_op jit(solution)/shard_map/ppermute | solution.py:16
  12.4 25.2 %collective-permute-start.2 = (f32[1,1,2,3,2,8,512]{6,5,4,3,2,1,0:T(8,128)S(1)}, f32[1,1,2,3,2,8,512]{6,5,4,3,2,1,0:T(8,128)S(1)}, u32[]{:S(2)}, u32[]{:S(2)}) collective-permute-start(f32[1,1,2,3,2,8,512]{6,5,4,3,2,1,0:T(8,128)S(1)} %bitcast.712), channel_id=1, source_target_pairs={{0,1},{1,2},{2,3},{4,5},{5,6},{6,7},{8,9},{9,10},{10,11},{12,13},{... | collective-permute-start | bytes 589832 | tf_op jit(solution)/shard_map/ppermute | solution.py:15
  15.8 21.8 %collective-permute-start.3 = (f32[1,1,2,3,2,8,512]{6,5,4,3,2,1,0:T(8,128)S(1)}, f32[1,1,2,3,2,8,512]{6,5,4,3,2,1,0:T(8,128)S(1)}, u32[]{:S(2)}, u32[]{:S(2)}) collective-permute-start(f32[1,1,2,3,2,8,512]{6,5,4,3,2,1,0:T(8,128)S(1)} %bitcast.713), channel_id=1, source_target_pairs={{1,0},{2,1},{3,2},{5,4},{6,5},{7,6},{9,8},{10,9},{11,10},{13,12},{... | collective-permute-start | bytes 589832 | tf_op jit(solution)/shard_map/ppermute | solution.py:16
  38.5 9.8 %copy-start.10 = (f32[13,1,1,8,512]{4,3,2,1,0:T(8,128)S(1)}, f32[13,1,1,8,512]{4,3,2,1,0:T(8,128)}, u32[]{:S(2)}) copy-start(f32[13,1,1,8,512]{4,3,2,1,0:T(8,128)} %get-tuple-element.59) | copy-start | bytes 638980
  55.3 8.1 %copy-start.18 = (f32[13,1,1,64]{3,2,1,0:T(1,128)S(1)}, f32[13,1,1,64]{3,2,1,0:T(1,128)}, u32[]{:S(2)}) copy-start(f32[13,1,1,64]{3,2,1,0:T(1,128)} %get-tuple-element.145) | copy-start | bytes 9988
  55.3 9.5 %copy-start.16 = (f32[13,1,1,64]{3,2,1,0:T(1,128)S(1)}, f32[13,1,1,64]{3,2,1,0:T(1,128)}, u32[]{:S(2)}) copy-start(f32[13,1,1,64]{3,2,1,0:T(1,128)} %get-tuple-element.155) | copy-start | bytes 9988
  55.3 9.5 %copy-start.17 = (f32[13,1,1,64]{3,2,1,0:T(1,128)S(1)}, f32[13,1,1,64]{3,2,1,0:T(1,128)}, u32[]{:S(2)}) copy-start(f32[13,1,1,64]{3,2,1,0:T(1,128)} %get-tuple-element.156) | copy-start | bytes 9988
  55.3 11.5 %copy-start.15 = (f32[13,1,1,64]{3,2,1,0:T(1,128)S(1)}, f32[13,1,1,64]{3,2,1,0:T(1,128)}, u32[]{:S(2)}) copy-start(f32[13,1,1,64]{3,2,1,0:T(1,128)} %get-tuple-element.144) | copy-start | bytes 9988
  55.4 13.5 %copy-start.7 = (f32[4,8,8,8,64]{4,0,3,2,1:T(4,128)S(1)}, f32[4,8,8,8,64]{4,0,3,2,1:T(4,128)}, u32[]{:S(2)}) copy-start(f32[4,8,8,8,64]{4,0,3,2,1:T(4,128)} %copy.40) | copy-start | bytes 1572868
  55.5 13.5 %copy-start.20 = (f32[4,8,64]{2,0,1:T(4,128)S(1)}, f32[4,8,64]{2,0,1:T(4,128)}, u32[]{:S(2)}) copy-start(f32[4,8,64]{2,0,1:T(4,128)} %copy.456) | copy-start | bytes 24580
  55.5 13.5 %copy-start.21 = (f32[4,8,64]{2,0,1:T(4,128)S(1)}, f32[4,8,64]{2,0,1:T(4,128)}, u32[]{:S(2)}) copy-start(f32[4,8,64]{2,0,1:T(4,128)} %copy.457) | copy-start | bytes 24580
  98.1 14.2 %collective-permute-start.4 = (f32[1,1,2,3,2,8,512]{6,5,2,4,3,1,0:T(8,128)S(1)}, f32[1,1,2,3,2,8,512]{6,5,2,4,3,1,0:T(8,128)S(1)}, u32[]{:S(2)}, u32[]{:S(2)}) collective-permute-start(f32[1,1,2,3,2,8,512]{6,5,2,4,3,1,0:T(8,128)S(1)} %bitcast.718), channel_id=1, source_target_pairs={{0,4},{4,8},{8,12},{12,16},{16,20},{20,24},{24,28},{28,32},{32,36}... | collective-permute-start | bytes 589832 | tf_op jit(solution)/shard_map/ppermute | solution.py:15
  100.5 11.8 %collective-permute-start.5 = (f32[1,1,2,3,2,8,512]{6,5,2,4,3,1,0:T(8,128)S(1)}, f32[1,1,2,3,2,8,512]{6,5,2,4,3,1,0:T(8,128)S(1)}, u32[]{:S(2)}, u32[]{:S(2)}) collective-permute-start(f32[1,1,2,3,2,8,512]{6,5,2,4,3,1,0:T(8,128)S(1)} %bitcast.719), channel_id=1, source_target_pairs={{4,0},{8,4},{12,8},{16,12},{20,16},{24,20},{28,24},{32,28},{36,32}... | collective-permute-start | bytes 589832 | tf_op jit(solution)/shard_map/ppermute | solution.py:16
  106.2 7.7 %collective-permute-start.6 = (f32[1,1,2,3,2,8,512]{6,5,2,4,3,1,0:T(8,128)S(1)}, f32[1,1,2,3,2,8,512]{6,5,2,4,3,1,0:T(8,128)S(1)}, u32[]{:S(2)}, u32[]{:S(2)}) collective-permute-start(f32[1,1,2,3,2,8,512]{6,5,2,4,3,1,0:T(8,128)S(1)} %bitcast.720), channel_id=1, source_target_pairs={{0,1},{1,2},{2,3},{4,5},{5,6},{6,7},{8,9},{9,10},{10,11},{12,13},{... | collective-permute-start | bytes 589832 | tf_op jit(solution)/shard_map/ppermute | solution.py:15
  110.8 7.6 %collective-permute-start.7 = (f32[1,1,2,3,2,8,512]{6,5,2,4,3,1,0:T(8,128)S(1)}, f32[1,1,2,3,2,8,512]{6,5,2,4,3,1,0:T(8,128)S(1)}, u32[]{:S(2)}, u32[]{:S(2)}) collective-permute-start(f32[1,1,2,3,2,8,512]{6,5,2,4,3,1,0:T(8,128)S(1)} %bitcast.721), channel_id=1, source_target_pairs={{1,0},{2,1},{3,2},{5,4},{6,5},{7,6},{9,8},{10,9},{11,10},{13,12},{... | collective-permute-start | bytes 589832 | tf_op jit(solution)/shard_map/ppermute | solution.py:16
  168.5 15.0 %collective-permute-start.8 = (f32[1,1,2,3,2,8,512]{6,5,2,4,3,1,0:T(8,128)}, f32[1,1,2,3,2,8,512]{6,5,2,4,3,1,0:T(8,128)}, u32[]{:S(2)}, u32[]{:S(2)}) collective-permute-start(f32[1,1,2,3,2,8,512]{6,5,2,4,3,1,0:T(8,128)} %bitcast.609), channel_id=1, source_target_pairs={{0,4},{4,8},{8,12},{12,16},{16,20},{20,24},{24,28},{28,32},{32,36}... | collective-permute-start | bytes 589832 | tf_op jit(solution)/shard_map/ppermute | solution.py:15
  172.4 12.1 %collective-permute-start.9 = (f32[1,1,2,3,2,8,512]{6,5,2,4,3,1,0:T(8,128)}, f32[1,1,2,3,2,8,512]{6,5,2,4,3,1,0:T(8,128)S(1)}, u32[]{:S(2)}, u32[]{:S(2)}) collective-permute-start(f32[1,1,2,3,2,8,512]{6,5,2,4,3,1,0:T(8,128)} %bitcast.609), channel_id=1, source_target_pairs={{4,0},{8,4},{12,8},{16,12},{20,16},{24,20},{28,24},{32,28},{36,32}... | collective-permute-start | bytes 589832 | tf_op jit(solution)/shard_map/ppermute | solution.py:16
  178.1 6.9 %collective-permute-start.10 = (f32[1,1,2,3,2,8,512]{6,5,2,4,3,1,0:T(8,128)}, f32[1,1,2,3,2,8,512]{6,5,2,4,3,1,0:T(8,128)S(1)}, u32[]{:S(2)}, u32[]{:S(2)}) collective-permute-start(f32[1,1,2,3,2,8,512]{6,5,2,4,3,1,0:T(8,128)} %bitcast.609), channel_id=1, source_target_pairs={{0,1},{1,2},{2,3},{4,5},{5,6},{6,7},{8,9},{9,10},{10,11},{12,13},{... | collective-permute-start | bytes 589832 | tf_op jit(solution)/shard_map/ppermute | solution.py:15
  181.5 7.8 %collective-permute-start.11 = (f32[1,1,2,3,2,8,512]{6,5,2,4,3,1,0:T(8,128)}, f32[1,1,2,3,2,8,512]{6,5,2,4,3,1,0:T(8,128)S(1)}, u32[]{:S(2)}, u32[]{:S(2)}) collective-permute-start(f32[1,1,2,3,2,8,512]{6,5,2,4,3,1,0:T(8,128)} %bitcast.609), channel_id=1, source_target_pairs={{1,0},{2,1},{3,2},{5,4},{6,5},{7,6},{9,8},{10,9},{11,10},{13,12},{... | collective-permute-start | bytes 589832 | tf_op jit(solution)/shard_map/ppermute | solution.py:16
  199.9 24.8 %copy-start.14 = (f32[13,1,1,64]{3,2,1,0:T(1,128)S(1)}, f32[13,1,1,64]{3,2,1,0:T(1,128)}, u32[]{:S(2)}) copy-start(f32[13,1,1,64]{3,2,1,0:T(1,128)} %get-tuple-element.106) | copy-start | bytes 9988
  200.0 30.2 %copy-start.8 = (f32[3,3,3,64,64]{4,3,2,1,0:T(8,128)S(1)}, f32[3,3,3,64,64]{4,3,2,1,0:T(8,128)}, u32[]{:S(2)}) copy-start(f32[3,3,3,64,64]{4,3,2,1,0:T(8,128)} %reshape_squeeze.76) | copy-start | bytes 1327108
  200.0 30.2 %copy-start.23 = (f32[4]{0:T(128)S(1)}, f32[4]{0:T(128)}, u32[]{:S(2)}) copy-start(f32[4]{0:T(128)} %copy-done.22) | copy-start | bytes 52
  259.2 12.6 %collective-permute-start.12 = (f32[1,1,2,3,2,8,512]{6,5,2,4,3,1,0:T(8,128)S(1)}, f32[1,1,2,3,2,8,512]{6,5,2,4,3,1,0:T(8,128)S(1)}, u32[]{:S(2)}, u32[]{:S(2)}) collective-permute-start(f32[1,1,2,3,2,8,512]{6,5,2,4,3,1,0:T(8,128)S(1)} %bitcast.714), channel_id=1, source_target_pairs={{0,4},{4,8},{8,12},{12,16},{16,20},{20,24},{24,28},{28,32},{32,36}... | collective-permute-start | bytes 589832 | tf_op jit(solution)/shard_map/ppermute | solution.py:15
  261.5 10.2 %collective-permute-start.13 = (f32[1,1,2,3,2,8,512]{6,5,2,4,3,1,0:T(8,128)S(1)}, f32[1,1,2,3,2,8,512]{6,5,2,4,3,1,0:T(8,128)S(1)}, u32[]{:S(2)}, u32[]{:S(2)}) collective-permute-start(f32[1,1,2,3,2,8,512]{6,5,2,4,3,1,0:T(8,128)S(1)} %bitcast.715), channel_id=1, source_target_pairs={{4,0},{8,4},{12,8},{16,12},{20,16},{24,20},{28,24},{32,28},{36,32}... | collective-permute-start | bytes 589832 | tf_op jit(solution)/shard_map/ppermute | solution.py:16
  267.3 6.3 %collective-permute-start.14 = (f32[1,1,2,3,2,8,512]{6,5,2,4,3,1,0:T(8,128)S(1)}, f32[1,1,2,3,2,8,512]{6,5,2,4,3,1,0:T(8,128)S(1)}, u32[]{:S(2)}, u32[]{:S(2)}) collective-permute-start(f32[1,1,2,3,2,8,512]{6,5,2,4,3,1,0:T(8,128)S(1)} %bitcast.716), channel_id=1, source_target_pairs={{0,1},{1,2},{2,3},{4,5},{5,6},{6,7},{8,9},{9,10},{10,11},{12,13},{... | collective-permute-start | bytes 589832 | tf_op jit(solution)/shard_map/ppermute | solution.py:15
  270.4 7.6 %collective-permute-start.15 = (f32[1,1,2,3,2,8,512]{6,5,2,4,3,1,0:T(8,128)S(1)}, f32[1,1,2,3,2,8,512]{6,5,2,4,3,1,0:T(8,128)S(1)}, u32[]{:S(2)}, u32[]{:S(2)}) collective-permute-start(f32[1,1,2,3,2,8,512]{6,5,2,4,3,1,0:T(8,128)S(1)} %bitcast.717), channel_id=1, source_target_pairs={{1,0},{2,1},{3,2},{5,4},{6,5},{7,6},{9,8},{10,9},{11,10},{13,12},{... | collective-permute-start | bytes 589832 | tf_op jit(solution)/shard_map/ppermute | solution.py:16
  (18 other events, 62.7 us)
where the time goes:
time: 330 us; the launch traced here: 325 us
  local copies, waits for them, and re-layouts  141 us (43%)
  matrix products  102 us (31%)
  starting transfers between devices  50.8 us (15%)
  waiting for transfers between devices  17 us (5%)
  other arithmetic  11.2 us (3%)
  between operations  3.61 us (1%)
    conv_general_dilated x4, matrix products, convolve(): lax.conv_general_dilated(padded, taps, (1, 1, 1), 'VALID', dimension_numb...  102 us
    gather x176, local copies, waits for them, and re-layouts, assemble(): piece = getter(table, direction)[nbr[:, jdir]]  95 us
    ppermute x8, starting transfers between devices, padded_2(): lax.ppermute(first, axis, [(b, a) for a, b in up])  28.5 us
    ppermute x8, starting transfers between devices, padded_2(): lax.ppermute(last, axis, up)  22.3 us
    ppermute x8, waiting for transfers between devices, padded_2(): lax.ppermute(first, axis, [(b, a) for a, b in up])  13.1 us
    gather x13, other arithmetic, assemble(): piece = getter(table, direction)[nbr[:, jdir]]  7.8 us
  transfers between devices with their start and end apart: 16, of which 6 were waited for; matrix products, arithmetic and copies ran while one was open for 8% of the time, Pallas kernels for 0%

commit v1 on v0

v1 whole, which is shorter than its diff:
```python
import functools

import jax
import jax.numpy as jnp
from jax import lax
from jax.experimental import pallas as pl
from jax.experimental.pallas import tpu as pltpu
from jax.sharding import PartitionSpec as P

BRICK = 4
FACE = 192
MIB = 1 << 20
VM = pl.BlockSpec(memory_space=pltpu.VMEM)
SM = pl.BlockSpec(memory_space=pltpu.SMEM)
F32, BF16 = jnp.float32, jnp.bfloat16


def direction(dx, dy, dz):
    at = (dx + 1) * 9 + (dy + 1) * 3 + dz + 1
    return at - (at > 13)


def lower_half(shape):
    return lax.broadcasted_iota(jnp.int32, shape, len(shape) - 1) < 64


def write_faces(field, faces):
    low = lower_half((8, 128))
    for b in range(BRICK):
        for s in range(2):
            for i in range(8):
                col = (7 * s * 8 + i) * 16 + 4 * b
                faces[b, 32 * s + 4 * i : 32 * s + 4 * i + 4, :] = field[col : col + 4, :]
                col = (i * 8 + 7 * s) * 16 + 4 * b
                at = 64 + 32 * s + 4 * i
                faces[b, at : at + 4, :] = field[col : col + 4, :]
        for x in range(8):
            first = field[pl.ds(x * 128 + 4 * b, 8, stride=16), :]
            last = field[pl.ds(x * 128 + 4 * b + 3, 8, stride=16), :]
            faces[b, 128 + 8 * x : 136 + 8 * x, :] = jnp.where(low, first, last)


def offer(slots, faces, send):
    for e in range(2):
        send[e] = faces[slots[0, e]]


def entry_kernel(live, slots, feat, field, faces, send):
    count = live[0]
    for b in range(BRICK):
        keep = jnp.where(b < count, 1.0, 0.0).astype(F32)
        for x in range(8):
            for q in range(4):
                tile = feat[b, x, :, 128 * q : 128 * q + 128] * keep
                field[pl.ds(x * 128 + 4 * b + q, 8, stride=16), :] = tile
    write_faces(field, faces)
    offer(slots, faces, send)


def taps_kernel(weights, taps, even, odd, wide):
    low = lower_half((32, 128))
    zero = jnp.zeros((32, 128), F32)
    for k in range(weights.shape[0]):
        for g in range(4):
            n = 8 if g < 3 else 3
            for i in range(32):
                tile = weights[k, 8 * g : 8 * g + n, 128 * i : 128 * i + 128]
                even[pl.ds(8 * g * 32 + i, n, stride=32), :] = tile
                odd[pl.ds(8 * g * 32 + i, n, stride=32), :] = pltpu.roll(tile, 64, 1)
        for t in range(9):
            def rows(ref, d):
                if d < 0 or d > 2:
                    return zero
                return ref[(3 * t + d) * 32 : (3 * t + d) * 32 + 32, :]

            for w, base in ((0, 192), (1, 0), (2, 64), (3, 128)):
                wide[pl.ds(base, 32, stride=2), :] = jnp.where(low, rows(even, w), rows(odd, w - 1))
                wide[pl.ds(base + 1, 32, stride=2), :] = jnp.where(low, rows(odd, w), rows(even, w - 1))
            full = wide[...]
            high = full.astype(BF16)
            taps[k, t, :, 0:128] = high
            taps[k, t, :, 128:256] = (full - high.astype(F32)).astype(BF16)


def fill_table(faces, arrived, table):
    table[0:4] = faces[...]
    for k, ref in enumerate(arrived):
        table[4 + 2 * k : 6 + 2 * k] = ref[...]
    table[12] = jnp.zeros((FACE, 128), F32)


def fill_margins(nbr, field, table, one, two):
    for x in range(8):
        one[(x + 1) * 160 + 16 : (x + 1) * 160 + 144, :] = field[x * 128 : x * 128 + 128, :]
    for b in range(BRICK):
        def cell(xp, yp):
            return (xp * 10 + yp) * 16 + 4 * b

        for d in (-1, 1):
            s, p = (1, 0) if d < 0 else (0, 9)
            t = nbr[b, direction(d, 0, 0)]
            for i in range(8):
                at = cell(p, i + 1)
                one[at : at + 4, :] = table[t, 32 * s + 4 * i : 32 * s + 4 * i + 4, :]
            t = nbr[b, direction(0, d, 0)]
            for i in range(8):
                at = cell(i + 1, p)
                one[at : at + 4, :] = table[t, 64 + 32 * s + 4 * i : 64 + 32 * s + 4 * i + 4, :]
            for e in (-1, 1):
                y, py = (7, 0) if e < 0 else (0, 9)
                t = nbr[b, direction(d, e, 0)]
                at = cell(p, py)
                one[at : at + 4, :] = table[t, 32 * s + 4 * y : 32 * s + 4 * y + 4, :]
    low3 = lower_half((20, 8, 128))
    for c in range(10):
        rows = one[c * 160 : c * 160 + 160, :].reshape(20, 8, 128)
        both = jnp.where(low3, pltpu.roll(rows, 7, 1), pltpu.roll(rows, 1, 1))
        two[c * 160 : c * 160 + 160, :] = both.reshape(160, 128)
    low = lower_half((8, 128))
    low1 = lower_half((1, 128))
    for b in range(BRICK):
        for dz in (-1, 1):
            def merge(start, stride, new):
                at = pl.ds(start, 8, stride=stride)
                old = two[at, :]
                two[at, :] = jnp.where(low, new, old) if dz > 0 else jnp.where(low, old, new)

            row = 4 * b + (3 if dz > 0 else 0)
            t = nbr[b, direction(0, 0, dz)]
            for x in range(8):
                merge(((x + 1) * 10 + 1) * 16 + row, 16, table[t, 128 + 8 * x : 136 + 8 * x, :])
            for d in (-1, 1):
                x, p = (7, 0) if d < 0 else (0, 9)
                t = nbr[b, direction(d, 0, dz)]
                merge((p * 10 + 1) * 16 + row, 16, table[t, 128 + 8 * x : 136 + 8 * x, :])
                t = nbr[b, direction(0, d, dz)]
                merge((10 + p) * 16 + row, 160, table[t, pl.ds(128 + x, 8, stride=8), :])
                for e in (-1, 1):
                    y, py = (7, 0) if e < 0 else (0, 9)
                    t = nbr[b, direction(d, e, dz)]
                    at = (p * 10 + py) * 16 + row
                    new = table[t, 128 + 8 * x + y : 129 + 8 * x + y, :]
                    old = two[at : at + 1, :]
                    two[at : at + 1, :] = jnp.where(low1, new, old) if dz > 0 else jnp.where(low1, old, new)


def split(one, two, high, rest):
    for c in range(10):
        for half, ref in enumerate((one, two)):
            full = ref[c * 160 : c * 160 + 160, :]
            top = full.astype(BF16)
            high[c, :, 128 * half : 128 * half + 128] = top
            rest[c, :, 128 * half : 128 * half + 128] = (full - top.astype(F32)).astype(BF16)


def convolve(high, rest, taps):
    wide = None
    narrow = None
    for dx in range(3):
        for dy in range(3):
            kernel = taps[3 * dx + dy]
            rows = high[dx : dx + 8, dy * 16 : dy * 16 + 128, :].reshape(1024, 256)
            part = jnp.dot(rows, kernel, preferred_element_type=F32)
            wide = part if wide is None else wide + part
            rows = rest[dx : dx + 8, dy * 16 : dy * 16 + 128, :].reshape(1024, 256)
            part = jnp.dot(rows, kernel[:, 0:128], preferred_element_type=F32)
            narrow = part if narrow is None else narrow + part
    return wide[:, 0:128] + (wide[:, 128:256] + narrow)


def layer_kernel(residual, last, index, live, slots, nbr, *refs):
    refs = list(refs)
    field, faces = refs[:2]
    arrived = refs[2:6]
    taps, biases = refs[6:8]
    refs = refs[8:]
    skip = refs.pop(0) if residual else None
    if last:
        (out,) = refs[:1]
        refs = refs[1:]
        table, one, two, high, rest, new = refs
    else:
        new, new_faces, send = refs[:3]
        table, one, two, high, rest = refs[3:]
    fill_table(faces, arrived, table)
    fill_margins(nbr, field, table, one, two)
    split(one, two, high, rest)
    total = convolve(high, rest, taps.at[index])
    bias = biases[index : index + 1, :]
    total = total + jnp.concatenate([bias, bias], 1)
    if residual:
        total = total + skip[...]
    brick = lax.broadcasted_iota(jnp.int32, (1024, 128), 0) % 16 // 4
    new[...] = jnp.where(brick < live[0], jnp.maximum(total, 0.0), 0.0)
    if last:
        for b in range(BRICK):
            for x in range(8):
                for q in range(4):
                    out[b, x, :, 128 * q : 128 * q + 128] = new[pl.ds(x * 128 + 4 * b + q, 8, stride=16), :]
    else:
        write_faces(new, new_faces)
        offer(slots, new_faces, send)


FIELD = jax.ShapeDtypeStruct((1024, 128), F32)
FACES = jax.ShapeDtypeStruct((BRICK, FACE, 128), F32)
SEND = jax.ShapeDtypeStruct((2, FACE, 128), F32)


def swaps(size, first):
    pairs = [(i, i + 1) for i in range(first, size - 1, 2)]
    return pairs + [(b, a) for a, b in pairs]


def exchange(send):
    got = []
    for axis in ("space", "slab"):
        size = lax.axis_size(axis)
        near = lax.ppermute(send, axis, swaps(size, 0))
        far = lax.ppermute(send, axis, swaps(size, 1))
        odd = lax.axis_index(axis) % 2 == 1
        got.append((near, far, odd))
    out = []
    for near, far, odd in got:
        out += [jnp.where(odd, near, far), jnp.where(odd, far, near)]
    return out


def shards(features, live, rim_slots, neighbours, weights, biases):
    params = pltpu.CompilerParams(vmem_limit_bytes=24 * MIB)
    field, faces, send = pl.pallas_call(
        entry_kernel,
        out_shape=(FIELD, FACES, SEND),
        in_specs=[SM, SM, VM],
        out_specs=(VM, VM, VM),
        compiler_params=params,
        name="entry",
    )(live, rim_slots, features)
    convs = weights.shape[0]
    taps = pl.pallas_call(
        taps_kernel,
        out_shape=jax.ShapeDtypeStruct((convs, 9, 256, 256), BF16),
        in_specs=[VM],
        out_specs=VM,
        scratch_shapes=[pltpu.VMEM((896, 128), F32), pltpu.VMEM((896, 128), F32), pltpu.VMEM((256, 128), F32)],
        compiler_params=params,
        name="taps",
    )(weights)

    def layer(index, field, faces, send, skip, last):
        arrived = exchange(send)
        args = [live, rim_slots, neighbours, field, faces, *arrived, taps, biases]
        if skip is not None:
            args.append(skip)
        out_shape = (jax.ShapeDtypeStruct(features.shape, F32),) if last else (FIELD, FACES, SEND)
        scratch = [
            pltpu.VMEM((13, FACE, 128), F32),
            pltpu.VMEM((1600, 128), F32),
            pltpu.VMEM((1600, 128), F32),
            pltpu.VMEM((10, 160, 256), BF16),
            pltpu.VMEM((10, 160, 256), BF16),
        ]
        if last:
            scratch.append(pltpu.VMEM((1024, 128), F32))
        return pl.pallas_call(
            functools.partial(layer_kernel, skip is not None, last, index),
            out_shape=out_shape,
            in_specs=[SM, SM, SM] + [VM] * (len(args) - 3),
            out_specs=(VM,) * len(out_shape),
            scratch_shapes=scratch,
            compiler_params=params,
            name=f"layer{index}",
        )(*args)

    for index in range(0, convs, 2):
        inner = layer(index, field, faces, send, None, False)
        outer = layer(index + 1, *inner, field, index + 2 == convs)
        if index + 2 < convs:
            field, faces, send = outer
    return outer[0]


def solution(mesh):
    in_specs = (
        P(("space", "slab"), None, None, None),
        P(("space", "slab")),
        P(("space", "slab"), None),
        P(("space", "slab"), None),
        P(),
        P(),
    )
    out_specs = P(("space", "slab"), None, None, None)
    return jax.shard_map(shards, mesh=mesh, in_specs=in_specs, out_specs=out_specs, check_vma=False)
```

time: 330 us -> 70.1 us (0.21); the launches traced: 325 us -> 69.7 us
  local copies, waits for them, and re-layouts: 141 us -> 4.22 us
  matrix products: 102 us -> 0 us
  starting transfers between devices: 50.8 us -> 26.9 us
  Pallas kernels: 0 us -> 19.4 us
  other arithmetic: 11.2 us -> 0.24 us
    conv_general_dilated x4 -> x0, matrix products: 102 us -> none  [convolve(): lax.conv_general_dilated(padded, taps, (1, 1, 1), 'VALID', dimension_numb...]
    gather x183 -> x0, local copies, waits for them, and re-layouts: 98.3 us -> none  [the longest x176 95 us: assemble(): piece = getter(table, direction)[nbr[:, jdir]]]
    ppermute x16, starting transfers between devices: 50.8 us -> 26.9 us  [the longest x8 15 us: exchange(): far = lax.ppermute(send, axis, swaps(size, 1))]
    pallas_call x0 -> x6, Pallas kernels: none -> 19.4 us  [the longest x4 15.3 us: layer(): pl.pallas_call(functools.partial(layer_kernel, skip is not None, last, in...]
    slice x41 -> x0, local copies, waits for them, and re-layouts: 17.8 us -> none  [the longest x1 5.62 us: layer(): return convolve(padded, weights[kidx])]
    another operation x52 -> x0, local copies, waits for them, and re-layouts: 9.6 us -> none  [the longest x4 3.23 us: convolve(): taps = kernel.reshape(3, 3, 3, channels, channels)]
    gather x14 -> x0, other arithmetic: 7.8 us -> none  [the longest x13 7.8 us: assemble(): piece = getter(table, direction)[nbr[:, jdir]]]
    reshape x12 -> x0, local copies, waits for them, and re-layouts: 4.36 us -> none  [the longest x4 2.77 us: faces_of(): cube = field.reshape(count, 8, 8, 8, channels)]
  transfers between devices with their start and end apart: 16 -> 16, of which waited for: 6 -> 6; matrix products, arithmetic and copies ran while one was open for 8% -> 4% of each run, Pallas kernels for 0% -> 5%
where the time goes in v1:
time: 70.1 us; the launch traced here: 69.7 us
  starting transfers between devices  26.9 us (38%)
  Pallas kernels  19.4 us (28%)
  waiting for transfers between devices  17.9 us (26%)
  local copies, waits for them, and re-layouts  4.22 us (6%)
  between operations  0.95 us (1%)
    pallas_call x4, Pallas kernels, layer(): pl.pallas_call(functools.partial(layer_kernel, skip is not None, last, in...  15.3 us
    ppermute x8, starting transfers between devices, exchange(): far = lax.ppermute(send, axis, swaps(size, 1))  15 us
    ppermute x8, waiting for transfers between devices, exchange(): far = lax.ppermute(send, axis, swaps(size, 1))  14.6 us
    ppermute x8, starting transfers between devices, exchange(): near = lax.ppermute(send, axis, swaps(size, 0))  11.9 us
    unnamed x11, local copies, waits for them, and re-layouts  4.22 us
    ppermute x8, waiting for transfers between devices, exchange(): near = lax.ppermute(send, axis, swaps(size, 0))  3.35 us
    pallas_call x1, Pallas kernels, shards(): pl.pallas_call(taps_kernel, out_shape=jax.ShapeDtypeStruct((convs, 9, 256...  3.3 us
  transfers between devices with their start and end apart: 16, of which 6 were waited for; matrix products, arithmetic and copies ran while one was open for 4% of the time, Pallas kernels for 5%

profile of v1, /device:TPU:96, one launch (start us, length us, event | category | flops | bytes accessed | tf_op | source)
XLA Modules:
  0.0 69.7 jit_solution(16205682566741412200)
XLA Ops:
  0.7 1.0 %copy-done = f32[4,8,8,512]{3,2,1,0:T(8,128)S(1)} copy-done((f32[4,8,8,512]{3,2,1,0:T(8,128)S(1)}, f32[4,8,8,512]{3,2,1,0:T(8,128)}, u32[]{:S(2)}) %copy-start) | copy-done | bytes 524312
  1.7 0.7 copy-done.3
  2.4 0.8 %entry.1 = (f32[1024,128]{1,0:T(8,128)S(1)}, f32[4,192,128]{2,1,0:T(8,128)S(1)}, f32[2,192,128]{2,1,0:T(8,128)S(1)}) custom-call(s32[1]{0:T(128)S(6)} %copy.8.live, s32[1,2]{1,0:T(1,128)S(1)} %copy-done.3, f32[4,8,8,512]{3,2,1,0:T(8,128)S(1)} %copy-done), custom_call_target="tpu_custom_call" | custom-call | tf_op jit(solution)/shard_map/entry/pallas_call | solution.py:231
  3.2 0.7 collective-permute-start.3
  3.9 4.3 %collective-permute-start.2 = (f32[2,192,128]{2,1,0:T(8,128)S(1)}, f32[2,192,128]{2,1,0:T(8,128)S(1)}, u32[]{:S(2)}, u32[]{:S(2)}) collective-permute-start(f32[2,192,128]{2,1,0:T(8,128)S(1)} %get-tuple-element.19), channel_id=1, source_target_pairs={{0,1},{2,3},{1,0},{3,2},{4,5},{6,7},{5,4},{7,6},{8,9},{10,11},{9,8... | collective-permute-start | bytes 589832 | tf_op jit(solution)/shard_map/ppermute | solution.py:219
  8.2 3.6 %collective-permute-start.1 = (f32[2,192,128]{2,1,0:T(8,128)S(1)}, f32[2,192,128]{2,1,0:T(8,128)S(1)}, u32[]{:S(2)}, u32[]{:S(2)}) collective-permute-start(f32[2,192,128]{2,1,0:T(8,128)S(1)} %get-tuple-element.19), channel_id=1, source_target_pairs={{4,8},{12,16},{20,24},{28,32},{36,40},{44,48},{52,56},{60,64},{68,... | collective-permute-start | bytes 589832 | tf_op jit(solution)/shard_map/ppermute | solution.py:220
  11.8 0.1 collective-permute-start
  11.9 2.5 %copy.7.weights = f32[4,27,4096]{2,1,0:T(8,128)S(1)} copy(f32[4,27,4096]{2,0,1:T(4,128)} %param.10) | data formatting | bytes 3538944 | tf_op args[4]
  14.4 0.0 copy-start.1
  14.5 3.3 %taps.1.refs_6_ = bf16[4,9,256,256]{3,2,1,0:T(8,128)(2,1)S(1)} custom-call(f32[4,27,4096]{2,1,0:T(8,128)S(1)} %copy.7.weights), custom_call_target="tpu_custom_call" | custom-call | tf_op jit(solution)/shard_map/taps/pallas_call | solution.py:240
  17.9 3.6 %layer0.1 = (f32[1024,128]{1,0:T(8,128)S(1)}, f32[4,192,128]{2,1,0:T(8,128)S(1)}, f32[2,192,128]{2,1,0:T(8,128)S(1)}) custom-call(s32[1]{0:T(128)S(6)} %copy.8.live, s32[1,2]{1,0:T(1,128)S(1)} %copy-done.4, s32[4,26]{1,0:T(4,128)S(1)} %copy-done.1, f32[1024,128]{1,0:T(8,128)S(1)} %get-tuple-element.17.refs_0_.refs_8_, ...), custom_call_target="tpu_custom_call" | custom-call | tf_op jit(solution)/shard_map/layer0/pallas_call | solution.py:265
  21.5 0.7 collective-permute-start.7
  22.2 2.2 %collective-permute-start.6 = (f32[2,192,128]{2,1,0:T(8,128)S(1)}, f32[2,192,128]{2,1,0:T(8,128)S(1)}, u32[]{:S(2)}, u32[]{:S(2)}) collective-permute-start(f32[2,192,128]{2,1,0:T(8,128)S(1)} %get-tuple-element.22), channel_id=1, source_target_pairs={{0,1},{2,3},{1,0},{3,2},{4,5},{6,7},{5,4},{7,6},{8,9},{10,11},{9,8... | collective-permute-start | bytes 589832 | tf_op jit(solution)/shard_map/ppermute | solution.py:219
  24.4 3.2 %collective-permute-start.5 = (f32[2,192,128]{2,1,0:T(8,128)S(1)}, f32[2,192,128]{2,1,0:T(8,128)S(1)}, u32[]{:S(2)}, u32[]{:S(2)}) collective-permute-start(f32[2,192,128]{2,1,0:T(8,128)S(1)} %get-tuple-element.22), channel_id=1, source_target_pairs={{4,8},{12,16},{20,24},{28,32},{36,40},{44,48},{52,56},{60,64},{68,... | collective-permute-start | bytes 589832 | tf_op jit(solution)/shard_map/ppermute | solution.py:220
  27.6 0.1 collective-permute-start.4
  27.7 1.9 %collective-permute-done.6 = f32[2,192,128]{2,1,0:T(8,128)S(1)} collective-permute-done((f32[2,192,128]{2,1,0:T(8,128)S(1)}, f32[2,192,128]{2,1,0:T(8,128)S(1)}, u32[]{:S(2)}, u32[]{:S(2)}) %collective-permute-start.6) | collective-permute-done | bytes 196640 | tf_op jit(solution)/shard_map/ppermute | solution.py:219
  29.7 3.8 %collective-permute-done.5 = f32[2,192,128]{2,1,0:T(8,128)S(1)} collective-permute-done((f32[2,192,128]{2,1,0:T(8,128)S(1)}, f32[2,192,128]{2,1,0:T(8,128)S(1)}, u32[]{:S(2)}, u32[]{:S(2)}) %collective-permute-start.5) | collective-permute-done | bytes 196640 | tf_op jit(solution)/shard_map/ppermute | solution.py:220
  33.5 3.6 %layer1.1 = (f32[1024,128]{1,0:T(8,128)S(1)}, f32[4,192,128]{2,1,0:T(8,128)S(1)}, f32[2,192,128]{2,1,0:T(8,128)S(1)}) custom-call(s32[1]{0:T(128)S(6)} %copy.8.live, s32[1,2]{1,0:T(1,128)S(1)} %copy-done.4, s32[4,26]{1,0:T(4,128)S(1)} %copy-done.1, f32[1024,128]{1,0:T(8,128)S(1)} %get-tuple-element.20.refs_0_, f32[4,192,128]{2,1,0:T(8,128)S(1)} %get-tuple-element.21.refs_1_, ...), custom_call_target="tpu_custom_call" | custom-call | tf_op jit(solution)/shard_map/layer1/pallas_call | solution.py:265
  37.1 0.7 collective-permute-start.11
  37.8 2.8 %collective-permute-start.10 = (f32[2,192,128]{2,1,0:T(8,128)S(1)}, f32[2,192,128]{2,1,0:T(8,128)S(1)}, u32[]{:S(2)}, u32[]{:S(2)}) collective-permute-start(f32[2,192,128]{2,1,0:T(8,128)S(1)} %get-tuple-element.25), channel_id=1, source_target_pairs={{0,1},{2,3},{1,0},{3,2},{4,5},{6,7},{5,4},{7,6},{8,9},{10,11},{9,8... | collective-permute-start | bytes 589832 | tf_op jit(solution)/shard_map/ppermute | solution.py:219
  40.7 2.9 %collective-permute-start.9 = (f32[2,192,128]{2,1,0:T(8,128)S(1)}, f32[2,192,128]{2,1,0:T(8,128)S(1)}, u32[]{:S(2)}, u32[]{:S(2)}) collective-permute-start(f32[2,192,128]{2,1,0:T(8,128)S(1)} %get-tuple-element.25), channel_id=1, source_target_pairs={{4,8},{12,16},{20,24},{28,32},{36,40},{44,48},{52,56},{60,64},{68,... | collective-permute-start | bytes 589832 | tf_op jit(solution)/shard_map/ppermute | solution.py:220
  43.6 0.3 collective-permute-start.8
  43.8 0.5 collective-permute-done.10
  44.3 5.4 %collective-permute-done.9 = f32[2,192,128]{2,1,0:T(8,128)S(1)} collective-permute-done((f32[2,192,128]{2,1,0:T(8,128)S(1)}, f32[2,192,128]{2,1,0:T(8,128)S(1)}, u32[]{:S(2)}, u32[]{:S(2)}) %collective-permute-start.9) | collective-permute-done | bytes 196640 | tf_op jit(solution)/shard_map/ppermute | solution.py:220
  49.8 3.6 %layer2.1 = (f32[1024,128]{1,0:T(8,128)S(1)}, f32[4,192,128]{2,1,0:T(8,128)S(1)}, f32[2,192,128]{2,1,0:T(8,128)S(1)}) custom-call(s32[1]{0:T(128)S(6)} %copy.8.live, s32[1,2]{1,0:T(1,128)S(1)} %copy-done.4, s32[4,26]{1,0:T(4,128)S(1)} %copy-done.1, f32[1024,128]{1,0:T(8,128)S(1)} %get-tuple-element.23.refs_0_.refs_8_, ...), custom_call_target="tpu_custom_call" | custom-call | tf_op jit(solution)/shard_map/layer2/pallas_call | solution.py:265
  53.4 0.7 collective-permute-start.15
  54.1 2.1 %collective-permute-start.14 = (f32[2,192,128]{2,1,0:T(8,128)S(1)}, f32[2,192,128]{2,1,0:T(8,128)S(1)}, u32[]{:S(2)}, u32[]{:S(2)}) collective-permute-start(f32[2,192,128]{2,1,0:T(8,128)S(1)} %get-tuple-element.28), channel_id=1, source_target_pairs={{0,1},{2,3},{1,0},{3,2},{4,5},{6,7},{5,4},{7,6},{8,9},{10,11},{9,8... | collective-permute-start | bytes 589832 | tf_op jit(solution)/shard_map/ppermute | solution.py:219
  56.2 2.6 %collective-permute-start.13 = (f32[2,192,128]{2,1,0:T(8,128)S(1)}, f32[2,192,128]{2,1,0:T(8,128)S(1)}, u32[]{:S(2)}, u32[]{:S(2)}) collective-permute-start(f32[2,192,128]{2,1,0:T(8,128)S(1)} %get-tuple-element.28), channel_id=1, source_target_pairs={{4,8},{12,16},{20,24},{28,32},{36,40},{44,48},{52,56},{60,64},{68,... | collective-permute-start | bytes 589832 | tf_op jit(solution)/shard_map/ppermute | solution.py:220
  58.8 0.1 collective-permute-start.12
  58.9 0.9 %collective-permute-done.14 = f32[2,192,128]{2,1,0:T(8,128)S(1)} collective-permute-done((f32[2,192,128]{2,1,0:T(8,128)S(1)}, f32[2,192,128]{2,1,0:T(8,128)S(1)}, u32[]{:S(2)}, u32[]{:S(2)}) %collective-permute-start.14) | collective-permute-done | bytes 196640 | tf_op jit(solution)/shard_map/ppermute | solution.py:219
  59.9 5.4 %collective-permute-done.13 = f32[2,192,128]{2,1,0:T(8,128)S(1)} collective-permute-done((f32[2,192,128]{2,1,0:T(8,128)S(1)}, f32[2,192,128]{2,1,0:T(8,128)S(1)}, u32[]{:S(2)}, u32[]{:S(2)}) %collective-permute-start.13) | collective-permute-done | bytes 196640 | tf_op jit(solution)/shard_map/ppermute | solution.py:220
  65.3 4.4 %layer3.1 = f32[4,8,8,512]{3,2,1,0:T(8,128)} custom-call(s32[1]{0:T(128)S(6)} %copy.8.live, s32[1,2]{1,0:T(1,128)S(1)} %copy-done.4, s32[4,26]{1,0:T(4,128)S(1)} %copy-done.1, f32[1024,128]{1,0:T(8,128)S(1)} %get-tuple-element.26.refs_0_, f32[4,192,128]{2,1,0:T(8,128)S(1)} %get-tuple-element.27.refs_1_, f32[2,192,128]{2,1,0:T(8,128)S(1)} %get-tuple-element.32.refs_2_, ...), custom_call_target="tpu_custom_call" | custom-call | tf_op jit(solution)/shard_map/layer3/pallas_call | solution.py:265
  (25 shorter events, 0.3 us)
Async XLA Ops:
  0.7 1.0 %copy-start = (f32[4,8,8,512]{3,2,1,0:T(8,128)S(1)}, f32[4,8,8,512]{3,2,1,0:T(8,128)}, u32[]{:S(2)}) copy-start(f32[4,8,8,512]{3,2,1,0:T(8,128)} %feat.1) | copy-start | bytes 1572868
  1.7 0.7 copy-start.3
  3.2 14.6 %collective-permute-start.3 = (f32[2,192,128]{2,1,0:T(8,128)S(1)}, f32[2,192,128]{2,1,0:T(8,128)S(1)}, u32[]{:S(2)}, u32[]{:S(2)}) collective-permute-start(f32[2,192,128]{2,1,0:T(8,128)S(1)} %get-tuple-element.19), channel_id=1, source_target_pairs={{1,2},{2,1},{5,6},{6,5},{9,10},{10,9},{13,14},{14,13},{17,18},{18,... | collective-permute-start | bytes 589832 | tf_op jit(solution)/shard_map/ppermute | solution.py:220
  3.9 13.9 %collective-permute-start.2 = (f32[2,192,128]{2,1,0:T(8,128)S(1)}, f32[2,192,128]{2,1,0:T(8,128)S(1)}, u32[]{:S(2)}, u32[]{:S(2)}) collective-permute-start(f32[2,192,128]{2,1,0:T(8,128)S(1)} %get-tuple-element.19), channel_id=1, source_target_pairs={{0,1},{2,3},{1,0},{3,2},{4,5},{6,7},{5,4},{7,6},{8,9},{10,11},{9,8... | collective-permute-start | bytes 589832 | tf_op jit(solution)/shard_map/ppermute | solution.py:219
  8.2 9.7 %collective-permute-start.1 = (f32[2,192,128]{2,1,0:T(8,128)S(1)}, f32[2,192,128]{2,1,0:T(8,128)S(1)}, u32[]{:S(2)}, u32[]{:S(2)}) collective-permute-start(f32[2,192,128]{2,1,0:T(8,128)S(1)} %get-tuple-element.19), channel_id=1, source_target_pairs={{4,8},{12,16},{20,24},{28,32},{36,40},{44,48},{52,56},{60,64},{68,... | collective-permute-start | bytes 589832 | tf_op jit(solution)/shard_map/ppermute | solution.py:220
  11.8 6.0 %collective-permute-start = (f32[2,192,128]{2,1,0:T(8,128)S(1)}, f32[2,192,128]{2,1,0:T(8,128)S(1)}, u32[]{:S(2)}, u32[]{:S(2)}) collective-permute-start(f32[2,192,128]{2,1,0:T(8,128)S(1)} %get-tuple-element.19), channel_id=1, source_target_pairs={{0,4},{8,12},{16,20},{24,28},{32,36},{40,44},{48,52},{56,60},{64,6... | collective-permute-start | bytes 589832 | tf_op jit(solution)/shard_map/ppermute | solution.py:219
  14.4 3.5 %copy-start.1 = (s32[4,26]{1,0:T(4,128)S(1)}, s32[4,26]{1,0:T(4,128)}, u32[]{:S(2)}) copy-start(s32[4,26]{1,0:T(4,128)} %nbr.7) | copy-start | bytes 1252
  14.4 3.5 %copy-start.2 = (f32[4,64]{1,0:T(4,128)S(1)}, f32[4,64]{1,0:T(4,128)}, u32[]{:S(2)}) copy-start(f32[4,64]{1,0:T(4,128)} %refs_7_.7) | copy-start | bytes 3076
  14.4 3.5 %copy-start.4 = (s32[1,2]{1,0:T(1,128)S(1)}, s32[1,2]{1,0:T(1,128)}, u32[]{:S(2)}) copy-start(s32[1,2]{1,0:T(1,128)} %slots.9) | copy-start | bytes 28
  21.5 6.2 %collective-permute-start.7 = (f32[2,192,128]{2,1,0:T(8,128)S(1)}, f32[2,192,128]{2,1,0:T(8,128)S(1)}, u32[]{:S(2)}, u32[]{:S(2)}) collective-permute-start(f32[2,192,128]{2,1,0:T(8,128)S(1)} %get-tuple-element.22), channel_id=1, source_target_pairs={{1,2},{2,1},{5,6},{6,5},{9,10},{10,9},{13,14},{14,13},{17,18},{18,... | collective-permute-start | bytes 589832 | tf_op jit(solution)/shard_map/ppermute | solution.py:220
  22.2 7.4 %collective-permute-start.6 = (f32[2,192,128]{2,1,0:T(8,128)S(1)}, f32[2,192,128]{2,1,0:T(8,128)S(1)}, u32[]{:S(2)}, u32[]{:S(2)}) collective-permute-start(f32[2,192,128]{2,1,0:T(8,128)S(1)} %get-tuple-element.22), channel_id=1, source_target_pairs={{0,1},{2,3},{1,0},{3,2},{4,5},{6,7},{5,4},{7,6},{8,9},{10,11},{9,8... | collective-permute-start | bytes 589832 | tf_op jit(solution)/shard_map/ppermute | solution.py:219
  24.4 9.1 %collective-permute-start.5 = (f32[2,192,128]{2,1,0:T(8,128)S(1)}, f32[2,192,128]{2,1,0:T(8,128)S(1)}, u32[]{:S(2)}, u32[]{:S(2)}) collective-permute-start(f32[2,192,128]{2,1,0:T(8,128)S(1)} %get-tuple-element.22), channel_id=1, source_target_pairs={{4,8},{12,16},{20,24},{28,32},{36,40},{44,48},{52,56},{60,64},{68,... | collective-permute-start | bytes 589832 | tf_op jit(solution)/shard_map/ppermute | solution.py:220
  27.6 5.9 %collective-permute-start.4 = (f32[2,192,128]{2,1,0:T(8,128)S(1)}, f32[2,192,128]{2,1,0:T(8,128)S(1)}, u32[]{:S(2)}, u32[]{:S(2)}) collective-permute-start(f32[2,192,128]{2,1,0:T(8,128)S(1)} %get-tuple-element.22), channel_id=1, source_target_pairs={{0,4},{8,12},{16,20},{24,28},{32,36},{40,44},{48,52},{56,60},{64,6... | collective-permute-start | bytes 589832 | tf_op jit(solution)/shard_map/ppermute | solution.py:219
  37.1 6.7 %collective-permute-start.11 = (f32[2,192,128]{2,1,0:T(8,128)S(1)}, f32[2,192,128]{2,1,0:T(8,128)S(1)}, u32[]{:S(2)}, u32[]{:S(2)}) collective-permute-start(f32[2,192,128]{2,1,0:T(8,128)S(1)} %get-tuple-element.25), channel_id=1, source_target_pairs={{1,2},{2,1},{5,6},{6,5},{9,10},{10,9},{13,14},{14,13},{17,18},{18,... | collective-permute-start | bytes 589832 | tf_op jit(solution)/shard_map/ppermute | solution.py:220
  37.8 6.5 %collective-permute-start.10 = (f32[2,192,128]{2,1,0:T(8,128)S(1)}, f32[2,192,128]{2,1,0:T(8,128)S(1)}, u32[]{:S(2)}, u32[]{:S(2)}) collective-permute-start(f32[2,192,128]{2,1,0:T(8,128)S(1)} %get-tuple-element.25), channel_id=1, source_target_pairs={{0,1},{2,3},{1,0},{3,2},{4,5},{6,7},{5,4},{7,6},{8,9},{10,11},{9,8... | collective-permute-start | bytes 589832 | tf_op jit(solution)/shard_map/ppermute | solution.py:219
  40.7 9.1 %collective-permute-start.9 = (f32[2,192,128]{2,1,0:T(8,128)S(1)}, f32[2,192,128]{2,1,0:T(8,128)S(1)}, u32[]{:S(2)}, u32[]{:S(2)}) collective-permute-start(f32[2,192,128]{2,1,0:T(8,128)S(1)} %get-tuple-element.25), channel_id=1, source_target_pairs={{4,8},{12,16},{20,24},{28,32},{36,40},{44,48},{52,56},{60,64},{68,... | collective-permute-start | bytes 589832 | tf_op jit(solution)/shard_map/ppermute | solution.py:220
  43.6 6.2 %collective-permute-start.8 = (f32[2,192,128]{2,1,0:T(8,128)S(1)}, f32[2,192,128]{2,1,0:T(8,128)S(1)}, u32[]{:S(2)}, u32[]{:S(2)}) collective-permute-start(f32[2,192,128]{2,1,0:T(8,128)S(1)} %get-tuple-element.25), channel_id=1, source_target_pairs={{0,4},{8,12},{16,20},{24,28},{32,36},{40,44},{48,52},{56,60},{64,6... | collective-permute-start | bytes 589832 | tf_op jit(solution)/shard_map/ppermute | solution.py:219
  53.4 5.5 %collective-permute-start.15 = (f32[2,192,128]{2,1,0:T(8,128)S(1)}, f32[2,192,128]{2,1,0:T(8,128)S(1)}, u32[]{:S(2)}, u32[]{:S(2)}) collective-permute-start(f32[2,192,128]{2,1,0:T(8,128)S(1)} %get-tuple-element.28), channel_id=1, source_target_pairs={{1,2},{2,1},{5,6},{6,5},{9,10},{10,9},{13,14},{14,13},{17,18},{18,... | collective-permute-start | bytes 589832 | tf_op jit(solution)/shard_map/ppermute | solution.py:220
  54.1 5.7 %collective-permute-start.14 = (f32[2,192,128]{2,1,0:T(8,128)S(1)}, f32[2,192,128]{2,1,0:T(8,128)S(1)}, u32[]{:S(2)}, u32[]{:S(2)}) collective-permute-start(f32[2,192,128]{2,1,0:T(8,128)S(1)} %get-tuple-element.28), channel_id=1, source_target_pairs={{0,1},{2,3},{1,0},{3,2},{4,5},{6,7},{5,4},{7,6},{8,9},{10,11},{9,8... | collective-permute-start | bytes 589832 | tf_op jit(solution)/shard_map/ppermute | solution.py:219
  56.2 9.1 %collective-permute-start.13 = (f32[2,192,128]{2,1,0:T(8,128)S(1)}, f32[2,192,128]{2,1,0:T(8,128)S(1)}, u32[]{:S(2)}, u32[]{:S(2)}) collective-permute-start(f32[2,192,128]{2,1,0:T(8,128)S(1)} %get-tuple-element.28), channel_id=1, source_target_pairs={{4,8},{12,16},{20,24},{28,32},{36,40},{44,48},{52,56},{60,64},{68,... | collective-permute-start | bytes 589832 | tf_op jit(solution)/shard_map/ppermute | solution.py:220
  58.8 6.5 %collective-permute-start.12 = (f32[2,192,128]{2,1,0:T(8,128)S(1)}, f32[2,192,128]{2,1,0:T(8,128)S(1)}, u32[]{:S(2)}, u32[]{:S(2)}) collective-permute-start(f32[2,192,128]{2,1,0:T(8,128)S(1)} %get-tuple-element.28), channel_id=1, source_target_pairs={{0,4},{8,12},{16,20},{24,28},{32,36},{40,44},{48,52},{56,60},{64,6... | collective-permute-start | bytes 589832 | tf_op jit(solution)/shard_map/ppermute | solution.py:219

commit v2 on v1

v2 whole, which is shorter than its diff:
```python
import functools

import jax
import jax.numpy as jnp
from jax import lax
from jax.experimental import pallas as pl
from jax.experimental.pallas import tpu as pltpu
from jax.sharding import PartitionSpec as P

BRICK = 4
FACE = 192
PACK = 152
MIB = 1 << 20
VM = pl.BlockSpec(memory_space=pltpu.VMEM)
SM = pl.BlockSpec(memory_space=pltpu.SMEM)
HB = pl.BlockSpec(memory_space=pltpu.HBM)
F32, BF16 = jnp.float32, jnp.bfloat16
ORDER = [0, 3, 2, 1]
PLACE, SECOND, LIVE = 104, 108, 109


def direction(dx, dy, dz):
    at = (dx + 1) * 9 + (dy + 1) * 3 + dz + 1
    return at - (at > 13)


def lower_half(shape):
    return lax.broadcasted_iota(jnp.int32, shape, len(shape) - 1) < 64


def write_faces(field, faces):
    low = lower_half((8, 128))
    for b in range(2):
        for s in range(2):
            for i in range(8):
                col = (7 * s * 8 + i) * 8 + 4 * b
                faces[b, 32 * s + 4 * i : 32 * s + 4 * i + 4, :] = field[col : col + 4, :]
                col = (i * 8 + 7 * s) * 8 + 4 * b
                at = 64 + 32 * s + 4 * i
                faces[b, at : at + 4, :] = field[col : col + 4, :]
        for x in range(8):
            first = field[pl.ds(x * 64 + 4 * b, 8, stride=8), :]
            last = field[pl.ds(x * 64 + 4 * b + 3, 8, stride=8), :]
            faces[b, 128 + 8 * x : 136 + 8 * x, :] = jnp.where(low, first, last)


def offer(second, faces, send):
    for e, b in ((0, 0), (1, second)):
        send[e, 0:64, :] = faces[b, 0:64, :]
        for s in range(2):
            send[e, 64 + 24 * s : 88 + 24 * s, :] = faces[b, 68 + 32 * s : 92 + 32 * s, :]
        for x in range(6):
            at = 128 + 8 * (x + 1) + 1
            send[e, 112 + 6 * x : 118 + 6 * x, :] = faces[b, at : at + 6, :]
        send[e, 148:152, :] = jnp.zeros((4, 128), F32)


def unpack(pack, e, table, t):
    low = lower_half((8, 128))
    table[t, 0:64, :] = pack[e, 0:64, :]
    for s in range(2):
        table[t, 68 + 32 * s : 92 + 32 * s, :] = pack[e, 64 + 24 * s : 88 + 24 * s, :]
        for x in range(2):
            at = 64 + 32 * s + 28 * x
            table[t, at : at + 4, :] = pack[e, 32 * x + 28 * s : 32 * x + 28 * s + 4, :]
    for x in range(6):
        at = 128 + 8 * (x + 1) + 1
        table[t, at : at + 6, :] = pack[e, 112 + 6 * x : 118 + 6 * x, :]
    for s in range(2):
        first = table[t, pl.ds(64 + 32 * s, 8, stride=4), :]
        last = table[t, pl.ds(64 + 32 * s + 3, 8, stride=4), :]
        table[t, pl.ds(128 + 7 * s, 8, stride=8), :] = jnp.where(low, first, last)
        first = table[t, pl.ds(32 * s, 8, stride=4), :]
        last = table[t, pl.ds(32 * s + 3, 8, stride=4), :]
        table[t, 128 + 56 * s : 136 + 56 * s, :] = jnp.where(low, first, last)


def places_of(s0, s1):
    p0 = s0
    p1 = jnp.where(s1 == s0, (s0 + 1) % BRICK, s1)

    def free(slot):
        return (p0 != slot) & (p1 != slot)

    p2 = jnp.where(free(0), 0, jnp.where(free(1), 1, 2))
    return p0, p1, p2, 6 - p0 - p1 - p2


def enter(pair, live, slots, feat, field, faces, own, picked, sems):
    pick = pltpu.make_async_copy(slots, picked, sems.at[0])
    pick.start()
    copy = pltpu.make_async_copy(feat, own, sems.at[1])
    copy.start()
    pick.wait()
    places = places_of(picked[0, 0], picked[0, 1])
    copy.wait()
    for b in range(2):
        place = places[2 * pair + b]
        keep = jnp.where(place < live[0], 1.0, 0.0).astype(F32)
        for x in range(8):
            for q in range(4):
                tile = own[place, x, :, 128 * q : 128 * q + 128] * keep
                field[pl.ds(x * 64 + 4 * b + q, 8, stride=8), :] = tile
    write_faces(field, faces)


def entry_kernel(live, slots, feat, field, faces, send, own, picked, sems):
    enter(0, live, slots, feat, field, faces, own, picked, sems)
    offer(jnp.where(picked[0, 0] == picked[0, 1], 0, 1), faces, send)


def second_entry_kernel(
    after, live, slots, feat, weights, neighbours, field, faces, held, scalars, own, picked, sems, nbr, far
):
    fetch = pltpu.make_async_copy(weights, held, far.at[0])
    look = pltpu.make_async_copy(neighbours, nbr, far.at[1])
    fetch.start()
    look.start()
    enter(1, live, slots, feat, field, faces, own, picked, sems)
    look.wait()
    places = places_of(picked[0, 0], picked[0, 1])
    turns = [jnp.where(lax.axis_index(axis) % 2 == 0, 2, 0) for axis in ("space", "slab")]

    def rename(at, carry):
        for b in range(BRICK):
            t = nbr[b, at]
            new = jnp.where(t < 8, t ^ turns[0], jnp.where(t < 12, t ^ turns[1], t))
            for k in range(BRICK):
                new = jnp.where(t == places[k], k, new)
            scalars[26 * b + at] = new
        return carry

    lax.fori_loop(0, 26, rename, 0)
    for k in range(BRICK):
        scalars[PLACE + k] = places[k]
    scalars[SECOND] = jnp.where(picked[0, 0] == picked[0, 1], 0, 1)
    scalars[LIVE] = live[0]
    fetch.wait()


def make_taps(index, plain, taps, wide):
    low = lower_half((32, 128))
    zero = jnp.zeros((32, 128), F32)
    for t in range(9):
        even = [plain[pl.ds((3 * t + d) * 128 + index, 32, stride=4), :] for d in range(3)]
        odd = [pltpu.roll(rows, 64, 1) for rows in even]

        def rows(held, d):
            return held[d] if 0 <= d <= 2 else zero

        for w, base in ((0, 192), (1, 0), (2, 64), (3, 128)):
            wide[t % 2, pl.ds(base, 32, stride=2), :] = jnp.where(low, rows(even, w), rows(odd, w - 1))
            wide[t % 2, pl.ds(base + 1, 32, stride=2), :] = jnp.where(low, rows(odd, w), rows(even, w - 1))
        full = wide[t % 2]
        high = full.astype(BF16)
        taps[t, :, 0:128] = high
        taps[t, :, 128:256] = (full - high.astype(F32)).astype(BF16)


def first_taps_kernel(weights, plain, taps, wide):
    for t in range(27):
        for i in range(32):
            plain[128 * t + 4 * i : 128 * t + 4 * i + 4, :] = weights[t, :, 128 * i : 128 * i + 128]
    make_taps(0, plain, taps, wide)


def taps_kernel(index, after, plain, taps, wide):
    make_taps(index, plain, taps, wide)


def fill_table(faces, arrived, table):
    for k, ref in enumerate(faces):
        table[2 * k : 2 * k + 2] = ref[...]
    for k, ref in zip(ORDER, arrived):
        for e in range(2):
            unpack(ref, e, table, 4 + 2 * k + e)
    table[12] = jnp.zeros((FACE, 128), F32)


def fill_margins(pair, scalars, field, table, one, two):
    for x in range(8):
        one[(x + 1) * 80 + 8 : (x + 1) * 80 + 72, :] = field[x * 64 : x * 64 + 64, :]
    for b in range(2):
        near = 26 * scalars[PLACE + 2 * pair + b]

        def cell(xp, yp):
            return (xp * 10 + yp) * 8 + 4 * b

        for d in (-1, 1):
            s, p = (1, 0) if d < 0 else (0, 9)
            t = scalars[near + direction(d, 0, 0)]
            for i in range(8):
                at = cell(p, i + 1)
                one[at : at + 4, :] = table[t, 32 * s + 4 * i : 32 * s + 4 * i + 4, :]
            t = scalars[near + direction(0, d, 0)]
            for i in range(8):
                at = cell(i + 1, p)
                one[at : at + 4, :] = table[t, 64 + 32 * s + 4 * i : 64 + 32 * s + 4 * i + 4, :]
            for e in (-1, 1):
                y, py = (7, 0) if e < 0 else (0, 9)
                t = scalars[near + direction(d, e, 0)]
                at = cell(p, py)
                one[at : at + 4, :] = table[t, 32 * s + 4 * y : 32 * s + 4 * y + 4, :]
    low3 = lower_half((10, 8, 128))
    for c in range(10):
        rows = one[c * 80 : c * 80 + 80, :].reshape(10, 8, 128)
        both = jnp.where(low3, pltpu.roll(rows, 7, 1), pltpu.roll(rows, 1, 1))
        two[c * 80 : c * 80 + 80, :] = both.reshape(80, 128)
    low = lower_half((8, 128))
    low1 = lower_half((1, 128))
    for b in range(2):
        near = 26 * scalars[PLACE + 2 * pair + b]
        for dz in (-1, 1):
            def merge(start, stride, new):
                at = pl.ds(start, 8, stride=stride)
                old = two[at, :]
                two[at, :] = jnp.where(low, new, old) if dz > 0 else jnp.where(low, old, new)

            row = 4 * b + (3 if dz > 0 else 0)
            t = scalars[near + direction(0, 0, dz)]
            for x in range(8):
                merge(((x + 1) * 10 + 1) * 8 + row, 8, table[t, 128 + 8 * x : 136 + 8 * x, :])
            for d in (-1, 1):
                x, p = (7, 0) if d < 0 else (0, 9)
                t = scalars[near + direction(d, 0, dz)]
                merge((p * 10 + 1) * 8 + row, 8, table[t, 128 + 8 * x : 136 + 8 * x, :])
                t = scalars[near + direction(0, d, dz)]
                merge((10 + p) * 8 + row, 80, table[t, pl.ds(128 + x, 8, stride=8), :])
                for e in (-1, 1):
                    y, py = (7, 0) if e < 0 else (0, 9)
                    t = scalars[near + direction(d, e, dz)]
                    at = (p * 10 + py) * 8 + row
                    new = table[t, 128 + 8 * x + y : 129 + 8 * x + y, :]
                    old = two[at : at + 1, :]
                    two[at : at + 1, :] = jnp.where(low1, new, old) if dz > 0 else jnp.where(low1, old, new)


def split(one, two, high, rest, mid_high, mid_rest):
    for c in range(10):
        for half, ref in enumerate((one, two)):
            lanes = slice(128 * half, 128 * half + 128)
            full = ref[c * 80 : c * 80 + 80, :]
            top = full.astype(BF16)
            high[c, :, lanes] = top
            rest[c, :, lanes] = (full - top.astype(F32)).astype(BF16)
            full = ref[c * 80 + 8 : c * 80 + 72, :]
            top = full.astype(BF16)
            mid_high[c, :, lanes] = top
            mid_rest[c, :, lanes] = (full - top.astype(F32)).astype(BF16)


def convolve(high, rest, mid_high, mid_rest, taps):
    def rows(ref, mid, dx, dy):
        if dy == 1:
            return mid[dx : dx + 8].reshape(512, 256)
        return ref[dx : dx + 8, 8 * dy : 8 * dy + 64, :].reshape(512, 256)

    wide = None
    narrow = None
    for dx in range(3):
        for dy in range(3):
            kernel = taps[3 * dx + dy]
            part = jnp.dot(rows(high, mid_high, dx, dy), kernel, preferred_element_type=F32)
            wide = part if wide is None else wide + part
            part = jnp.dot(rows(rest, mid_rest, dx, dy), kernel[:, 0:128], preferred_element_type=F32)
            narrow = part if narrow is None else narrow + part
    return wide[:, 0:128] + (wide[:, 128:256] + narrow)


def run_pair(pair, index, scalars, field, table, taps, biases, skip, new, work):
    one, two, high, rest, mid_high, mid_rest = work
    fill_margins(pair, scalars, field, table, one, two)
    split(one, two, high, rest, mid_high, mid_rest)
    total = convolve(high, rest, mid_high, mid_rest, taps)
    bias = biases[index : index + 1, :]
    total = total + jnp.concatenate([bias, bias], 1)
    if skip is not None:
        total = total + skip[...]
    second = lax.broadcasted_iota(jnp.int32, (512, 128), 0) % 8 >= 4
    slot = jnp.where(second, scalars[PLACE + 2 * pair + 1], scalars[PLACE + 2 * pair])
    new[...] = jnp.where(slot < scalars[LIVE], jnp.maximum(total, 0.0), 0.0)


def near_kernel(residual, index, scalars, field, faces_a, faces_b, *refs):
    arrived, (taps, biases), refs = refs[:4], refs[4:6], refs[6:]
    skip, refs = (refs[0], refs[1:]) if residual else (None, refs)
    new, faces, send, table = refs[:4]
    fill_table((faces_a, faces_b), arrived, table)
    run_pair(0, index, scalars, field, table, taps, biases, skip, new, refs[4:])
    write_faces(new, faces)
    offer(scalars[SECOND], faces, send)


def far_kernel(residual, index, scalars, field, table, taps, biases, *refs):
    skip, refs = (refs[0], refs[1:]) if residual else (None, refs)
    new, faces = refs[:2]
    run_pair(1, index, scalars, field, table, taps, biases, skip, new, refs[2:])
    write_faces(new, faces)


def last_kernel(index, scalars, field_a, field_b, faces_a, faces_b, *refs):
    arrived, (taps, biases, skip_a, skip_b, out, table, new, stage, sems), work = refs[:4], refs[4:13], refs[13:]
    fill_table((faces_a, faces_b), arrived, table)
    copies = []
    for pair, field, skip in ((0, field_a, skip_a), (1, field_b, skip_b)):
        run_pair(pair, index, scalars, field, table, taps, biases, skip, new, work)
        for b in range(2):
            at = 2 * pair + b
            for x in range(8):
                for q in range(4):
                    stage[at, x, :, 128 * q : 128 * q + 128] = new[pl.ds(x * 64 + 4 * b + q, 8, stride=8), :]
            copies.append(pltpu.make_async_copy(stage.at[at], out.at[scalars[PLACE + at]], sems.at[at]))
            copies[-1].start()
    for copy in copies:
        copy.wait()


FIELD = jax.ShapeDtypeStruct((512, 128), F32)
FACES = jax.ShapeDtypeStruct((2, FACE, 128), F32)
SEND = jax.ShapeDtypeStruct((2, PACK, 128), F32)
TABLE = jax.ShapeDtypeStruct((13, FACE, 128), F32)
WORK = [
    pltpu.VMEM((800, 128), F32),
    pltpu.VMEM((800, 128), F32),
    pltpu.VMEM((10, 80, 256), BF16),
    pltpu.VMEM((10, 80, 256), BF16),
    pltpu.VMEM((10, 64, 256), BF16),
    pltpu.VMEM((10, 64, 256), BF16),
]


def swaps(size, first):
    pairs = [(i, i + 1) for i in range(first, size - 1, 2)]
    return pairs + [(b, a) for a, b in pairs]


def exchange(send):
    got = []
    for axis in ("space", "slab"):
        size = lax.axis_size(axis)
        got += [lax.ppermute(send, axis, swaps(size, first)) for first in (0, 1)]
    return [got[at] for at in ORDER]


def shards(features, live, rim_slots, neighbours, weights, biases):
    params = pltpu.CompilerParams(vmem_limit_bytes=24 * MIB)
    cost = pl.CostEstimate(flops=600_000_000, bytes_accessed=4 * MIB, transcendentals=0)
    convs = weights.shape[0]
    in_hbm = lambda array: pltpu.with_memory_space_constraint(array, pltpu.HBM)

    def call(kernel, name, out_shape, in_specs, scratch, args, out_specs=None):
        return pl.pallas_call(
            kernel,
            out_shape=out_shape,
            in_specs=in_specs,
            out_specs=tuple(VM for _ in out_shape) if out_specs is None else out_specs,
            scratch_shapes=scratch,
            compiler_params=params,
            cost_estimate=cost,
            name=name,
        )(*args)

    entry_scratch = [
        pltpu.VMEM(features.shape, F32),
        pltpu.SMEM((1, 2), jnp.int32),
        pltpu.SemaphoreType.DMA((2,)),
    ]
    field_a, faces_a, send = call(
        entry_kernel, "entry", (FIELD, FACES, SEND), [SM, HB, HB], entry_scratch,
        (live, in_hbm(rim_slots), in_hbm(features)),
    )
    turned = jnp.transpose(weights, (1, 0, 2))
    field_b, faces_b, held, scalars = call(
        second_entry_kernel,
        "second_entry",
        (FIELD, FACES, jax.ShapeDtypeStruct(turned.shape, F32), jax.ShapeDtypeStruct((LIVE + 1,), jnp.int32)),
        [pl.BlockSpec(memory_space=pl.ANY), SM, HB, HB, HB, HB],
        entry_scratch + [pltpu.SMEM(neighbours.shape, jnp.int32), pltpu.SemaphoreType.DMA((2,))],
        (send, live, in_hbm(rim_slots), in_hbm(features), in_hbm(turned), in_hbm(neighbours)),
        (VM, VM, VM, SM),
    )
    plain = None

    def taps_of(index, send):
        nonlocal plain
        shape = jax.ShapeDtypeStruct((9, 256, 256), BF16)
        scratch = [pltpu.VMEM((2, 256, 128), F32)]
        if index == 0:
            wide = jax.ShapeDtypeStruct((27 * 32 * convs, 128), F32)
            plain, taps = call(first_taps_kernel, "taps0", (wide, shape), [VM], scratch, (held,))
            return taps
        kernel = functools.partial(taps_kernel, index)
        specs = [pl.BlockSpec(memory_space=pl.ANY), VM]
        return call(kernel, f"taps{index}", (shape,), specs, scratch, (send, plain))[0]

    def layer(index, fields, faces, send, skips):
        arrived = exchange(send)
        taps = taps_of(index, send)
        args = [scalars, fields[0], *faces, *arrived, taps, biases]
        if skips is not None:
            args.append(skips[0])
        kernel = functools.partial(near_kernel, skips is not None, index)
        specs = [SM] + [VM] * (len(args) - 1)
        new_a, faces_a, send, table = call(
            kernel, f"near{index}", (FIELD, FACES, SEND, TABLE), specs, WORK, args
        )
        args = [scalars, fields[1], table, taps, biases]
        if skips is not None:
            args.append(skips[1])
        kernel = functools.partial(far_kernel, skips is not None, index)
        specs = [SM] + [VM] * (len(args) - 1)
        new_b, faces_b = call(kernel, f"far{index}", (FIELD, FACES), specs, WORK, args)
        return (new_a, new_b), (faces_a, faces_b), send

    def finish(index, fields, faces, send, skips):
        arrived = exchange(send)
        taps = taps_of(index, send)
        args = [scalars, *fields, *faces, *arrived, taps, biases, *skips]
        scratch = [
            pltpu.VMEM(TABLE.shape, F32),
            pltpu.VMEM(FIELD.shape, F32),
            pltpu.VMEM(features.shape, F32),
            pltpu.SemaphoreType.DMA((BRICK,)),
        ]
        out = (jax.ShapeDtypeStruct(features.shape, F32),)
        kernel = functools.partial(last_kernel, index)
        specs = [SM] + [VM] * (len(args) - 1)
        return call(kernel, f"last{index}", out, specs, scratch + WORK, args, (HB,))[0]

    state = (field_a, field_b), (faces_a, faces_b), send
    for index in range(0, convs, 2):
        skips = state[0]
        state = layer(index, *state, None)
        if index + 2 == convs:
            return finish(index + 1, *state, skips)
        state = layer(index + 1, *state, skips)


def solution(mesh):
    in_specs = (
        P(("space", "slab"), None, None, None),
        P(("space", "slab")),
        P(("space", "slab"), None),
        P(("space", "slab"), None),
        P(),
        P(),
    )
    out_specs = P(("space", "slab"), None, None, None)
    return jax.shard_map(shards, mesh=mesh, in_specs=in_specs, out_specs=out_specs, check_vma=False)
```

time: 70.1 us -> 58.5 us (0.83)
  the two profiles are of different devices: /device:TPU:96 before, /device:TPU:75 now
where the time goes in v2:
time: 58.5 us; the launch traced here: 58.1 us
  starting transfers between devices  28.3 us (48%)
  Pallas kernels  22.8 us (39%)
  waiting for transfers between devices  5.78 us (10%)
  between operations  1.09 us (2%)
    ppermute x16, starting transfers between devices, exchange(): got += [lax.ppermute(send, axis, swaps(size, first)) for first in (0, 1)]  28.3 us
    pallas_call x13, Pallas kernels, call(): pl.pallas_call(kernel, out_shape=out_shape, in_specs=in_specs, out_specs=...  22.8 us
    ppermute x16, waiting for transfers between devices, exchange(): got += [lax.ppermute(send, axis, swaps(size, first)) for first in (0, 1)]  5.78 us
  transfers between devices with their start and end apart: 16, of which 4 were waited for; matrix products, arithmetic and copies ran while one was open for 0% of the time, Pallas kernels for 18%

profile of v2, /device:TPU:75, one launch (start us, length us, event | category | flops | bytes accessed | tf_op | source)
XLA Modules:
  0.0 58.1 jit_solution(11874858264943267256)
XLA Ops:
  0.7 1.2 %entry.1 = (f32[512,128]{1,0:T(8,128)S(1)}, f32[2,192,128]{2,1,0:T(8,128)S(1)}, f32[2,152,128]{2,1,0:T(8,128)S(1)}) custom-call(s32[1]{0:T(128)S(6)} %copy.7.live, s32[1,2]{1,0:T(1,128)} %slots.3, f32[4,8,8,512]{3,2,1,0:T(8,128)} %feat.3), custom_call_target="tpu_custom_call" | custom-call | flops 600000000 | bytes 4194304 | tf_op jit(solution)/shard_map/entry/pallas_call | solution.py:352
  1.8 3.8 %collective-permute-start.3 = (f32[2,152,128]{2,1,0:T(8,128)S(1)}, f32[2,152,128]{2,1,0:T(8,128)S(1)}, u32[]{:S(2)}, u32[]{:S(2)}) collective-permute-start(f32[2,152,128]{2,1,0:T(8,128)S(1)} %get-tuple-element.32.after), channel_id=1, source_target_pairs={{4,8},{12,16},{20,24},{28,32},{36,40},{44,48},{52,56},{60,64},{68,... | collective-permute-start | bytes 466952 | tf_op jit(solution)/shard_map/ppermute | solution.py:341
  5.6 0.3 collective-permute-start.2
  5.9 3.8 %collective-permute-start.1 = (f32[2,152,128]{2,1,0:T(8,128)S(1)}, f32[2,152,128]{2,1,0:T(8,128)S(1)}, u32[]{:S(2)}, u32[]{:S(2)}) collective-permute-start(f32[2,152,128]{2,1,0:T(8,128)S(1)} %get-tuple-element.32.after), channel_id=1, source_target_pairs={{1,2},{2,1},{5,6},{6,5},{9,10},{10,9},{13,14},{14,13},{17,18},{18,... | collective-permute-start | bytes 466952 | tf_op jit(solution)/shard_map/ppermute | solution.py:341
  9.7 0.1 collective-permute-start
  9.8 3.0 %second_entry.1 = (f32[512,128]{1,0:T(8,128)S(1)}, f32[2,192,128]{2,1,0:T(8,128)S(1)}, f32[27,4,4096]{2,1,0:T(4,128)S(1)}, s32[110]{0:T(128)S(1)}) custom-call(f32[2,152,128]{2,1,0:T(8,128)S(1)} %get-tuple-element.32.after, s32[1]{0:T(128)S(6)} %copy.7.live, s32[1,2]{1,0:T(1,128)} %slots.3, f32[4,8,8,512]{3,2,1,0:T(8,128)} %feat.3, f32[27,4,4096]{2,1,0:T(4,128)} %bitcast.1, ...), custom_call_target="tpu_custom_call" | custom-call | flops 600000000 | bytes 4194304 | tf_op jit(solution)/shard_map/second_entry/pallas_call | solution.py:352
  12.8 0.4 taps0.1
  13.3 0.2 copy-done
  13.5 2.2 %near0.1 = (f32[512,128]{1,0:T(8,128)S(1)}, f32[2,192,128]{2,1,0:T(8,128)S(1)}, f32[2,152,128]{2,1,0:T(8,128)S(1)}, f32[13,192,128]{2,1,0:T(8,128)S(1)}) custom-call(s32[110]{0:T(128)S(1)} %get-tuple-element.33.scalars, f32[512,128]{1,0:T(8,128)S(1)} %get-tuple-element.34.field.refs_6_, f32[2,192,128]{2,1,0:T(8,128)S(1)} %get-tuple-element.35.faces_a, ...), custom_call_target="tpu_custom_call" | custom-call | flops 600000000 | bytes 4194304 | tf_op jit(solution)/shard_map/near0/pallas_call | solution.py:352
  15.7 3.3 %collective-permute-start.7 = (f32[2,152,128]{2,1,0:T(8,128)S(1)}, f32[2,152,128]{2,1,0:T(8,128)S(1)}, u32[]{:S(2)}, u32[]{:S(2)}) collective-permute-start(f32[2,152,128]{2,1,0:T(8,128)S(1)} %get-tuple-element.44.after), channel_id=1, source_target_pairs={{4,8},{12,16},{20,24},{28,32},{36,40},{44,48},{52,56},{60,64},{68,... | collective-permute-start | bytes 466952 | tf_op jit(solution)/shard_map/ppermute | solution.py:341
  19.1 3.8 %collective-permute-start.5 = (f32[2,152,128]{2,1,0:T(8,128)S(1)}, f32[2,152,128]{2,1,0:T(8,128)S(1)}, u32[]{:S(2)}, u32[]{:S(2)}) collective-permute-start(f32[2,152,128]{2,1,0:T(8,128)S(1)} %get-tuple-element.44.after), channel_id=1, source_target_pairs={{1,2},{2,1},{5,6},{6,5},{9,10},{10,9},{13,14},{14,13},{17,18},{18,... | collective-permute-start | bytes 466952 | tf_op jit(solution)/shard_map/ppermute | solution.py:341
  22.9 0.1 collective-permute-start.4
  23.0 0.4 taps1.1.refs_4_.taps
  23.3 2.1 %far0.1 = (f32[512,128]{1,0:T(8,128)S(1)}, f32[2,192,128]{2,1,0:T(8,128)S(1)}) custom-call(s32[110]{0:T(128)S(1)} %get-tuple-element.33.scalars, f32[512,128]{1,0:T(8,128)S(1)} %get-tuple-element.41.field.refs_0_, f32[13,192,128]{2,1,0:T(8,128)S(1)} %get-tuple-element.42.table, bf16[9,256,256]{2,1,0:T(8,128)(2,1)S(1)} %get-tuple-element.38.refs_4_.taps, ...), custom_call_target="tpu_custom_call" | custom-call | flops 600000000 | bytes 4194304 | tf_op jit(solution)/shard_map/far0/pallas_call | solution.py:352
  25.4 1.5 %collective-permute-done.5.refs_1_ = f32[2,152,128]{2,1,0:T(8,128)S(1)} collective-permute-done((f32[2,152,128]{2,1,0:T(8,128)S(1)}, f32[2,152,128]{2,1,0:T(8,128)S(1)}, u32[]{:S(2)}, u32[]{:S(2)}) %collective-permute-start.5) | collective-permute-done | bytes 155680 | tf_op jit(solution)/shard_map/ppermute | solution.py:341
  26.9 2.2 %near1.1 = (f32[512,128]{1,0:T(8,128)S(1)}, f32[2,192,128]{2,1,0:T(8,128)S(1)}, f32[2,152,128]{2,1,0:T(8,128)S(1)}, f32[13,192,128]{2,1,0:T(8,128)S(1)}) custom-call(s32[110]{0:T(128)S(1)} %get-tuple-element.33.scalars, f32[512,128]{1,0:T(8,128)S(1)} %get-tuple-element.39.field, f32[2,192,128]{2,1,0:T(8,128)S(1)} %get-tuple-element.40.faces_a, ...), custom_call_target="tpu_custom_call" | custom-call | flops 600000000 | bytes 4194304 | tf_op jit(solution)/shard_map/near1/pallas_call | solution.py:352
  29.1 2.5 %collective-permute-start.11 = (f32[2,152,128]{2,1,0:T(8,128)S(1)}, f32[2,152,128]{2,1,0:T(8,128)S(1)}, u32[]{:S(2)}, u32[]{:S(2)}) collective-permute-start(f32[2,152,128]{2,1,0:T(8,128)S(1)} %get-tuple-element.51.after), channel_id=1, source_target_pairs={{4,8},{12,16},{20,24},{28,32},{36,40},{44,48},{52,56},{60,64},{68,... | collective-permute-start | bytes 466952 | tf_op jit(solution)/shard_map/ppermute | solution.py:341
  31.7 3.5 %collective-permute-start.9 = (f32[2,152,128]{2,1,0:T(8,128)S(1)}, f32[2,152,128]{2,1,0:T(8,128)S(1)}, u32[]{:S(2)}, u32[]{:S(2)}) collective-permute-start(f32[2,152,128]{2,1,0:T(8,128)S(1)} %get-tuple-element.51.after), channel_id=1, source_target_pairs={{1,2},{2,1},{5,6},{6,5},{9,10},{10,9},{13,14},{14,13},{17,18},{18,... | collective-permute-start | bytes 466952 | tf_op jit(solution)/shard_map/ppermute | solution.py:341
  35.3 0.1 collective-permute-start.8
  35.4 0.4 taps2.1.refs_4_.taps
  35.7 2.1 %far1.1 = (f32[512,128]{1,0:T(8,128)S(1)}, f32[2,192,128]{2,1,0:T(8,128)S(1)}) custom-call(s32[110]{0:T(128)S(1)} %get-tuple-element.33.scalars, f32[512,128]{1,0:T(8,128)S(1)} %get-tuple-element.48.field, f32[13,192,128]{2,1,0:T(8,128)S(1)} %get-tuple-element.49.table, bf16[9,256,256]{2,1,0:T(8,128)(2,1)S(1)} %taps1.1.refs_4_.taps, f32[4,64]{1,0:T(4,128)S(1)} %copy-done, ...), custom_call_target="tpu_custom_call" | custom-call | flops 600000000 | bytes 4194304 | tf_op jit(solution)/shard_map/far1/pallas_call | solution.py:352
  37.8 1.4 %collective-permute-done.9.refs_1_ = f32[2,152,128]{2,1,0:T(8,128)S(1)} collective-permute-done((f32[2,152,128]{2,1,0:T(8,128)S(1)}, f32[2,152,128]{2,1,0:T(8,128)S(1)}, u32[]{:S(2)}, u32[]{:S(2)}) %collective-permute-start.9) | collective-permute-done | bytes 155680 | tf_op jit(solution)/shard_map/ppermute | solution.py:341
  39.2 2.2 %near2.1 = (f32[512,128]{1,0:T(8,128)S(1)}, f32[2,192,128]{2,1,0:T(8,128)S(1)}, f32[2,152,128]{2,1,0:T(8,128)S(1)}, f32[13,192,128]{2,1,0:T(8,128)S(1)}) custom-call(s32[110]{0:T(128)S(1)} %get-tuple-element.33.scalars, f32[512,128]{1,0:T(8,128)S(1)} %get-tuple-element.46.field.refs_6_, f32[2,192,128]{2,1,0:T(8,128)S(1)} %get-tuple-element.47.faces_a, ...), custom_call_target="tpu_custom_call" | custom-call | flops 600000000 | bytes 4194304 | tf_op jit(solution)/shard_map/near2/pallas_call | solution.py:352
  41.4 4.2 %collective-permute-start.15 = (f32[2,152,128]{2,1,0:T(8,128)S(1)}, f32[2,152,128]{2,1,0:T(8,128)S(1)}, u32[]{:S(2)}, u32[]{:S(2)}) collective-permute-start(f32[2,152,128]{2,1,0:T(8,128)S(1)} %get-tuple-element.58.after), channel_id=1, source_target_pairs={{4,8},{12,16},{20,24},{28,32},{36,40},{44,48},{52,56},{60,64},{68,... | collective-permute-start | bytes 466952 | tf_op jit(solution)/shard_map/ppermute | solution.py:341
  45.7 0.1 collective-permute-start.14
  45.8 2.3 %collective-permute-start.13 = (f32[2,152,128]{2,1,0:T(8,128)S(1)}, f32[2,152,128]{2,1,0:T(8,128)S(1)}, u32[]{:S(2)}, u32[]{:S(2)}) collective-permute-start(f32[2,152,128]{2,1,0:T(8,128)S(1)} %get-tuple-element.58.after), channel_id=1, source_target_pairs={{1,2},{2,1},{5,6},{6,5},{9,10},{10,9},{13,14},{14,13},{17,18},{18,... | collective-permute-start | bytes 466952 | tf_op jit(solution)/shard_map/ppermute | solution.py:341
  48.1 0.3 collective-permute-start.12
  48.4 0.4 taps3.1.refs_4_
  48.7 2.1 %far2.1 = (f32[512,128]{1,0:T(8,128)S(1)}, f32[2,192,128]{2,1,0:T(8,128)S(1)}) custom-call(s32[110]{0:T(128)S(1)} %get-tuple-element.33.scalars, f32[512,128]{1,0:T(8,128)S(1)} %get-tuple-element.53.field.refs_7_, f32[13,192,128]{2,1,0:T(8,128)S(1)} %get-tuple-element.54.table, bf16[9,256,256]{2,1,0:T(8,128)(2,1)S(1)} %taps2.1.refs_4_.taps, f32[4,64]{1,0:T(4,128)S(1)} %copy-done), custom_call_target="tpu_custom_call" | custom-call | flops 600000000 | bytes 4194304 | tf_op jit(solution)/shard_map/far2/pallas_call | solution.py:352
  50.8 1.0 %collective-permute-done.14.refs_2_ = f32[2,152,128]{2,1,0:T(8,128)S(1)} collective-permute-done((f32[2,152,128]{2,1,0:T(8,128)S(1)}, f32[2,152,128]{2,1,0:T(8,128)S(1)}, u32[]{:S(2)}, u32[]{:S(2)}) %collective-permute-start.14) | collective-permute-done | bytes 155680 | tf_op jit(solution)/shard_map/ppermute | solution.py:341
  51.8 1.9 %collective-permute-done.13.refs_1_ = f32[2,152,128]{2,1,0:T(8,128)S(1)} collective-permute-done((f32[2,152,128]{2,1,0:T(8,128)S(1)}, f32[2,152,128]{2,1,0:T(8,128)S(1)}, u32[]{:S(2)}, u32[]{:S(2)}) %collective-permute-start.13) | collective-permute-done | bytes 155680 | tf_op jit(solution)/shard_map/ppermute | solution.py:341
  53.7 4.3 %last3.1 = f32[4,8,8,512]{3,2,1,0:T(8,128)} custom-call(s32[110]{0:T(128)S(1)} %get-tuple-element.33.scalars, f32[512,128]{1,0:T(8,128)S(1)} %get-tuple-element.52.field_a, f32[512,128]{1,0:T(8,128)S(1)} %get-tuple-element.55.field_b, f32[2,192,128]{2,1,0:T(8,128)S(1)} %get-tuple-element.56.faces_a, f32[2,192,128]{2,1,0:T(8,128)S(1)} %get-tuple-element.57.faces_b, ...), custom_call_target="tpu_custom_call" | custom-call | flops 600000000 | bytes 4194304 | tf_op jit(solution)/shard_map/last3/pallas_call | solution.py:352
  (15 shorter events, 0.2 us)
Async XLA Ops:
  1.8 11.4 %collective-permute-start.3 = (f32[2,152,128]{2,1,0:T(8,128)S(1)}, f32[2,152,128]{2,1,0:T(8,128)S(1)}, u32[]{:S(2)}, u32[]{:S(2)}) collective-permute-start(f32[2,152,128]{2,1,0:T(8,128)S(1)} %get-tuple-element.32.after), channel_id=1, source_target_pairs={{4,8},{12,16},{20,24},{28,32},{36,40},{44,48},{52,56},{60,64},{68,... | collective-permute-start | bytes 466952 | tf_op jit(solution)/shard_map/ppermute | solution.py:341
  5.6 7.7 %collective-permute-start.2 = (f32[2,152,128]{2,1,0:T(8,128)S(1)}, f32[2,152,128]{2,1,0:T(8,128)S(1)}, u32[]{:S(2)}, u32[]{:S(2)}) collective-permute-start(f32[2,152,128]{2,1,0:T(8,128)S(1)} %get-tuple-element.32.after), channel_id=1, source_target_pairs={{0,1},{2,3},{1,0},{3,2},{4,5},{6,7},{5,4},{7,6},{8,9},{10,11},{9,8... | collective-permute-start | bytes 466952 | tf_op jit(solution)/shard_map/ppermute | solution.py:341
  5.9 7.3 %collective-permute-start.1 = (f32[2,152,128]{2,1,0:T(8,128)S(1)}, f32[2,152,128]{2,1,0:T(8,128)S(1)}, u32[]{:S(2)}, u32[]{:S(2)}) collective-permute-start(f32[2,152,128]{2,1,0:T(8,128)S(1)} %get-tuple-element.32.after), channel_id=1, source_target_pairs={{1,2},{2,1},{5,6},{6,5},{9,10},{10,9},{13,14},{14,13},{17,18},{18,... | collective-permute-start | bytes 466952 | tf_op jit(solution)/shard_map/ppermute | solution.py:341
  9.7 3.6 %collective-permute-start = (f32[2,152,128]{2,1,0:T(8,128)S(1)}, f32[2,152,128]{2,1,0:T(8,128)S(1)}, u32[]{:S(2)}, u32[]{:S(2)}) collective-permute-start(f32[2,152,128]{2,1,0:T(8,128)S(1)} %get-tuple-element.32.after), channel_id=1, source_target_pairs={{0,4},{8,12},{16,20},{24,28},{32,36},{40,44},{48,52},{56,60},{64,6... | collective-permute-start | bytes 466952 | tf_op jit(solution)/shard_map/ppermute | solution.py:341
  12.8 0.7 %copy-start = (f32[4,64]{1,0:T(4,128)S(1)}, f32[4,64]{1,0:T(4,128)}, u32[]{:S(2)}) copy-start(f32[4,64]{1,0:T(4,128)} %refs_5_.7) | copy-start | bytes 3076
  15.7 9.7 %collective-permute-start.7 = (f32[2,152,128]{2,1,0:T(8,128)S(1)}, f32[2,152,128]{2,1,0:T(8,128)S(1)}, u32[]{:S(2)}, u32[]{:S(2)}) collective-permute-start(f32[2,152,128]{2,1,0:T(8,128)S(1)} %get-tuple-element.44.after), channel_id=1, source_target_pairs={{4,8},{12,16},{20,24},{28,32},{36,40},{44,48},{52,56},{60,64},{68,... | collective-permute-start | bytes 466952 | tf_op jit(solution)/shard_map/ppermute | solution.py:341
  19.0 6.4 %collective-permute-start.6 = (f32[2,152,128]{2,1,0:T(8,128)S(1)}, f32[2,152,128]{2,1,0:T(8,128)S(1)}, u32[]{:S(2)}, u32[]{:S(2)}) collective-permute-start(f32[2,152,128]{2,1,0:T(8,128)S(1)} %get-tuple-element.44.after), channel_id=1, source_target_pairs={{0,1},{2,3},{1,0},{3,2},{4,5},{6,7},{5,4},{7,6},{8,9},{10,11},{9,8... | collective-permute-start | bytes 466952 | tf_op jit(solution)/shard_map/ppermute | solution.py:341
  19.1 7.8 %collective-permute-start.5 = (f32[2,152,128]{2,1,0:T(8,128)S(1)}, f32[2,152,128]{2,1,0:T(8,128)S(1)}, u32[]{:S(2)}, u32[]{:S(2)}) collective-permute-start(f32[2,152,128]{2,1,0:T(8,128)S(1)} %get-tuple-element.44.after), channel_id=1, source_target_pairs={{1,2},{2,1},{5,6},{6,5},{9,10},{10,9},{13,14},{14,13},{17,18},{18,... | collective-permute-start | bytes 466952 | tf_op jit(solution)/shard_map/ppermute | solution.py:341
  22.9 4.0 %collective-permute-start.4 = (f32[2,152,128]{2,1,0:T(8,128)S(1)}, f32[2,152,128]{2,1,0:T(8,128)S(1)}, u32[]{:S(2)}, u32[]{:S(2)}) collective-permute-start(f32[2,152,128]{2,1,0:T(8,128)S(1)} %get-tuple-element.44.after), channel_id=1, source_target_pairs={{0,4},{8,12},{16,20},{24,28},{32,36},{40,44},{48,52},{56,60},{64,6... | collective-permute-start | bytes 466952 | tf_op jit(solution)/shard_map/ppermute | solution.py:341
  29.1 8.7 %collective-permute-start.11 = (f32[2,152,128]{2,1,0:T(8,128)S(1)}, f32[2,152,128]{2,1,0:T(8,128)S(1)}, u32[]{:S(2)}, u32[]{:S(2)}) collective-permute-start(f32[2,152,128]{2,1,0:T(8,128)S(1)} %get-tuple-element.51.after), channel_id=1, source_target_pairs={{4,8},{12,16},{20,24},{28,32},{36,40},{44,48},{52,56},{60,64},{68,... | collective-permute-start | bytes 466952 | tf_op jit(solution)/shard_map/ppermute | solution.py:341
  31.6 6.2 %collective-permute-start.10 = (f32[2,152,128]{2,1,0:T(8,128)S(1)}, f32[2,152,128]{2,1,0:T(8,128)S(1)}, u32[]{:S(2)}, u32[]{:S(2)}) collective-permute-start(f32[2,152,128]{2,1,0:T(8,128)S(1)} %get-tuple-element.51.after), channel_id=1, source_target_pairs={{0,1},{2,3},{1,0},{3,2},{4,5},{6,7},{5,4},{7,6},{8,9},{10,11},{9,8... | collective-permute-start | bytes 466952 | tf_op jit(solution)/shard_map/ppermute | solution.py:341
  31.7 7.5 %collective-permute-start.9 = (f32[2,152,128]{2,1,0:T(8,128)S(1)}, f32[2,152,128]{2,1,0:T(8,128)S(1)}, u32[]{:S(2)}, u32[]{:S(2)}) collective-permute-start(f32[2,152,128]{2,1,0:T(8,128)S(1)} %get-tuple-element.51.after), channel_id=1, source_target_pairs={{1,2},{2,1},{5,6},{6,5},{9,10},{10,9},{13,14},{14,13},{17,18},{18,... | collective-permute-start | bytes 466952 | tf_op jit(solution)/shard_map/ppermute | solution.py:341
  35.3 4.0 %collective-permute-start.8 = (f32[2,152,128]{2,1,0:T(8,128)S(1)}, f32[2,152,128]{2,1,0:T(8,128)S(1)}, u32[]{:S(2)}, u32[]{:S(2)}) collective-permute-start(f32[2,152,128]{2,1,0:T(8,128)S(1)} %get-tuple-element.51.after), channel_id=1, source_target_pairs={{0,4},{8,12},{16,20},{24,28},{32,36},{40,44},{48,52},{56,60},{64,6... | collective-permute-start | bytes 466952 | tf_op jit(solution)/shard_map/ppermute | solution.py:341
  41.4 9.4 %collective-permute-start.15 = (f32[2,152,128]{2,1,0:T(8,128)S(1)}, f32[2,152,128]{2,1,0:T(8,128)S(1)}, u32[]{:S(2)}, u32[]{:S(2)}) collective-permute-start(f32[2,152,128]{2,1,0:T(8,128)S(1)} %get-tuple-element.58.after), channel_id=1, source_target_pairs={{4,8},{12,16},{20,24},{28,32},{36,40},{44,48},{52,56},{60,64},{68,... | collective-permute-start | bytes 466952 | tf_op jit(solution)/shard_map/ppermute | solution.py:341
  45.7 6.1 %collective-permute-start.14 = (f32[2,152,128]{2,1,0:T(8,128)S(1)}, f32[2,152,128]{2,1,0:T(8,128)S(1)}, u32[]{:S(2)}, u32[]{:S(2)}) collective-permute-start(f32[2,152,128]{2,1,0:T(8,128)S(1)} %get-tuple-element.58.after), channel_id=1, source_target_pairs={{0,1},{2,3},{1,0},{3,2},{4,5},{6,7},{5,4},{7,6},{8,9},{10,11},{9,8... | collective-permute-start | bytes 466952 | tf_op jit(solution)/shard_map/ppermute | solution.py:341
  45.8 7.9 %collective-permute-start.13 = (f32[2,152,128]{2,1,0:T(8,128)S(1)}, f32[2,152,128]{2,1,0:T(8,128)S(1)}, u32[]{:S(2)}, u32[]{:S(2)}) collective-permute-start(f32[2,152,128]{2,1,0:T(8,128)S(1)} %get-tuple-element.58.after), channel_id=1, source_target_pairs={{1,2},{2,1},{5,6},{6,5},{9,10},{10,9},{13,14},{14,13},{17,18},{18,... | collective-permute-start | bytes 466952 | tf_op jit(solution)/shard_map/ppermute | solution.py:341
  48.1 5.6 %collective-permute-start.12 = (f32[2,152,128]{2,1,0:T(8,128)S(1)}, f32[2,152,128]{2,1,0:T(8,128)S(1)}, u32[]{:S(2)}, u32[]{:S(2)}) collective-permute-start(f32[2,152,128]{2,1,0:T(8,128)S(1)} %get-tuple-element.58.after), channel_id=1, source_target_pairs={{0,4},{8,12},{16,20},{24,28},{32,36},{40,44},{48,52},{56,60},{64,6... | collective-permute-start | bytes 466952 | tf_op jit(solution)/shard_map/ppermute | solution.py:341

commit v3 on v2

--- a/solution.py
+++ b/solution.py
@@ -250,21 +250,28 @@
 
 
 def convolve(high, rest, mid_high, mid_rest, taps):
-    def rows(ref, mid, dx, dy):
+    def rows(ref, mid, dx, dy, planes=8):
         if dy == 1:
-            return mid[dx : dx + 8].reshape(512, 256)
-        return ref[dx : dx + 8, 8 * dy : 8 * dy + 64, :].reshape(512, 256)
+            return mid[dx : dx + planes].reshape(64 * planes, 256)
+        return ref[dx : dx + planes, 8 * dy : 8 * dy + 64, :].reshape(64 * planes, 256)
+
+    def product(left, right):
+        return jnp.dot(left, right, preferred_element_type=F32)
 
     wide = None
-    narrow = None
     for dx in range(3):
         for dy in range(3):
-            kernel = taps[3 * dx + dy]
-            part = jnp.dot(rows(high, mid_high, dx, dy), kernel, preferred_element_type=F32)
+            part = product(rows(high, mid_high, dx, dy), taps[3 * dx + dy])
             wide = part if wide is None else wide + part
-            part = jnp.dot(rows(rest, mid_rest, dx, dy), kernel[:, 0:128], preferred_element_type=F32)
-            narrow = part if narrow is None else narrow + part
-    return wide[:, 0:128] + (wide[:, 128:256] + narrow)
+    total = wide[:, 0:128] + wide[:, 128:256]
+    for dy in range(3):
+        two = jnp.concatenate([taps[dy, :, 0:128], taps[3 + dy, :, 0:128]], 1)
+        part = product(rows(rest, mid_rest, 0, dy, 9), two)
+        total = total + (part[0:512, 0:128] + part[64:576, 128:256])
+    two = jnp.concatenate([taps[6, :, 0:128], taps[7, :, 0:128]], 1)
+    part = product(rest[2:10].reshape(640, 256), two).reshape(8, 80, 256)
+    total = total + (part[:, 0:64, 0:128] + part[:, 8:72, 128:256]).reshape(512, 128)
+    return total + product(rows(rest, mid_rest, 2, 2), taps[8, :, 0:128])
 
 
 def run_pair(pair, index, scalars, field, table, taps, biases, skip, new, work):
@@ -299,11 +306,12 @@
 
 
 def last_kernel(index, scalars, field_a, field_b, faces_a, faces_b, *refs):
-    arrived, (taps, biases, skip_a, skip_b, out, table, new, stage, sems), work = refs[:4], refs[4:13], refs[13:]
+    arrived, (taps, biases, skip_a, skip_b, out, table, new_a, new_b, stage, sems), work = refs[:4], refs[4:14], refs[14:]
     fill_table((faces_a, faces_b), arrived, table)
     copies = []
-    for pair, field, skip in ((0, field_a, skip_a), (1, field_b, skip_b)):
-        run_pair(pair, index, scalars, field, table, taps, biases, skip, new, work)
+    for pair, field, skip, new in ((0, field_a, skip_a, new_a), (1, field_b, skip_b, new_b)):
+        own = work[6 * pair : 6 * pair + 6]
+        run_pair(pair, index, scalars, field, table, taps, biases, skip, new, own)
         for b in range(2):
             at = 2 * pair + b
             for x in range(8):
@@ -373,7 +381,7 @@
     field_b, faces_b, held, scalars = call(
         second_entry_kernel,
         "second_entry",
-        (FIELD, FACES, jax.ShapeDtypeStruct(turned.shape, F32), jax.ShapeDtypeStruct((LIVE + 1,), jnp.int32)),
+        (FIELD, FACES, jax.ShapeDtypeStruct(turned.shape, F32), pltpu.SMEM((LIVE + 1,), jnp.int32)),
         [pl.BlockSpec(memory_space=pl.ANY), SM, HB, HB, HB, HB],
         entry_scratch + [pltpu.SMEM(neighbours.shape, jnp.int32), pltpu.SemaphoreType.DMA((2,))],
         (send, live, in_hbm(rim_slots), in_hbm(features), in_hbm(turned), in_hbm(neighbours)),
@@ -419,13 +427,14 @@
         scratch = [
             pltpu.VMEM(TABLE.shape, F32),
             pltpu.VMEM(FIELD.shape, F32),
+            pltpu.VMEM(FIELD.shape, F32),
             pltpu.VMEM(features.shape, F32),
             pltpu.SemaphoreType.DMA((BRICK,)),
         ]
         out = (jax.ShapeDtypeStruct(features.shape, F32),)
         kernel = functools.partial(last_kernel, index)
         specs = [SM] + [VM] * (len(args) - 1)
-        return call(kernel, f"last{index}", out, specs, scratch + WORK, args, (HB,))[0]
+        return call(kernel, f"last{index}", out, specs, scratch + WORK + WORK, args, (HB,))[0]
 
     state = (field_a, field_b), (faces_a, faces_b), send
     for index in range(0, convs, 2):

time: 58.5 us -> 55.3 us (0.945)
  Pallas kernels: 22.8 us -> 16.9 us
  waiting for transfers between devices: 5.78 us -> 8.98 us
    pallas_call x13, Pallas kernels: 22.8 us -> 16.9 us  [call(): pl.pallas_call(kernel, out_shape=out_shape, in_specs=in_specs, out_specs=...]
    ppermute x16, waiting for transfers between devices: 5.78 us -> 8.98 us  [exchange(): got += [lax.ppermute(send, axis, swaps(size, first)) for first in (0, 1)]]
  transfers between devices with their start and end apart: 16 -> 16, of which waited for: 4 -> 5; matrix products, arithmetic and copies ran while one was open for 0% -> 0% of each run, Pallas kernels for 18% -> 14%
where the time goes in v3:
time: 55.3 us; the launch traced here: 54.9 us
  starting transfers between devices  28 us (51%)
  Pallas kernels  16.9 us (31%)
  waiting for transfers between devices  8.98 us (16%)
  between operations  1.07 us (2%)
    ppermute x16, starting transfers between devices, exchange(): got += [lax.ppermute(send, axis, swaps(size, first)) for first in (0, 1)]  28 us
    pallas_call x13, Pallas kernels, call(): pl.pallas_call(kernel, out_shape=out_shape, in_specs=in_specs, out_specs=...  16.9 us
    ppermute x16, waiting for transfers between devices, exchange(): got += [lax.ppermute(send, axis, swaps(size, first)) for first in (0, 1)]  8.98 us
  transfers between devices with their start and end apart: 16, of which 5 were waited for; matrix products, arithmetic and copies ran while one was open for 0% of the time, Pallas kernels for 14%

profile of v3, /device:TPU:75, one launch (start us, length us, event | category | flops | bytes accessed | tf_op | source)
XLA Modules:
  0.0 54.9 jit_solution(4350293655985063587)
XLA Ops:
  0.7 1.2 %entry.1 = (f32[512,128]{1,0:T(8,128)S(1)}, f32[2,192,128]{2,1,0:T(8,128)S(1)}, f32[2,152,128]{2,1,0:T(8,128)S(1)}) custom-call(s32[1]{0:T(128)S(6)} %copy.7.live, s32[1,2]{1,0:T(1,128)} %slots.3, f32[4,8,8,512]{3,2,1,0:T(8,128)} %feat.3), custom_call_target="tpu_custom_call" | custom-call | flops 600000000 | bytes 4194304 | tf_op jit(solution)/shard_map/entry/pallas_call | solution.py:360
  1.8 3.8 %collective-permute-start.3 = (f32[2,152,128]{2,1,0:T(8,128)S(1)}, f32[2,152,128]{2,1,0:T(8,128)S(1)}, u32[]{:S(2)}, u32[]{:S(2)}) collective-permute-start(f32[2,152,128]{2,1,0:T(8,128)S(1)} %get-tuple-element.32.after), channel_id=1, source_target_pairs={{4,8},{12,16},{20,24},{28,32},{36,40},{44,48},{52,56},{60,64},{68,... | collective-permute-start | bytes 466952 | tf_op jit(solution)/shard_map/ppermute | solution.py:349
  5.6 0.3 collective-permute-start.2
  5.9 3.8 %collective-permute-start.1 = (f32[2,152,128]{2,1,0:T(8,128)S(1)}, f32[2,152,128]{2,1,0:T(8,128)S(1)}, u32[]{:S(2)}, u32[]{:S(2)}) collective-permute-start(f32[2,152,128]{2,1,0:T(8,128)S(1)} %get-tuple-element.32.after), channel_id=1, source_target_pairs={{1,2},{2,1},{5,6},{6,5},{9,10},{10,9},{13,14},{14,13},{17,18},{18,... | collective-permute-start | bytes 466952 | tf_op jit(solution)/shard_map/ppermute | solution.py:349
  9.7 0.1 collective-permute-start
  9.8 2.4 %second_entry.1 = (f32[512,128]{1,0:T(8,128)S(1)}, f32[2,192,128]{2,1,0:T(8,128)S(1)}, f32[27,4,4096]{2,1,0:T(4,128)S(1)}, s32[110]{0:T(128)S(4)}) custom-call(f32[2,152,128]{2,1,0:T(8,128)S(1)} %get-tuple-element.32.after, s32[1]{0:T(128)S(6)} %copy.7.live, s32[1,2]{1,0:T(1,128)} %slots.3, f32[4,8,8,512]{3,2,1,0:T(8,128)} %feat.3, f32[27,4,4096]{2,1,0:T(4,128)} %bitcast.1, ...), custom_call_target="tpu_custom_call" | custom-call | flops 600000000 | bytes 4194304 | tf_op jit(solution)/shard_map/second_entry/pallas_call | solution.py:360
  12.2 0.4 taps0.1
  12.7 0.6 %collective-permute-done.1.refs_1_ = f32[2,152,128]{2,1,0:T(8,128)S(1)} collective-permute-done((f32[2,152,128]{2,1,0:T(8,128)S(1)}, f32[2,152,128]{2,1,0:T(8,128)S(1)}, u32[]{:S(2)}, u32[]{:S(2)}) %collective-permute-start.1) | collective-permute-done | bytes 155680 | tf_op jit(solution)/shard_map/ppermute | solution.py:349
  13.3 1.5 %near0.1 = (f32[512,128]{1,0:T(8,128)S(1)}, f32[2,192,128]{2,1,0:T(8,128)S(1)}, f32[2,152,128]{2,1,0:T(8,128)S(1)}, f32[13,192,128]{2,1,0:T(8,128)S(1)}) custom-call(s32[110]{0:T(128)S(4)} %get-tuple-element.33.scalars, f32[512,128]{1,0:T(8,128)S(1)} %get-tuple-element.34.field.refs_6_, f32[2,192,128]{2,1,0:T(8,128)S(1)} %get-tuple-element.35.faces_a, ...), custom_call_target="tpu_custom_call" | custom-call | flops 600000000 | bytes 4194304 | tf_op jit(solution)/shard_map/near0/pallas_call | solution.py:360
  14.7 3.4 %collective-permute-start.7 = (f32[2,152,128]{2,1,0:T(8,128)S(1)}, f32[2,152,128]{2,1,0:T(8,128)S(1)}, u32[]{:S(2)}, u32[]{:S(2)}) collective-permute-start(f32[2,152,128]{2,1,0:T(8,128)S(1)} %get-tuple-element.44.after), channel_id=1, source_target_pairs={{4,8},{12,16},{20,24},{28,32},{36,40},{44,48},{52,56},{60,64},{68,... | collective-permute-start | bytes 466952 | tf_op jit(solution)/shard_map/ppermute | solution.py:349
  18.2 0.1 collective-permute-start.6
  18.3 3.8 %collective-permute-start.5 = (f32[2,152,128]{2,1,0:T(8,128)S(1)}, f32[2,152,128]{2,1,0:T(8,128)S(1)}, u32[]{:S(2)}, u32[]{:S(2)}) collective-permute-start(f32[2,152,128]{2,1,0:T(8,128)S(1)} %get-tuple-element.44.after), channel_id=1, source_target_pairs={{1,2},{2,1},{5,6},{6,5},{9,10},{10,9},{13,14},{14,13},{17,18},{18,... | collective-permute-start | bytes 466952 | tf_op jit(solution)/shard_map/ppermute | solution.py:349
  22.1 0.1 collective-permute-start.4
  22.2 0.4 taps1.1.refs_4_.taps
  22.6 1.3 %far0.1 = (f32[512,128]{1,0:T(8,128)S(1)}, f32[2,192,128]{2,1,0:T(8,128)S(1)}) custom-call(s32[110]{0:T(128)S(4)} %get-tuple-element.33.scalars, f32[512,128]{1,0:T(8,128)S(1)} %get-tuple-element.41.field.refs_0_, f32[13,192,128]{2,1,0:T(8,128)S(1)} %get-tuple-element.42.table, bf16[9,256,256]{2,1,0:T(8,128)(2,1)S(1)} %get-tuple-element.38.refs_4_.taps, ...), custom_call_target="tpu_custom_call" | custom-call | flops 600000000 | bytes 4194304 | tf_op jit(solution)/shard_map/far0/pallas_call | solution.py:360
  24.0 2.7 %collective-permute-done.5.refs_1_ = f32[2,152,128]{2,1,0:T(8,128)S(1)} collective-permute-done((f32[2,152,128]{2,1,0:T(8,128)S(1)}, f32[2,152,128]{2,1,0:T(8,128)S(1)}, u32[]{:S(2)}, u32[]{:S(2)}) %collective-permute-start.5) | collective-permute-done | bytes 155680 | tf_op jit(solution)/shard_map/ppermute | solution.py:349
  26.7 1.5 %near1.1 = (f32[512,128]{1,0:T(8,128)S(1)}, f32[2,192,128]{2,1,0:T(8,128)S(1)}, f32[2,152,128]{2,1,0:T(8,128)S(1)}, f32[13,192,128]{2,1,0:T(8,128)S(1)}) custom-call(s32[110]{0:T(128)S(4)} %get-tuple-element.33.scalars, f32[512,128]{1,0:T(8,128)S(1)} %get-tuple-element.39.field, f32[2,192,128]{2,1,0:T(8,128)S(1)} %get-tuple-element.40.faces_a, ...), custom_call_target="tpu_custom_call" | custom-call | flops 600000000 | bytes 4194304 | tf_op jit(solution)/shard_map/near1/pallas_call | solution.py:360
  28.2 1.9 %collective-permute-start.11 = (f32[2,152,128]{2,1,0:T(8,128)S(1)}, f32[2,152,128]{2,1,0:T(8,128)S(1)}, u32[]{:S(2)}, u32[]{:S(2)}) collective-permute-start(f32[2,152,128]{2,1,0:T(8,128)S(1)} %get-tuple-element.51.after), channel_id=1, source_target_pairs={{4,8},{12,16},{20,24},{28,32},{36,40},{44,48},{52,56},{60,64},{68,... | collective-permute-start | bytes 466952 | tf_op jit(solution)/shard_map/ppermute | solution.py:349
  30.2 3.6 %collective-permute-start.9 = (f32[2,152,128]{2,1,0:T(8,128)S(1)}, f32[2,152,128]{2,1,0:T(8,128)S(1)}, u32[]{:S(2)}, u32[]{:S(2)}) collective-permute-start(f32[2,152,128]{2,1,0:T(8,128)S(1)} %get-tuple-element.51.after), channel_id=1, source_target_pairs={{1,2},{2,1},{5,6},{6,5},{9,10},{10,9},{13,14},{14,13},{17,18},{18,... | collective-permute-start | bytes 466952 | tf_op jit(solution)/shard_map/ppermute | solution.py:349
  33.8 0.1 collective-permute-start.8
  33.9 0.4 taps2.1.refs_4_.taps
  34.2 1.3 %far1.1 = (f32[512,128]{1,0:T(8,128)S(1)}, f32[2,192,128]{2,1,0:T(8,128)S(1)}) custom-call(s32[110]{0:T(128)S(4)} %get-tuple-element.33.scalars, f32[512,128]{1,0:T(8,128)S(1)} %get-tuple-element.48.field, f32[13,192,128]{2,1,0:T(8,128)S(1)} %get-tuple-element.49.table, bf16[9,256,256]{2,1,0:T(8,128)(2,1)S(1)} %taps1.1.refs_4_.taps, f32[4,64]{1,0:T(4,128)S(1)} %copy-done, ...), custom_call_target="tpu_custom_call" | custom-call | flops 600000000 | bytes 4194304 | tf_op jit(solution)/shard_map/far1/pallas_call | solution.py:360
  35.6 2.2 %collective-permute-done.9.refs_1_ = f32[2,152,128]{2,1,0:T(8,128)S(1)} collective-permute-done((f32[2,152,128]{2,1,0:T(8,128)S(1)}, f32[2,152,128]{2,1,0:T(8,128)S(1)}, u32[]{:S(2)}, u32[]{:S(2)}) %collective-permute-start.9) | collective-permute-done | bytes 155680 | tf_op jit(solution)/shard_map/ppermute | solution.py:349
  37.8 1.5 %near2.1 = (f32[512,128]{1,0:T(8,128)S(1)}, f32[2,192,128]{2,1,0:T(8,128)S(1)}, f32[2,152,128]{2,1,0:T(8,128)S(1)}, f32[13,192,128]{2,1,0:T(8,128)S(1)}) custom-call(s32[110]{0:T(128)S(4)} %get-tuple-element.33.scalars, f32[512,128]{1,0:T(8,128)S(1)} %get-tuple-element.46.field.refs_6_, f32[2,192,128]{2,1,0:T(8,128)S(1)} %get-tuple-element.47.faces_a, ...), custom_call_target="tpu_custom_call" | custom-call | flops 600000000 | bytes 4194304 | tf_op jit(solution)/shard_map/near2/pallas_call | solution.py:360
  39.3 4.2 %collective-permute-start.15 = (f32[2,152,128]{2,1,0:T(8,128)S(1)}, f32[2,152,128]{2,1,0:T(8,128)S(1)}, u32[]{:S(2)}, u32[]{:S(2)}) collective-permute-start(f32[2,152,128]{2,1,0:T(8,128)S(1)} %get-tuple-element.58.after), channel_id=1, source_target_pairs={{4,8},{12,16},{20,24},{28,32},{36,40},{44,48},{52,56},{60,64},{68,... | collective-permute-start | bytes 466952 | tf_op jit(solution)/shard_map/ppermute | solution.py:349
  43.5 2.3 %collective-permute-start.13 = (f32[2,152,128]{2,1,0:T(8,128)S(1)}, f32[2,152,128]{2,1,0:T(8,128)S(1)}, u32[]{:S(2)}, u32[]{:S(2)}) collective-permute-start(f32[2,152,128]{2,1,0:T(8,128)S(1)} %get-tuple-element.58.after), channel_id=1, source_target_pairs={{1,2},{2,1},{5,6},{6,5},{9,10},{10,9},{13,14},{14,13},{17,18},{18,... | collective-permute-start | bytes 466952 | tf_op jit(solution)/shard_map/ppermute | solution.py:349
  45.9 0.3 collective-permute-start.12
  46.2 0.4 taps3.1.refs_4_
  46.5 1.3 %far2.1 = (f32[512,128]{1,0:T(8,128)S(1)}, f32[2,192,128]{2,1,0:T(8,128)S(1)}) custom-call(s32[110]{0:T(128)S(4)} %get-tuple-element.33.scalars, f32[512,128]{1,0:T(8,128)S(1)} %get-tuple-element.53.field.refs_7_, f32[13,192,128]{2,1,0:T(8,128)S(1)} %get-tuple-element.54.table, bf16[9,256,256]{2,1,0:T(8,128)(2,1)S(1)} %taps2.1.refs_4_.taps, f32[4,64]{1,0:T(4,128)S(1)} %copy-done), custom_call_target="tpu_custom_call" | custom-call | flops 600000000 | bytes 4194304 | tf_op jit(solution)/shard_map/far2/pallas_call | solution.py:360
  47.9 1.6 %collective-permute-done.14.refs_2_ = f32[2,152,128]{2,1,0:T(8,128)S(1)} collective-permute-done((f32[2,152,128]{2,1,0:T(8,128)S(1)}, f32[2,152,128]{2,1,0:T(8,128)S(1)}, u32[]{:S(2)}, u32[]{:S(2)}) %collective-permute-start.14) | collective-permute-done | bytes 155680 | tf_op jit(solution)/shard_map/ppermute | solution.py:349
  49.5 1.9 %collective-permute-done.13.refs_1_ = f32[2,152,128]{2,1,0:T(8,128)S(1)} collective-permute-done((f32[2,152,128]{2,1,0:T(8,128)S(1)}, f32[2,152,128]{2,1,0:T(8,128)S(1)}, u32[]{:S(2)}, u32[]{:S(2)}) %collective-permute-start.13) | collective-permute-done | bytes 155680 | tf_op jit(solution)/shard_map/ppermute | solution.py:349
  51.4 3.4 %last3.1 = f32[4,8,8,512]{3,2,1,0:T(8,128)} custom-call(s32[110]{0:T(128)S(4)} %get-tuple-element.33.scalars, f32[512,128]{1,0:T(8,128)S(1)} %get-tuple-element.52.field_a, f32[512,128]{1,0:T(8,128)S(1)} %get-tuple-element.55.field_b, f32[2,192,128]{2,1,0:T(8,128)S(1)} %get-tuple-element.56.faces_a, f32[2,192,128]{2,1,0:T(8,128)S(1)} %get-tuple-element.57.faces_b, ...), custom_call_target="tpu_custom_call" | custom-call | flops 600000000 | bytes 4194304 | tf_op jit(solution)/shard_map/last3/pallas_call | solution.py:360
  (15 shorter events, 0.2 us)
Async XLA Ops:
  1.8 10.8 %collective-permute-start.3 = (f32[2,152,128]{2,1,0:T(8,128)S(1)}, f32[2,152,128]{2,1,0:T(8,128)S(1)}, u32[]{:S(2)}, u32[]{:S(2)}) collective-permute-start(f32[2,152,128]{2,1,0:T(8,128)S(1)} %get-tuple-element.32.after), channel_id=1, source_target_pairs={{4,8},{12,16},{20,24},{28,32},{36,40},{44,48},{52,56},{60,64},{68,... | collective-permute-start | bytes 466952 | tf_op jit(solution)/shard_map/ppermute | solution.py:349
  5.6 7.1 %collective-permute-start.2 = (f32[2,152,128]{2,1,0:T(8,128)S(1)}, f32[2,152,128]{2,1,0:T(8,128)S(1)}, u32[]{:S(2)}, u32[]{:S(2)}) collective-permute-start(f32[2,152,128]{2,1,0:T(8,128)S(1)} %get-tuple-element.32.after), channel_id=1, source_target_pairs={{0,1},{2,3},{1,0},{3,2},{4,5},{6,7},{5,4},{7,6},{8,9},{10,11},{9,8... | collective-permute-start | bytes 466952 | tf_op jit(solution)/shard_map/ppermute | solution.py:349
  5.9 7.3 %collective-permute-start.1 = (f32[2,152,128]{2,1,0:T(8,128)S(1)}, f32[2,152,128]{2,1,0:T(8,128)S(1)}, u32[]{:S(2)}, u32[]{:S(2)}) collective-permute-start(f32[2,152,128]{2,1,0:T(8,128)S(1)} %get-tuple-element.32.after), channel_id=1, source_target_pairs={{1,2},{2,1},{5,6},{6,5},{9,10},{10,9},{13,14},{14,13},{17,18},{18,... | collective-permute-start | bytes 466952 | tf_op jit(solution)/shard_map/ppermute | solution.py:349
  9.7 3.6 %collective-permute-start = (f32[2,152,128]{2,1,0:T(8,128)S(1)}, f32[2,152,128]{2,1,0:T(8,128)S(1)}, u32[]{:S(2)}, u32[]{:S(2)}) collective-permute-start(f32[2,152,128]{2,1,0:T(8,128)S(1)} %get-tuple-element.32.after), channel_id=1, source_target_pairs={{0,4},{8,12},{16,20},{24,28},{32,36},{40,44},{48,52},{56,60},{64,6... | collective-permute-start | bytes 466952 | tf_op jit(solution)/shard_map/ppermute | solution.py:349
  12.2 1.1 %copy-start = (f32[4,64]{1,0:T(4,128)S(1)}, f32[4,64]{1,0:T(4,128)}, u32[]{:S(2)}) copy-start(f32[4,64]{1,0:T(4,128)} %refs_5_.7) | copy-start | bytes 3076
  14.7 9.2 %collective-permute-start.7 = (f32[2,152,128]{2,1,0:T(8,128)S(1)}, f32[2,152,128]{2,1,0:T(8,128)S(1)}, u32[]{:S(2)}, u32[]{:S(2)}) collective-permute-start(f32[2,152,128]{2,1,0:T(8,128)S(1)} %get-tuple-element.44.after), channel_id=1, source_target_pairs={{4,8},{12,16},{20,24},{28,32},{36,40},{44,48},{52,56},{60,64},{68,... | collective-permute-start | bytes 466952 | tf_op jit(solution)/shard_map/ppermute | solution.py:349
  18.2 5.8 %collective-permute-start.6 = (f32[2,152,128]{2,1,0:T(8,128)S(1)}, f32[2,152,128]{2,1,0:T(8,128)S(1)}, u32[]{:S(2)}, u32[]{:S(2)}) collective-permute-start(f32[2,152,128]{2,1,0:T(8,128)S(1)} %get-tuple-element.44.after), channel_id=1, source_target_pairs={{0,1},{2,3},{1,0},{3,2},{4,5},{6,7},{5,4},{7,6},{8,9},{10,11},{9,8... | collective-permute-start | bytes 466952 | tf_op jit(solution)/shard_map/ppermute | solution.py:349
  18.3 8.4 %collective-permute-start.5 = (f32[2,152,128]{2,1,0:T(8,128)S(1)}, f32[2,152,128]{2,1,0:T(8,128)S(1)}, u32[]{:S(2)}, u32[]{:S(2)}) collective-permute-start(f32[2,152,128]{2,1,0:T(8,128)S(1)} %get-tuple-element.44.after), channel_id=1, source_target_pairs={{1,2},{2,1},{5,6},{6,5},{9,10},{10,9},{13,14},{14,13},{17,18},{18,... | collective-permute-start | bytes 466952 | tf_op jit(solution)/shard_map/ppermute | solution.py:349
  22.1 4.6 %collective-permute-start.4 = (f32[2,152,128]{2,1,0:T(8,128)S(1)}, f32[2,152,128]{2,1,0:T(8,128)S(1)}, u32[]{:S(2)}, u32[]{:S(2)}) collective-permute-start(f32[2,152,128]{2,1,0:T(8,128)S(1)} %get-tuple-element.44.after), channel_id=1, source_target_pairs={{0,4},{8,12},{16,20},{24,28},{32,36},{40,44},{48,52},{56,60},{64,6... | collective-permute-start | bytes 466952 | tf_op jit(solution)/shard_map/ppermute | solution.py:349
  28.2 7.4 %collective-permute-start.11 = (f32[2,152,128]{2,1,0:T(8,128)S(1)}, f32[2,152,128]{2,1,0:T(8,128)S(1)}, u32[]{:S(2)}, u32[]{:S(2)}) collective-permute-start(f32[2,152,128]{2,1,0:T(8,128)S(1)} %get-tuple-element.51.after), channel_id=1, source_target_pairs={{4,8},{12,16},{20,24},{28,32},{36,40},{44,48},{52,56},{60,64},{68,... | collective-permute-start | bytes 466952 | tf_op jit(solution)/shard_map/ppermute | solution.py:349
  30.1 5.5 %collective-permute-start.10 = (f32[2,152,128]{2,1,0:T(8,128)S(1)}, f32[2,152,128]{2,1,0:T(8,128)S(1)}, u32[]{:S(2)}, u32[]{:S(2)}) collective-permute-start(f32[2,152,128]{2,1,0:T(8,128)S(1)} %get-tuple-element.51.after), channel_id=1, source_target_pairs={{0,1},{2,3},{1,0},{3,2},{4,5},{6,7},{5,4},{7,6},{8,9},{10,11},{9,8... | collective-permute-start | bytes 466952 | tf_op jit(solution)/shard_map/ppermute | solution.py:349
  30.2 7.6 %collective-permute-start.9 = (f32[2,152,128]{2,1,0:T(8,128)S(1)}, f32[2,152,128]{2,1,0:T(8,128)S(1)}, u32[]{:S(2)}, u32[]{:S(2)}) collective-permute-start(f32[2,152,128]{2,1,0:T(8,128)S(1)} %get-tuple-element.51.after), channel_id=1, source_target_pairs={{1,2},{2,1},{5,6},{6,5},{9,10},{10,9},{13,14},{14,13},{17,18},{18,... | collective-permute-start | bytes 466952 | tf_op jit(solution)/shard_map/ppermute | solution.py:349
  33.8 4.0 %collective-permute-start.8 = (f32[2,152,128]{2,1,0:T(8,128)S(1)}, f32[2,152,128]{2,1,0:T(8,128)S(1)}, u32[]{:S(2)}, u32[]{:S(2)}) collective-permute-start(f32[2,152,128]{2,1,0:T(8,128)S(1)} %get-tuple-element.51.after), channel_id=1, source_target_pairs={{0,4},{8,12},{16,20},{24,28},{32,36},{40,44},{48,52},{56,60},{64,6... | collective-permute-start | bytes 466952 | tf_op jit(solution)/shard_map/ppermute | solution.py:349
  39.3 8.6 %collective-permute-start.15 = (f32[2,152,128]{2,1,0:T(8,128)S(1)}, f32[2,152,128]{2,1,0:T(8,128)S(1)}, u32[]{:S(2)}, u32[]{:S(2)}) collective-permute-start(f32[2,152,128]{2,1,0:T(8,128)S(1)} %get-tuple-element.58.after), channel_id=1, source_target_pairs={{4,8},{12,16},{20,24},{28,32},{36,40},{44,48},{52,56},{60,64},{68,... | collective-permute-start | bytes 466952 | tf_op jit(solution)/shard_map/ppermute | solution.py:349
  43.4 6.1 %collective-permute-start.14 = (f32[2,152,128]{2,1,0:T(8,128)S(1)}, f32[2,152,128]{2,1,0:T(8,128)S(1)}, u32[]{:S(2)}, u32[]{:S(2)}) collective-permute-start(f32[2,152,128]{2,1,0:T(8,128)S(1)} %get-tuple-element.58.after), channel_id=1, source_target_pairs={{0,1},{2,3},{1,0},{3,2},{4,5},{6,7},{5,4},{7,6},{8,9},{10,11},{9,8... | collective-permute-start | bytes 466952 | tf_op jit(solution)/shard_map/ppermute | solution.py:349
  43.5 7.8 %collective-permute-start.13 = (f32[2,152,128]{2,1,0:T(8,128)S(1)}, f32[2,152,128]{2,1,0:T(8,128)S(1)}, u32[]{:S(2)}, u32[]{:S(2)}) collective-permute-start(f32[2,152,128]{2,1,0:T(8,128)S(1)} %get-tuple-element.58.after), channel_id=1, source_target_pairs={{1,2},{2,1},{5,6},{6,5},{9,10},{10,9},{13,14},{14,13},{17,18},{18,... | collective-permute-start | bytes 466952 | tf_op jit(solution)/shard_map/ppermute | solution.py:349
  45.9 5.5 %collective-permute-start.12 = (f32[2,152,128]{2,1,0:T(8,128)S(1)}, f32[2,152,128]{2,1,0:T(8,128)S(1)}, u32[]{:S(2)}, u32[]{:S(2)}) collective-permute-start(f32[2,152,128]{2,1,0:T(8,128)S(1)} %get-tuple-element.58.after), channel_id=1, source_target_pairs={{0,4},{8,12},{16,20},{24,28},{32,36},{40,44},{48,52},{56,60},{64,6... | collective-permute-start | bytes 466952 | tf_op jit(solution)/shard_map/ppermute | solution.py:349

commit v4 on v3

--- a/solution.py
+++ b/solution.py
@@ -120,11 +120,15 @@
     look.wait()
     places = places_of(picked[0, 0], picked[0, 1])
     turns = [jnp.where(lax.axis_index(axis) % 2 == 0, 2, 0) for axis in ("space", "slab")]
+    ends = [(lax.axis_index(axis), lax.axis_size(axis) - 1) for axis in ("space", "slab")]
 
     def rename(at, carry):
         for b in range(BRICK):
             t = nbr[b, at]
             new = jnp.where(t < 8, t ^ turns[0], jnp.where(t < 12, t ^ turns[1], t))
+            for k, (place, end) in enumerate(ends):
+                side = (t - 4 - 4 * k) // 2
+                new = jnp.where(((side == 0) & (place == 0)) | ((side == 1) & (place == end)), 12, new)
             for k in range(BRICK):
                 new = jnp.where(t == places[k], k, new)
             scalars[26 * b + at] = new
@@ -338,7 +342,7 @@
 
 
 def swaps(size, first):
-    pairs = [(i, i + 1) for i in range(first, size - 1, 2)]
+    pairs = [(i, (i + 1) % size) for i in range(first, size, 2)]
     return pairs + [(b, a) for a, b in pairs]
 
 

time: 55.3 us -> 49.8 us (0.901)
  the two profiles are of different devices: /device:TPU:75 before, /device:TPU:0 now
where the time goes in v4:
time: 49.8 us; the launch traced here: 49.6 us
  starting transfers between devices  21.9 us (44%)
  Pallas kernels  18.3 us (37%)
  waiting for transfers between devices  8.29 us (17%)
  between operations  0.94 us (2%)
    ppermute x16, starting transfers between devices, exchange(): got += [lax.ppermute(send, axis, swaps(size, first)) for first in (0, 1)]  21.9 us
    pallas_call x13, Pallas kernels, call(): pl.pallas_call(kernel, out_shape=out_shape, in_specs=in_specs, out_specs=...  18.3 us
    ppermute x16, waiting for transfers between devices, exchange(): got += [lax.ppermute(send, axis, swaps(size, first)) for first in (0, 1)]  8.29 us
  transfers between devices with their start and end apart: 16, of which 6 were waited for; matrix products, arithmetic and copies ran while one was open for 0% of the time, Pallas kernels for 19%

profile of v4, /device:TPU:0, one launch (start us, length us, event | category | flops | bytes accessed | tf_op | source)
XLA Modules:
  0.0 49.6 jit_solution(15604432635770847562)
XLA Ops:
  0.7 1.2 %entry.1 = (f32[512,128]{1,0:T(8,128)S(1)}, f32[2,192,128]{2,1,0:T(8,128)S(1)}, f32[2,152,128]{2,1,0:T(8,128)S(1)}) custom-call(s32[1]{0:T(128)S(6)} %copy.7.live, s32[1,2]{1,0:T(1,128)} %slots.3, f32[4,8,8,512]{3,2,1,0:T(8,128)} %feat.3), custom_call_target="tpu_custom_call" | custom-call | flops 600000000 | bytes 4194304 | tf_op jit(solution)/shard_map/entry/pallas_call | solution.py:364
  1.8 6.1 %collective-permute-start.3 = (f32[2,152,128]{2,1,0:T(8,128)S(1)}, f32[2,152,128]{2,1,0:T(8,128)S(1)}, u32[]{:S(2)}, u32[]{:S(2)}) collective-permute-start(f32[2,152,128]{2,1,0:T(8,128)S(1)} %get-tuple-element.32.after), channel_id=1, source_target_pairs={{4,8},{12,16},{20,24},{28,32},{36,40},{44,48},{52,56},{60,64},{68,... | collective-permute-start | bytes 466952 | tf_op jit(solution)/shard_map/ppermute | solution.py:353
  7.9 1.5 %collective-permute-start.2 = (f32[2,152,128]{2,1,0:T(8,128)S(1)}, f32[2,152,128]{2,1,0:T(8,128)S(1)}, u32[]{:S(2)}, u32[]{:S(2)}) collective-permute-start(f32[2,152,128]{2,1,0:T(8,128)S(1)} %get-tuple-element.32.after), channel_id=1, source_target_pairs={{0,1},{2,3},{1,0},{3,2},{4,5},{6,7},{5,4},{7,6},{8,9},{10,11},{9,8... | collective-permute-start | bytes 466952 | tf_op jit(solution)/shard_map/ppermute | solution.py:353
  9.4 2.1 %collective-permute-start.1 = (f32[2,152,128]{2,1,0:T(8,128)S(1)}, f32[2,152,128]{2,1,0:T(8,128)S(1)}, u32[]{:S(2)}, u32[]{:S(2)}) collective-permute-start(f32[2,152,128]{2,1,0:T(8,128)S(1)} %get-tuple-element.32.after), channel_id=1, source_target_pairs={{1,2},{3,0},{2,1},{0,3},{5,6},{7,4},{6,5},{4,7},{9,10},{11,8},{10,... | collective-permute-start | bytes 466952 | tf_op jit(solution)/shard_map/ppermute | solution.py:353
  11.5 3.9 %second_entry.1 = (f32[512,128]{1,0:T(8,128)S(1)}, f32[2,192,128]{2,1,0:T(8,128)S(1)}, f32[27,4,4096]{2,1,0:T(4,128)S(1)}, s32[110]{0:T(128)S(4)}) custom-call(f32[2,152,128]{2,1,0:T(8,128)S(1)} %get-tuple-element.32.after, s32[1]{0:T(128)S(6)} %copy.7.live, s32[1,2]{1,0:T(1,128)} %slots.3, f32[4,8,8,512]{3,2,1,0:T(8,128)} %feat.3, f32[27,4,4096]{2,1,0:T(4,128)} %bitcast.1, ...), custom_call_target="tpu_custom_call" | custom-call | flops 600000000 | bytes 4194304 | tf_op jit(solution)/shard_map/second_entry/pallas_call | solution.py:364
  15.4 0.4 taps0.1
  15.9 0.2 copy-done
  16.1 1.5 %near0.1 = (f32[512,128]{1,0:T(8,128)S(1)}, f32[2,192,128]{2,1,0:T(8,128)S(1)}, f32[2,152,128]{2,1,0:T(8,128)S(1)}, f32[13,192,128]{2,1,0:T(8,128)S(1)}) custom-call(s32[110]{0:T(128)S(4)} %get-tuple-element.33.scalars, f32[512,128]{1,0:T(8,128)S(1)} %get-tuple-element.34.field.refs_6_, f32[2,192,128]{2,1,0:T(8,128)S(1)} %get-tuple-element.35.faces_a, ...), custom_call_target="tpu_custom_call" | custom-call | flops 600000000 | bytes 4194304 | tf_op jit(solution)/shard_map/near0/pallas_call | solution.py:364
  17.5 0.9 %collective-permute-start.7 = (f32[2,152,128]{2,1,0:T(8,128)S(1)}, f32[2,152,128]{2,1,0:T(8,128)S(1)}, u32[]{:S(2)}, u32[]{:S(2)}) collective-permute-start(f32[2,152,128]{2,1,0:T(8,128)S(1)} %get-tuple-element.44.after), channel_id=1, source_target_pairs={{4,8},{12,16},{20,24},{28,32},{36,40},{44,48},{52,56},{60,64},{68,... | collective-permute-start | bytes 466952 | tf_op jit(solution)/shard_map/ppermute | solution.py:353
  18.5 0.6 %collective-permute-start.6 = (f32[2,152,128]{2,1,0:T(8,128)S(1)}, f32[2,152,128]{2,1,0:T(8,128)S(1)}, u32[]{:S(2)}, u32[]{:S(2)}) collective-permute-start(f32[2,152,128]{2,1,0:T(8,128)S(1)} %get-tuple-element.44.after), channel_id=1, source_target_pairs={{0,1},{2,3},{1,0},{3,2},{4,5},{6,7},{5,4},{7,6},{8,9},{10,11},{9,8... | collective-permute-start | bytes 466952 | tf_op jit(solution)/shard_map/ppermute | solution.py:353
  19.1 2.0 %collective-permute-start.5 = (f32[2,152,128]{2,1,0:T(8,128)S(1)}, f32[2,152,128]{2,1,0:T(8,128)S(1)}, u32[]{:S(2)}, u32[]{:S(2)}) collective-permute-start(f32[2,152,128]{2,1,0:T(8,128)S(1)} %get-tuple-element.44.after), channel_id=1, source_target_pairs={{1,2},{3,0},{2,1},{0,3},{5,6},{7,4},{6,5},{4,7},{9,10},{11,8},{10,... | collective-permute-start | bytes 466952 | tf_op jit(solution)/shard_map/ppermute | solution.py:353
  21.1 0.4 taps1.1.refs_4_.taps
  21.4 1.3 %far0.1 = (f32[512,128]{1,0:T(8,128)S(1)}, f32[2,192,128]{2,1,0:T(8,128)S(1)}) custom-call(s32[110]{0:T(128)S(4)} %get-tuple-element.33.scalars, f32[512,128]{1,0:T(8,128)S(1)} %get-tuple-element.41.field.refs_0_, f32[13,192,128]{2,1,0:T(8,128)S(1)} %get-tuple-element.42.table, bf16[9,256,256]{2,1,0:T(8,128)(2,1)S(1)} %get-tuple-element.38.refs_4_.taps, ...), custom_call_target="tpu_custom_call" | custom-call | flops 600000000 | bytes 4194304 | tf_op jit(solution)/shard_map/far0/pallas_call | solution.py:364
  22.8 2.8 %collective-permute-done.7.refs_3_ = f32[2,152,128]{2,1,0:T(8,128)S(1)} collective-permute-done((f32[2,152,128]{2,1,0:T(8,128)S(1)}, f32[2,152,128]{2,1,0:T(8,128)S(1)}, u32[]{:S(2)}, u32[]{:S(2)}) %collective-permute-start.7) | collective-permute-done | bytes 155680 | tf_op jit(solution)/shard_map/ppermute | solution.py:353
  25.6 0.1 collective-permute-done.5.refs_1_
  25.7 1.5 %near1.1 = (f32[512,128]{1,0:T(8,128)S(1)}, f32[2,192,128]{2,1,0:T(8,128)S(1)}, f32[2,152,128]{2,1,0:T(8,128)S(1)}, f32[13,192,128]{2,1,0:T(8,128)S(1)}) custom-call(s32[110]{0:T(128)S(4)} %get-tuple-element.33.scalars, f32[512,128]{1,0:T(8,128)S(1)} %get-tuple-element.39.field, f32[2,192,128]{2,1,0:T(8,128)S(1)} %get-tuple-element.40.faces_a, ...), custom_call_target="tpu_custom_call" | custom-call | flops 600000000 | bytes 4194304 | tf_op jit(solution)/shard_map/near1/pallas_call | solution.py:364
  27.1 2.7 %collective-permute-start.11 = (f32[2,152,128]{2,1,0:T(8,128)S(1)}, f32[2,152,128]{2,1,0:T(8,128)S(1)}, u32[]{:S(2)}, u32[]{:S(2)}) collective-permute-start(f32[2,152,128]{2,1,0:T(8,128)S(1)} %get-tuple-element.51.after), channel_id=1, source_target_pairs={{4,8},{12,16},{20,24},{28,32},{36,40},{44,48},{52,56},{60,64},{68,... | collective-permute-start | bytes 466952 | tf_op jit(solution)/shard_map/ppermute | solution.py:353
  29.8 0.2 collective-permute-start.10
  30.1 2.1 %collective-permute-start.9 = (f32[2,152,128]{2,1,0:T(8,128)S(1)}, f32[2,152,128]{2,1,0:T(8,128)S(1)}, u32[]{:S(2)}, u32[]{:S(2)}) collective-permute-start(f32[2,152,128]{2,1,0:T(8,128)S(1)} %get-tuple-element.51.after), channel_id=1, source_target_pairs={{1,2},{3,0},{2,1},{0,3},{5,6},{7,4},{6,5},{4,7},{9,10},{11,8},{10,... | collective-permute-start | bytes 466952 | tf_op jit(solution)/shard_map/ppermute | solution.py:353
  32.1 0.4 taps2.1.refs_4_.taps
  32.5 1.3 %far1.1 = (f32[512,128]{1,0:T(8,128)S(1)}, f32[2,192,128]{2,1,0:T(8,128)S(1)}) custom-call(s32[110]{0:T(128)S(4)} %get-tuple-element.33.scalars, f32[512,128]{1,0:T(8,128)S(1)} %get-tuple-element.48.field, f32[13,192,128]{2,1,0:T(8,128)S(1)} %get-tuple-element.49.table, bf16[9,256,256]{2,1,0:T(8,128)(2,1)S(1)} %taps1.1.refs_4_.taps, f32[4,64]{1,0:T(4,128)S(1)} %copy-done, ...), custom_call_target="tpu_custom_call" | custom-call | flops 600000000 | bytes 4194304 | tf_op jit(solution)/shard_map/far1/pallas_call | solution.py:364
  33.8 1.3 %collective-permute-done.11.refs_3_ = f32[2,152,128]{2,1,0:T(8,128)S(1)} collective-permute-done((f32[2,152,128]{2,1,0:T(8,128)S(1)}, f32[2,152,128]{2,1,0:T(8,128)S(1)}, u32[]{:S(2)}, u32[]{:S(2)}) %collective-permute-start.11) | collective-permute-done | bytes 155680 | tf_op jit(solution)/shard_map/ppermute | solution.py:353
  35.2 1.3 %collective-permute-done.9.refs_1_ = f32[2,152,128]{2,1,0:T(8,128)S(1)} collective-permute-done((f32[2,152,128]{2,1,0:T(8,128)S(1)}, f32[2,152,128]{2,1,0:T(8,128)S(1)}, u32[]{:S(2)}, u32[]{:S(2)}) %collective-permute-start.9) | collective-permute-done | bytes 155680 | tf_op jit(solution)/shard_map/ppermute | solution.py:353
  36.5 1.5 %near2.1 = (f32[512,128]{1,0:T(8,128)S(1)}, f32[2,192,128]{2,1,0:T(8,128)S(1)}, f32[2,152,128]{2,1,0:T(8,128)S(1)}, f32[13,192,128]{2,1,0:T(8,128)S(1)}) custom-call(s32[110]{0:T(128)S(4)} %get-tuple-element.33.scalars, f32[512,128]{1,0:T(8,128)S(1)} %get-tuple-element.46.field.refs_6_, f32[2,192,128]{2,1,0:T(8,128)S(1)} %get-tuple-element.47.faces_a, ...), custom_call_target="tpu_custom_call" | custom-call | flops 600000000 | bytes 4194304 | tf_op jit(solution)/shard_map/near2/pallas_call | solution.py:364
  38.0 1.4 %collective-permute-start.15 = (f32[2,152,128]{2,1,0:T(8,128)S(1)}, f32[2,152,128]{2,1,0:T(8,128)S(1)}, u32[]{:S(2)}, u32[]{:S(2)}) collective-permute-start(f32[2,152,128]{2,1,0:T(8,128)S(1)} %get-tuple-element.58.after), channel_id=1, source_target_pairs={{4,8},{12,16},{20,24},{28,32},{36,40},{44,48},{52,56},{60,64},{68,... | collective-permute-start | bytes 466952 | tf_op jit(solution)/shard_map/ppermute | solution.py:353
  39.4 0.3 collective-permute-start.14
  39.7 2.0 %collective-permute-start.13 = (f32[2,152,128]{2,1,0:T(8,128)S(1)}, f32[2,152,128]{2,1,0:T(8,128)S(1)}, u32[]{:S(2)}, u32[]{:S(2)}) collective-permute-start(f32[2,152,128]{2,1,0:T(8,128)S(1)} %get-tuple-element.58.after), channel_id=1, source_target_pairs={{1,2},{3,0},{2,1},{0,3},{5,6},{7,4},{6,5},{4,7},{9,10},{11,8},{10,... | collective-permute-start | bytes 466952 | tf_op jit(solution)/shard_map/ppermute | solution.py:353
  41.7 0.4 taps3.1.refs_4_
  42.0 1.3 %far2.1 = (f32[512,128]{1,0:T(8,128)S(1)}, f32[2,192,128]{2,1,0:T(8,128)S(1)}) custom-call(s32[110]{0:T(128)S(4)} %get-tuple-element.33.scalars, f32[512,128]{1,0:T(8,128)S(1)} %get-tuple-element.53.field.refs_7_, f32[13,192,128]{2,1,0:T(8,128)S(1)} %get-tuple-element.54.table, bf16[9,256,256]{2,1,0:T(8,128)(2,1)S(1)} %taps2.1.refs_4_.taps, f32[4,64]{1,0:T(4,128)S(1)} %copy-done), custom_call_target="tpu_custom_call" | custom-call | flops 600000000 | bytes 4194304 | tf_op jit(solution)/shard_map/far2/pallas_call | solution.py:364
  43.4 2.6 %collective-permute-done.15.refs_3_ = f32[2,152,128]{2,1,0:T(8,128)S(1)} collective-permute-done((f32[2,152,128]{2,1,0:T(8,128)S(1)}, f32[2,152,128]{2,1,0:T(8,128)S(1)}, u32[]{:S(2)}, u32[]{:S(2)}) %collective-permute-start.15) | collective-permute-done | bytes 155680 | tf_op jit(solution)/shard_map/ppermute | solution.py:353
  46.0 0.1 collective-permute-done.13.refs_1_
  46.1 3.4 %last3.1 = f32[4,8,8,512]{3,2,1,0:T(8,128)} custom-call(s32[110]{0:T(128)S(4)} %get-tuple-element.33.scalars, f32[512,128]{1,0:T(8,128)S(1)} %get-tuple-element.52.field_a, f32[512,128]{1,0:T(8,128)S(1)} %get-tuple-element.55.field_b, f32[2,192,128]{2,1,0:T(8,128)S(1)} %get-tuple-element.56.faces_a, f32[2,192,128]{2,1,0:T(8,128)S(1)} %get-tuple-element.57.faces_b, ...), custom_call_target="tpu_custom_call" | custom-call | flops 600000000 | bytes 4194304 | tf_op jit(solution)/shard_map/last3/pallas_call | solution.py:364
  (15 shorter events, 0.0 us)
Async XLA Ops:
  1.8 14.0 %collective-permute-start.3 = (f32[2,152,128]{2,1,0:T(8,128)S(1)}, f32[2,152,128]{2,1,0:T(8,128)S(1)}, u32[]{:S(2)}, u32[]{:S(2)}) collective-permute-start(f32[2,152,128]{2,1,0:T(8,128)S(1)} %get-tuple-element.32.after), channel_id=1, source_target_pairs={{4,8},{12,16},{20,24},{28,32},{36,40},{44,48},{52,56},{60,64},{68,... | collective-permute-start | bytes 466952 | tf_op jit(solution)/shard_map/ppermute | solution.py:353
  7.9 7.9 %collective-permute-start.2 = (f32[2,152,128]{2,1,0:T(8,128)S(1)}, f32[2,152,128]{2,1,0:T(8,128)S(1)}, u32[]{:S(2)}, u32[]{:S(2)}) collective-permute-start(f32[2,152,128]{2,1,0:T(8,128)S(1)} %get-tuple-element.32.after), channel_id=1, source_target_pairs={{0,1},{2,3},{1,0},{3,2},{4,5},{6,7},{5,4},{7,6},{8,9},{10,11},{9,8... | collective-permute-start | bytes 466952 | tf_op jit(solution)/shard_map/ppermute | solution.py:353
  9.4 6.4 %collective-permute-start.1 = (f32[2,152,128]{2,1,0:T(8,128)S(1)}, f32[2,152,128]{2,1,0:T(8,128)S(1)}, u32[]{:S(2)}, u32[]{:S(2)}) collective-permute-start(f32[2,152,128]{2,1,0:T(8,128)S(1)} %get-tuple-element.32.after), channel_id=1, source_target_pairs={{1,2},{3,0},{2,1},{0,3},{5,6},{7,4},{6,5},{4,7},{9,10},{11,8},{10,... | collective-permute-start | bytes 466952 | tf_op jit(solution)/shard_map/ppermute | solution.py:353
  11.5 4.4 %collective-permute-start = (f32[2,152,128]{2,1,0:T(8,128)S(1)}, f32[2,152,128]{2,1,0:T(8,128)S(1)}, u32[]{:S(2)}, u32[]{:S(2)}) collective-permute-start(f32[2,152,128]{2,1,0:T(8,128)S(1)} %get-tuple-element.32.after), channel_id=1, source_target_pairs={{0,4},{8,12},{16,20},{24,28},{32,36},{40,44},{48,52},{56,60},{64,6... | collective-permute-start | bytes 466952 | tf_op jit(solution)/shard_map/ppermute | solution.py:353
  15.4 0.7 %copy-start = (f32[4,64]{1,0:T(4,128)S(1)}, f32[4,64]{1,0:T(4,128)}, u32[]{:S(2)}) copy-start(f32[4,64]{1,0:T(4,128)} %refs_5_.7) | copy-start | bytes 3076
  17.5 8.1 %collective-permute-start.7 = (f32[2,152,128]{2,1,0:T(8,128)S(1)}, f32[2,152,128]{2,1,0:T(8,128)S(1)}, u32[]{:S(2)}, u32[]{:S(2)}) collective-permute-start(f32[2,152,128]{2,1,0:T(8,128)S(1)} %get-tuple-element.44.after), channel_id=1, source_target_pairs={{4,8},{12,16},{20,24},{28,32},{36,40},{44,48},{52,56},{60,64},{68,... | collective-permute-start | bytes 466952 | tf_op jit(solution)/shard_map/ppermute | solution.py:353
  18.5 7.1 %collective-permute-start.6 = (f32[2,152,128]{2,1,0:T(8,128)S(1)}, f32[2,152,128]{2,1,0:T(8,128)S(1)}, u32[]{:S(2)}, u32[]{:S(2)}) collective-permute-start(f32[2,152,128]{2,1,0:T(8,128)S(1)} %get-tuple-element.44.after), channel_id=1, source_target_pairs={{0,1},{2,3},{1,0},{3,2},{4,5},{6,7},{5,4},{7,6},{8,9},{10,11},{9,8... | collective-permute-start | bytes 466952 | tf_op jit(solution)/shard_map/ppermute | solution.py:353
  19.1 6.6 %collective-permute-start.5 = (f32[2,152,128]{2,1,0:T(8,128)S(1)}, f32[2,152,128]{2,1,0:T(8,128)S(1)}, u32[]{:S(2)}, u32[]{:S(2)}) collective-permute-start(f32[2,152,128]{2,1,0:T(8,128)S(1)} %get-tuple-element.44.after), channel_id=1, source_target_pairs={{1,2},{3,0},{2,1},{0,3},{5,6},{7,4},{6,5},{4,7},{9,10},{11,8},{10,... | collective-permute-start | bytes 466952 | tf_op jit(solution)/shard_map/ppermute | solution.py:353
  21.1 4.6 %collective-permute-start.4 = (f32[2,152,128]{2,1,0:T(8,128)S(1)}, f32[2,152,128]{2,1,0:T(8,128)S(1)}, u32[]{:S(2)}, u32[]{:S(2)}) collective-permute-start(f32[2,152,128]{2,1,0:T(8,128)S(1)} %get-tuple-element.44.after), channel_id=1, source_target_pairs={{0,4},{8,12},{16,20},{24,28},{32,36},{40,44},{48,52},{56,60},{64,6... | collective-permute-start | bytes 466952 | tf_op jit(solution)/shard_map/ppermute | solution.py:353
  27.1 8.1 %collective-permute-start.11 = (f32[2,152,128]{2,1,0:T(8,128)S(1)}, f32[2,152,128]{2,1,0:T(8,128)S(1)}, u32[]{:S(2)}, u32[]{:S(2)}) collective-permute-start(f32[2,152,128]{2,1,0:T(8,128)S(1)} %get-tuple-element.51.after), channel_id=1, source_target_pairs={{4,8},{12,16},{20,24},{28,32},{36,40},{44,48},{52,56},{60,64},{68,... | collective-permute-start | bytes 466952 | tf_op jit(solution)/shard_map/ppermute | solution.py:353
  29.8 5.4 %collective-permute-start.10 = (f32[2,152,128]{2,1,0:T(8,128)S(1)}, f32[2,152,128]{2,1,0:T(8,128)S(1)}, u32[]{:S(2)}, u32[]{:S(2)}) collective-permute-start(f32[2,152,128]{2,1,0:T(8,128)S(1)} %get-tuple-element.51.after), channel_id=1, source_target_pairs={{0,1},{2,3},{1,0},{3,2},{4,5},{6,7},{5,4},{7,6},{8,9},{10,11},{9,8... | collective-permute-start | bytes 466952 | tf_op jit(solution)/shard_map/ppermute | solution.py:353
  30.1 6.4 %collective-permute-start.9 = (f32[2,152,128]{2,1,0:T(8,128)S(1)}, f32[2,152,128]{2,1,0:T(8,128)S(1)}, u32[]{:S(2)}, u32[]{:S(2)}) collective-permute-start(f32[2,152,128]{2,1,0:T(8,128)S(1)} %get-tuple-element.51.after), channel_id=1, source_target_pairs={{1,2},{3,0},{2,1},{0,3},{5,6},{7,4},{6,5},{4,7},{9,10},{11,8},{10,... | collective-permute-start | bytes 466952 | tf_op jit(solution)/shard_map/ppermute | solution.py:353
  32.1 4.4 %collective-permute-start.8 = (f32[2,152,128]{2,1,0:T(8,128)S(1)}, f32[2,152,128]{2,1,0:T(8,128)S(1)}, u32[]{:S(2)}, u32[]{:S(2)}) collective-permute-start(f32[2,152,128]{2,1,0:T(8,128)S(1)} %get-tuple-element.51.after), channel_id=1, source_target_pairs={{0,4},{8,12},{16,20},{24,28},{32,36},{40,44},{48,52},{56,60},{64,6... | collective-permute-start | bytes 466952 | tf_op jit(solution)/shard_map/ppermute | solution.py:353
  38.0 8.1 %collective-permute-start.15 = (f32[2,152,128]{2,1,0:T(8,128)S(1)}, f32[2,152,128]{2,1,0:T(8,128)S(1)}, u32[]{:S(2)}, u32[]{:S(2)}) collective-permute-start(f32[2,152,128]{2,1,0:T(8,128)S(1)} %get-tuple-element.58.after), channel_id=1, source_target_pairs={{4,8},{12,16},{20,24},{28,32},{36,40},{44,48},{52,56},{60,64},{68,... | collective-permute-start | bytes 466952 | tf_op jit(solution)/shard_map/ppermute | solution.py:353
  39.4 6.7 %collective-permute-start.14 = (f32[2,152,128]{2,1,0:T(8,128)S(1)}, f32[2,152,128]{2,1,0:T(8,128)S(1)}, u32[]{:S(2)}, u32[]{:S(2)}) collective-permute-start(f32[2,152,128]{2,1,0:T(8,128)S(1)} %get-tuple-element.58.after), channel_id=1, source_target_pairs={{0,1},{2,3},{1,0},{3,2},{4,5},{6,7},{5,4},{7,6},{8,9},{10,11},{9,8... | collective-permute-start | bytes 466952 | tf_op jit(solution)/shard_map/ppermute | solution.py:353
  39.7 6.4 %collective-permute-start.13 = (f32[2,152,128]{2,1,0:T(8,128)S(1)}, f32[2,152,128]{2,1,0:T(8,128)S(1)}, u32[]{:S(2)}, u32[]{:S(2)}) collective-permute-start(f32[2,152,128]{2,1,0:T(8,128)S(1)} %get-tuple-element.58.after), channel_id=1, source_target_pairs={{1,2},{3,0},{2,1},{0,3},{5,6},{7,4},{6,5},{4,7},{9,10},{11,8},{10,... | collective-permute-start | bytes 466952 | tf_op jit(solution)/shard_map/ppermute | solution.py:353
  41.7 4.4 %collective-permute-start.12 = (f32[2,152,128]{2,1,0:T(8,128)S(1)}, f32[2,152,128]{2,1,0:T(8,128)S(1)}, u32[]{:S(2)}, u32[]{:S(2)}) collective-permute-start(f32[2,152,128]{2,1,0:T(8,128)S(1)} %get-tuple-element.58.after), channel_id=1, source_target_pairs={{0,4},{8,12},{16,20},{24,28},{32,36},{40,44},{48,52},{56,60},{64,6... | collective-permute-start | bytes 466952 | tf_op jit(solution)/shard_map/ppermute | solution.py:353

commit v5 on v3

--- a/solution.py
+++ b/solution.py
@@ -16,7 +16,7 @@
 HB = pl.BlockSpec(memory_space=pltpu.HBM)
 F32, BF16 = jnp.float32, jnp.bfloat16
 ORDER = [0, 3, 2, 1]
-PLACE, SECOND, LIVE = 104, 108, 109
+PLACE, SECOND, LIVE = 0, 4, 5
 
 
 def direction(dx, dy, dz):
@@ -110,32 +110,36 @@
 
 
 def second_entry_kernel(
-    after, live, slots, feat, weights, neighbours, field, faces, held, scalars, own, picked, sems, nbr, far
+    after, live, slots, feat, weights, neighbours, field, faces, held, names, scalars, own, picked, sems, nbr, named, far
 ):
+    look = pltpu.make_async_copy(neighbours, nbr, far.at[1])
     fetch = pltpu.make_async_copy(weights, held, far.at[0])
-    look = pltpu.make_async_copy(neighbours, nbr, far.at[1])
+    look.start()
     fetch.start()
-    look.start()
     enter(1, live, slots, feat, field, faces, own, picked, sems)
+    places = places_of(picked[0, 0], picked[0, 1])
     look.wait()
-    places = places_of(picked[0, 0], picked[0, 1])
-    turns = [jnp.where(lax.axis_index(axis) % 2 == 0, 2, 0) for axis in ("space", "slab")]
-
-    def rename(at, carry):
-        for b in range(BRICK):
-            t = nbr[b, at]
-            new = jnp.where(t < 8, t ^ turns[0], jnp.where(t < 12, t ^ turns[1], t))
-            for k in range(BRICK):
-                new = jnp.where(t == places[k], k, new)
-            scalars[26 * b + at] = new
-        return carry
-
-    lax.fori_loop(0, 26, rename, 0)
+    t = nbr[...]
+    new = t
+    for k in range(BRICK):
+        new = jnp.where(t == places[k], k, new)
+    for k, axis in enumerate(("space", "slab")):
+        place = lax.axis_index(axis)
+        turn = jnp.where(place % 2 == 0, 2, 0)
+        low = jnp.where(place == 0, 12, 4 + 4 * k + turn)
+        high = jnp.where(place == lax.axis_size(axis) - 1, 12, 6 + 4 * k - turn)
+        for e in range(2):
+            new = jnp.where(t == 4 + 4 * k + e, jnp.minimum(low + e, 12), new)
+            new = jnp.where(t == 6 + 4 * k + e, jnp.minimum(high + e, 12), new)
+    named[:, 0:26] = new
+    hand = pltpu.make_async_copy(named, names, far.at[2])
+    hand.start()
     for k in range(BRICK):
         scalars[PLACE + k] = places[k]
     scalars[SECOND] = jnp.where(picked[0, 0] == picked[0, 1], 0, 1)
     scalars[LIVE] = live[0]
     fetch.wait()
+    hand.wait()
 
 
 def make_taps(index, plain, taps, wide):
@@ -177,28 +181,28 @@
     table[12] = jnp.zeros((FACE, 128), F32)
 
 
-def fill_margins(pair, scalars, field, table, one, two):
+def fill_margins(pair, names, scalars, field, table, one, two):
     for x in range(8):
         one[(x + 1) * 80 + 8 : (x + 1) * 80 + 72, :] = field[x * 64 : x * 64 + 64, :]
     for b in range(2):
-        near = 26 * scalars[PLACE + 2 * pair + b]
+        near = scalars[PLACE + 2 * pair + b]
 
         def cell(xp, yp):
             return (xp * 10 + yp) * 8 + 4 * b
 
         for d in (-1, 1):
             s, p = (1, 0) if d < 0 else (0, 9)
-            t = scalars[near + direction(d, 0, 0)]
+            t = names[near, direction(d, 0, 0)]
             for i in range(8):
                 at = cell(p, i + 1)
                 one[at : at + 4, :] = table[t, 32 * s + 4 * i : 32 * s + 4 * i + 4, :]
-            t = scalars[near + direction(0, d, 0)]
+            t = names[near, direction(0, d, 0)]
             for i in range(8):
                 at = cell(i + 1, p)
                 one[at : at + 4, :] = table[t, 64 + 32 * s + 4 * i : 64 + 32 * s + 4 * i + 4, :]
             for e in (-1, 1):
                 y, py = (7, 0) if e < 0 else (0, 9)
-                t = scalars[near + direction(d, e, 0)]
+                t = names[near, direction(d, e, 0)]
                 at = cell(p, py)
                 one[at : at + 4, :] = table[t, 32 * s + 4 * y : 32 * s + 4 * y + 4, :]
     low3 = lower_half((10, 8, 128))
@@ -209,7 +213,7 @@
     low = lower_half((8, 128))
     low1 = lower_half((1, 128))
     for b in range(2):
-        near = 26 * scalars[PLACE + 2 * pair + b]
+        near = scalars[PLACE + 2 * pair + b]
         for dz in (-1, 1):
             def merge(start, stride, new):
                 at = pl.ds(start, 8, stride=stride)
@@ -217,18 +221,18 @@
                 two[at, :] = jnp.where(low, new, old) if dz > 0 else jnp.where(low, old, new)
 
             row = 4 * b + (3 if dz > 0 else 0)
-            t = scalars[near + direction(0, 0, dz)]
+            t = names[near, direction(0, 0, dz)]
             for x in range(8):
                 merge(((x + 1) * 10 + 1) * 8 + row, 8, table[t, 128 + 8 * x : 136 + 8 * x, :])
             for d in (-1, 1):
                 x, p = (7, 0) if d < 0 else (0, 9)
-                t = scalars[near + direction(d, 0, dz)]
+                t = names[near, direction(d, 0, dz)]
                 merge((p * 10 + 1) * 8 + row, 8, table[t, 128 + 8 * x : 136 + 8 * x, :])
-                t = scalars[near + direction(0, d, dz)]
+                t = names[near, direction(0, d, dz)]
                 merge((10 + p) * 8 + row, 80, table[t, pl.ds(128 + x, 8, stride=8), :])
                 for e in (-1, 1):
                     y, py = (7, 0) if e < 0 else (0, 9)
-                    t = scalars[near + direction(d, e, dz)]
+                    t = names[near, direction(d, e, dz)]
                     at = (p * 10 + py) * 8 + row
                     new = table[t, 128 + 8 * x + y : 129 + 8 * x + y, :]
                     old = two[at : at + 1, :]
@@ -274,9 +278,9 @@
     return total + product(rows(rest, mid_rest, 2, 2), taps[8, :, 0:128])
 
 
-def run_pair(pair, index, scalars, field, table, taps, biases, skip, new, work):
+def run_pair(pair, index, names, scalars, field, table, taps, biases, skip, new, work):
     one, two, high, rest, mid_high, mid_rest = work
-    fill_margins(pair, scalars, field, table, one, two)
+    fill_margins(pair, names, scalars, field, table, one, two)
     split(one, two, high, rest, mid_high, mid_rest)
     total = convolve(high, rest, mid_high, mid_rest, taps)
     bias = biases[index : index + 1, :]
@@ -288,30 +292,30 @@
     new[...] = jnp.where(slot < scalars[LIVE], jnp.maximum(total, 0.0), 0.0)
 
 
-def near_kernel(residual, index, scalars, field, faces_a, faces_b, *refs):
+def near_kernel(residual, index, names, scalars, field, faces_a, faces_b, *refs):
     arrived, (taps, biases), refs = refs[:4], refs[4:6], refs[6:]
     skip, refs = (refs[0], refs[1:]) if residual else (None, refs)
     new, faces, send, table = refs[:4]
     fill_table((faces_a, faces_b), arrived, table)
-    run_pair(0, index, scalars, field, table, taps, biases, skip, new, refs[4:])
+    run_pair(0, index, names, scalars, field, table, taps, biases, skip, new, refs[4:])
     write_faces(new, faces)
     offer(scalars[SECOND], faces, send)
 
 
-def far_kernel(residual, index, scalars, field, table, taps, biases, *refs):
+def far_kernel(residual, index, names, scalars, field, table, taps, biases, *refs):
     skip, refs = (refs[0], refs[1:]) if residual else (None, refs)
     new, faces = refs[:2]
-    run_pair(1, index, scalars, field, table, taps, biases, skip, new, refs[2:])
+    run_pair(1, index, names, scalars, field, table, taps, biases, skip, new, refs[2:])
     write_faces(new, faces)
 
 
-def last_kernel(index, scalars, field_a, field_b, faces_a, faces_b, *refs):
+def last_kernel(index, names, scalars, field_a, field_b, faces_a, faces_b, *refs):
     arrived, (taps, biases, skip_a, skip_b, out, table, new_a, new_b, stage, sems), work = refs[:4], refs[4:14], refs[14:]
     fill_table((faces_a, faces_b), arrived, table)
     copies = []
     for pair, field, skip, new in ((0, field_a, skip_a, new_a), (1, field_b, skip_b, new_b)):
         own = work[6 * pair : 6 * pair + 6]
-        run_pair(pair, index, scalars, field, table, taps, biases, skip, new, own)
+        run_pair(pair, index, names, scalars, field, table, taps, biases, skip, new, own)
         for b in range(2):
             at = 2 * pair + b
             for x in range(8):
@@ -337,16 +341,23 @@
 ]
 
 
-def swaps(size, first):
-    pairs = [(i, i + 1) for i in range(first, size - 1, 2)]
-    return pairs + [(b, a) for a, b in pairs]
+def swaps(along, first):
+    spaces, slabs = lax.axis_size("space"), lax.axis_size("slab")
+    pairs = []
+    for space in range(spaces):
+        for slab in range(slabs):
+            place, size = ((space, spaces), (slab, slabs))[along]
+            other = place + 1 if (place - first) % 2 == 0 else place - 1
+            if 0 <= other < size:
+                to = ((other, slab), (space, other))[along]
+            else:
+                to = ((space, slab ^ 1), (space ^ 1, slab))[along]
+            pairs.append((space * slabs + slab, to[0] * slabs + to[1]))
+    return pairs
 
 
 def exchange(send):
-    got = []
-    for axis in ("space", "slab"):
-        size = lax.axis_size(axis)
-        got += [lax.ppermute(send, axis, swaps(size, first)) for first in (0, 1)]
+    got = [lax.ppermute(send, ("space", "slab"), swaps(at // 2, at % 2)) for at in range(4)]
     return [got[at] for at in ORDER]
 
 
@@ -378,14 +389,19 @@
         (live, in_hbm(rim_slots), in_hbm(features)),
     )
     turned = jnp.transpose(weights, (1, 0, 2))
-    field_b, faces_b, held, scalars = call(
+    field_b, faces_b, held, names, scalars = call(
         second_entry_kernel,
         "second_entry",
-        (FIELD, FACES, jax.ShapeDtypeStruct(turned.shape, F32), pltpu.SMEM((LIVE + 1,), jnp.int32)),
+        (FIELD, FACES, jax.ShapeDtypeStruct(turned.shape, F32), pltpu.SMEM((BRICK, 128), jnp.int32), pltpu.SMEM((LIVE + 1,), jnp.int32)),
         [pl.BlockSpec(memory_space=pl.ANY), SM, HB, HB, HB, HB],
-        entry_scratch + [pltpu.SMEM(neighbours.shape, jnp.int32), pltpu.SemaphoreType.DMA((2,))],
+        entry_scratch
+        + [
+            pltpu.VMEM(neighbours.shape, jnp.int32),
+            pltpu.VMEM((BRICK, 128), jnp.int32),
+            pltpu.SemaphoreType.DMA((3,)),
+        ],
         (send, live, in_hbm(rim_slots), in_hbm(features), in_hbm(turned), in_hbm(neighbours)),
-        (VM, VM, VM, SM),
+        (VM, VM, VM, SM, SM),
     )
     plain = None
 
@@ -404,26 +420,26 @@
     def layer(index, fields, faces, send, skips):
         arrived = exchange(send)
         taps = taps_of(index, send)
-        args = [scalars, fields[0], *faces, *arrived, taps, biases]
+        args = [names, scalars, fields[0], *faces, *arrived, taps, biases]
         if skips is not None:
             args.append(skips[0])
         kernel = functools.partial(near_kernel, skips is not None, index)
-        specs = [SM] + [VM] * (len(args) - 1)
+        specs = [SM, SM] + [VM] * (len(args) - 2)
         new_a, faces_a, send, table = call(
             kernel, f"near{index}", (FIELD, FACES, SEND, TABLE), specs, WORK, args
         )
-        args = [scalars, fields[1], table, taps, biases]
+        args = [names, scalars, fields[1], table, taps, biases]
         if skips is not None:
             args.append(skips[1])
         kernel = functools.partial(far_kernel, skips is not None, index)
-        specs = [SM] + [VM] * (len(args) - 1)
+        specs = [SM, SM] + [VM] * (len(args) - 2)
         new_b, faces_b = call(kernel, f"far{index}", (FIELD, FACES), specs, WORK, args)
         return (new_a, new_b), (faces_a, faces_b), send
 
     def finish(index, fields, faces, send, skips):
         arrived = exchange(send)
         taps = taps_of(index, send)
-        args = [scalars, *fields, *faces, *arrived, taps, biases, *skips]
+        args = [names, scalars, *fields, *faces, *arrived, taps, biases, *skips]
         scratch = [
             pltpu.VMEM(TABLE.shape, F32),
             pltpu.VMEM(FIELD.shape, F32),
@@ -433,7 +449,7 @@
         ]
         out = (jax.ShapeDtypeStruct(features.shape, F32),)
         kernel = functools.partial(last_kernel, index)
-        specs = [SM] + [VM] * (len(args) - 1)
+        specs = [SM, SM] + [VM] * (len(args) - 2)
         return call(kernel, f"last{index}", out, specs, scratch + WORK + WORK, args, (HB,))[0]
 
     state = (field_a, field_b), (faces_a, faces_b), send

time: 55.3 us -> 42.5 us (0.77)
  the two profiles are of different devices: /device:TPU:75 before, /device:TPU:4 now
where the time goes in v5:
time: 42.5 us; the launch traced here: 42.4 us
  Pallas kernels  16.7 us (39%)
  waiting for transfers between devices  15.2 us (36%)
  starting transfers between devices  9.56 us (22%)
  between operations  0.91 us (2%)
    pallas_call x13, Pallas kernels, call(): pl.pallas_call(kernel, out_shape=out_shape, in_specs=in_specs, out_specs=...  16.7 us
    ppermute x16, waiting for transfers between devices, exchange(): lax.ppermute(send, ('space', 'slab'), swaps(at // 2, at % 2))  15.2 us
    ppermute x16, starting transfers between devices, exchange(): lax.ppermute(send, ('space', 'slab'), swaps(at // 2, at % 2))  9.56 us
  transfers between devices with their start and end apart: 16, of which 9 were waited for; matrix products, arithmetic and copies ran while one was open for 0% of the time, Pallas kernels for 18%

profile of v5, /device:TPU:4, one launch (start us, length us, event | category | flops | bytes accessed | tf_op | source)
XLA Modules:
  0.0 42.4 jit_solution(14760761702162324086)
XLA Ops:
  0.7 1.2 %entry.1 = (f32[512,128]{1,0:T(8,128)S(1)}, f32[2,192,128]{2,1,0:T(8,128)S(1)}, f32[2,152,128]{2,1,0:T(8,128)S(1)}) custom-call(s32[1]{0:T(128)S(6)} %copy.7.live, s32[1,2]{1,0:T(1,128)} %slots.3, f32[4,8,8,512]{3,2,1,0:T(8,128)} %feat.3), custom_call_target="tpu_custom_call" | custom-call | flops 600000000 | bytes 4194304 | tf_op jit(solution)/shard_map/entry/pallas_call | solution.py:371
  1.8 1.3 %collective-permute-start.3 = (f32[2,152,128]{2,1,0:T(8,128)S(1)}, f32[2,152,128]{2,1,0:T(8,128)S(1)}, u32[]{:S(2)}, u32[]{:S(2)}) collective-permute-start(f32[2,152,128]{2,1,0:T(8,128)S(1)} %get-tuple-element.33.after), channel_id=1, source_target_pairs={{0,1},{1,0},{2,3},{3,2},{4,8},{5,9},{6,10},{7,11},{8,4},{9,5},{10,... | collective-permute-start | bytes 466952 | tf_op jit(solution)/shard_map/ppermute | solution.py:360
  3.1 0.8 %collective-permute-start.2 = (f32[2,152,128]{2,1,0:T(8,128)S(1)}, f32[2,152,128]{2,1,0:T(8,128)S(1)}, u32[]{:S(2)}, u32[]{:S(2)}) collective-permute-start(f32[2,152,128]{2,1,0:T(8,128)S(1)} %get-tuple-element.33.after), channel_id=1, source_target_pairs={{0,1},{1,0},{2,3},{3,2},{4,5},{5,4},{6,7},{7,6},{8,9},{9,8},{10,11... | collective-permute-start | bytes 466952 | tf_op jit(solution)/shard_map/ppermute | solution.py:360
  3.9 0.5 %collective-permute-start.1 = (f32[2,152,128]{2,1,0:T(8,128)S(1)}, f32[2,152,128]{2,1,0:T(8,128)S(1)}, u32[]{:S(2)}, u32[]{:S(2)}) collective-permute-start(f32[2,152,128]{2,1,0:T(8,128)S(1)} %get-tuple-element.33.after), channel_id=1, source_target_pairs={{0,4},{1,2},{2,1},{3,7},{4,0},{5,6},{6,5},{7,3},{8,12},{9,10},{10,... | collective-permute-start | bytes 466952 | tf_op jit(solution)/shard_map/ppermute | solution.py:360
  4.5 2.3 %second_entry.1 = (f32[512,128]{1,0:T(8,128)S(1)}, f32[2,192,128]{2,1,0:T(8,128)S(1)}, f32[27,4,4096]{2,1,0:T(4,128)S(1)}, s32[4,128]{1,0:T(4,128)S(4)}, s32[6]{0:T(128)S(4)}) custom-call(f32[2,152,128]{2,1,0:T(8,128)S(1)} %get-tuple-element.33.after, s32[1]{0:T(128)S(6)} %copy.7.live, s32[1,2]{1,0:T(1,128)} %slots.3, f32[4,8,8,512]{3,2,1,0:T(8,128)} %feat.3, ...), custom_call_target="tpu_custom_call" | custom-call | flops 600000000 | bytes 4194304 | tf_op jit(solution)/shard_map/second_entry/pallas_call | solution.py:371
  6.8 0.4 %taps0.1 = (f32[3456,128]{1,0:T(8,128)S(1)}, bf16[9,256,256]{2,1,0:T(8,128)(2,1)S(1)}) custom-call(f32[27,4,4096]{2,1,0:T(4,128)S(1)} %get-tuple-element.39.weights), custom_call_target="tpu_custom_call" | custom-call | flops 600000000 | bytes 4194304 | tf_op jit(solution)/shard_map/taps0/pallas_call | solution.py:371
  7.3 0.8 %collective-permute-done.3.refs_3_ = f32[2,152,128]{2,1,0:T(8,128)S(1)} collective-permute-done((f32[2,152,128]{2,1,0:T(8,128)S(1)}, f32[2,152,128]{2,1,0:T(8,128)S(1)}, u32[]{:S(2)}, u32[]{:S(2)}) %collective-permute-start.3) | collective-permute-done | bytes 155680 | tf_op jit(solution)/shard_map/ppermute | solution.py:360
  8.1 2.3 %collective-permute-done.2.refs_2_ = f32[2,152,128]{2,1,0:T(8,128)S(1)} collective-permute-done((f32[2,152,128]{2,1,0:T(8,128)S(1)}, f32[2,152,128]{2,1,0:T(8,128)S(1)}, u32[]{:S(2)}, u32[]{:S(2)}) %collective-permute-start.2) | collective-permute-done | bytes 155680 | tf_op jit(solution)/shard_map/ppermute | solution.py:360
  10.5 1.5 %near0.1 = (f32[512,128]{1,0:T(8,128)S(1)}, f32[2,192,128]{2,1,0:T(8,128)S(1)}, f32[2,152,128]{2,1,0:T(8,128)S(1)}, f32[13,192,128]{2,1,0:T(8,128)S(1)}) custom-call(s32[4,128]{1,0:T(4,128)S(4)} %get-tuple-element.34.names, s32[6]{0:T(128)S(4)} %get-tuple-element.35.scalars, f32[512,128]{1,0:T(8,128)S(1)} %get-tuple-element.36.field.refs_6_, ...), custom_call_target="tpu_custom_call" | custom-call | flops 600000000 | bytes 4194304 | tf_op jit(solution)/shard_map/near0/pallas_call | solution.py:371
  12.0 1.3 %collective-permute-start.7 = (f32[2,152,128]{2,1,0:T(8,128)S(1)}, f32[2,152,128]{2,1,0:T(8,128)S(1)}, u32[]{:S(2)}, u32[]{:S(2)}) collective-permute-start(f32[2,152,128]{2,1,0:T(8,128)S(1)} %get-tuple-element.46.after), channel_id=1, source_target_pairs={{0,1},{1,0},{2,3},{3,2},{4,8},{5,9},{6,10},{7,11},{8,4},{9,5},{10,... | collective-permute-start | bytes 466952 | tf_op jit(solution)/shard_map/ppermute | solution.py:360
  13.2 0.8 %collective-permute-start.6 = (f32[2,152,128]{2,1,0:T(8,128)S(1)}, f32[2,152,128]{2,1,0:T(8,128)S(1)}, u32[]{:S(2)}, u32[]{:S(2)}) collective-permute-start(f32[2,152,128]{2,1,0:T(8,128)S(1)} %get-tuple-element.46.after), channel_id=1, source_target_pairs={{0,1},{1,0},{2,3},{3,2},{4,5},{5,4},{6,7},{7,6},{8,9},{9,8},{10,11... | collective-permute-start | bytes 466952 | tf_op jit(solution)/shard_map/ppermute | solution.py:360
  14.1 0.5 %collective-permute-start.5 = (f32[2,152,128]{2,1,0:T(8,128)S(1)}, f32[2,152,128]{2,1,0:T(8,128)S(1)}, u32[]{:S(2)}, u32[]{:S(2)}) collective-permute-start(f32[2,152,128]{2,1,0:T(8,128)S(1)} %get-tuple-element.46.after), channel_id=1, source_target_pairs={{0,4},{1,2},{2,1},{3,7},{4,0},{5,6},{6,5},{7,3},{8,12},{9,10},{10,... | collective-permute-start | bytes 466952 | tf_op jit(solution)/shard_map/ppermute | solution.py:360
  14.6 0.4 taps1.1.refs_4_.taps
  15.0 1.3 %far0.1 = (f32[512,128]{1,0:T(8,128)S(1)}, f32[2,192,128]{2,1,0:T(8,128)S(1)}) custom-call(s32[4,128]{1,0:T(4,128)S(4)} %get-tuple-element.34.names, s32[6]{0:T(128)S(4)} %get-tuple-element.35.scalars, f32[512,128]{1,0:T(8,128)S(1)} %get-tuple-element.43.field.refs_0_, f32[13,192,128]{2,1,0:T(8,128)S(1)} %get-tuple-element.44.table, ...), custom_call_target="tpu_custom_call" | custom-call | flops 600000000 | bytes 4194304 | tf_op jit(solution)/shard_map/far0/pallas_call | solution.py:371
  16.3 2.5 %collective-permute-done.7.refs_3_ = f32[2,152,128]{2,1,0:T(8,128)S(1)} collective-permute-done((f32[2,152,128]{2,1,0:T(8,128)S(1)}, f32[2,152,128]{2,1,0:T(8,128)S(1)}, u32[]{:S(2)}, u32[]{:S(2)}) %collective-permute-start.7) | collective-permute-done | bytes 155680 | tf_op jit(solution)/shard_map/ppermute | solution.py:360
  18.9 1.7 %collective-permute-done.6.refs_2_ = f32[2,152,128]{2,1,0:T(8,128)S(1)} collective-permute-done((f32[2,152,128]{2,1,0:T(8,128)S(1)}, f32[2,152,128]{2,1,0:T(8,128)S(1)}, u32[]{:S(2)}, u32[]{:S(2)}) %collective-permute-start.6) | collective-permute-done | bytes 155680 | tf_op jit(solution)/shard_map/ppermute | solution.py:360
  20.6 1.5 %near1.1 = (f32[512,128]{1,0:T(8,128)S(1)}, f32[2,192,128]{2,1,0:T(8,128)S(1)}, f32[2,152,128]{2,1,0:T(8,128)S(1)}, f32[13,192,128]{2,1,0:T(8,128)S(1)}) custom-call(s32[4,128]{1,0:T(4,128)S(4)} %get-tuple-element.34.names, s32[6]{0:T(128)S(4)} %get-tuple-element.35.scalars, f32[512,128]{1,0:T(8,128)S(1)} %get-tuple-element.41.field, ...), custom_call_target="tpu_custom_call" | custom-call | flops 600000000 | bytes 4194304 | tf_op jit(solution)/shard_map/near1/pallas_call | solution.py:371
  22.1 0.4 %collective-permute-start.11 = (f32[2,152,128]{2,1,0:T(8,128)S(1)}, f32[2,152,128]{2,1,0:T(8,128)S(1)}, u32[]{:S(2)}, u32[]{:S(2)}) collective-permute-start(f32[2,152,128]{2,1,0:T(8,128)S(1)} %get-tuple-element.53.after), channel_id=1, source_target_pairs={{0,1},{1,0},{2,3},{3,2},{4,8},{5,9},{6,10},{7,11},{8,4},{9,5},{10,... | collective-permute-start | bytes 466952 | tf_op jit(solution)/shard_map/ppermute | solution.py:360
  22.5 1.7 %collective-permute-start.10 = (f32[2,152,128]{2,1,0:T(8,128)S(1)}, f32[2,152,128]{2,1,0:T(8,128)S(1)}, u32[]{:S(2)}, u32[]{:S(2)}) collective-permute-start(f32[2,152,128]{2,1,0:T(8,128)S(1)} %get-tuple-element.53.after), channel_id=1, source_target_pairs={{0,1},{1,0},{2,3},{3,2},{4,5},{5,4},{6,7},{7,6},{8,9},{9,8},{10,11... | collective-permute-start | bytes 466952 | tf_op jit(solution)/shard_map/ppermute | solution.py:360
  24.2 0.4 taps2.1.refs_4_.taps
  24.6 1.3 %far1.1 = (f32[512,128]{1,0:T(8,128)S(1)}, f32[2,192,128]{2,1,0:T(8,128)S(1)}) custom-call(s32[4,128]{1,0:T(4,128)S(4)} %get-tuple-element.34.names, s32[6]{0:T(128)S(4)} %get-tuple-element.35.scalars, f32[512,128]{1,0:T(8,128)S(1)} %get-tuple-element.50.field, f32[13,192,128]{2,1,0:T(8,128)S(1)} %get-tuple-element.51.table, ...), custom_call_target="tpu_custom_call" | custom-call | flops 600000000 | bytes 4194304 | tf_op jit(solution)/shard_map/far1/pallas_call | solution.py:371
  25.9 2.5 %collective-permute-done.11.refs_3_ = f32[2,152,128]{2,1,0:T(8,128)S(1)} collective-permute-done((f32[2,152,128]{2,1,0:T(8,128)S(1)}, f32[2,152,128]{2,1,0:T(8,128)S(1)}, u32[]{:S(2)}, u32[]{:S(2)}) %collective-permute-start.11) | collective-permute-done | bytes 155680 | tf_op jit(solution)/shard_map/ppermute | solution.py:360
  28.4 1.7 %collective-permute-done.10.refs_2_ = f32[2,152,128]{2,1,0:T(8,128)S(1)} collective-permute-done((f32[2,152,128]{2,1,0:T(8,128)S(1)}, f32[2,152,128]{2,1,0:T(8,128)S(1)}, u32[]{:S(2)}, u32[]{:S(2)}) %collective-permute-start.10) | collective-permute-done | bytes 155680 | tf_op jit(solution)/shard_map/ppermute | solution.py:360
  30.1 1.5 %near2.1 = (f32[512,128]{1,0:T(8,128)S(1)}, f32[2,192,128]{2,1,0:T(8,128)S(1)}, f32[2,152,128]{2,1,0:T(8,128)S(1)}, f32[13,192,128]{2,1,0:T(8,128)S(1)}) custom-call(s32[4,128]{1,0:T(4,128)S(4)} %get-tuple-element.34.names, s32[6]{0:T(128)S(4)} %get-tuple-element.35.scalars, f32[512,128]{1,0:T(8,128)S(1)} %get-tuple-element.48.field.refs_6_, ...), custom_call_target="tpu_custom_call" | custom-call | flops 600000000 | bytes 4194304 | tf_op jit(solution)/shard_map/near2/pallas_call | solution.py:371
  31.5 0.4 collective-permute-start.15
  31.9 1.7 %collective-permute-start.14 = (f32[2,152,128]{2,1,0:T(8,128)S(1)}, f32[2,152,128]{2,1,0:T(8,128)S(1)}, u32[]{:S(2)}, u32[]{:S(2)}) collective-permute-start(f32[2,152,128]{2,1,0:T(8,128)S(1)} %get-tuple-element.60.after), channel_id=1, source_target_pairs={{0,1},{1,0},{2,3},{3,2},{4,5},{5,4},{6,7},{7,6},{8,9},{9,8},{10,11... | collective-permute-start | bytes 466952 | tf_op jit(solution)/shard_map/ppermute | solution.py:360
  33.7 0.4 taps3.1.refs_4_
  34.0 1.3 %far2.1 = (f32[512,128]{1,0:T(8,128)S(1)}, f32[2,192,128]{2,1,0:T(8,128)S(1)}) custom-call(s32[4,128]{1,0:T(4,128)S(4)} %get-tuple-element.34.names, s32[6]{0:T(128)S(4)} %get-tuple-element.35.scalars, f32[512,128]{1,0:T(8,128)S(1)} %get-tuple-element.55.field.refs_7_, f32[13,192,128]{2,1,0:T(8,128)S(1)} %get-tuple-element.56.table, ...), custom_call_target="tpu_custom_call" | custom-call | flops 600000000 | bytes 4194304 | tf_op jit(solution)/shard_map/far2/pallas_call | solution.py:371
  35.4 1.5 %collective-permute-done.15.refs_3_ = f32[2,152,128]{2,1,0:T(8,128)S(1)} collective-permute-done((f32[2,152,128]{2,1,0:T(8,128)S(1)}, f32[2,152,128]{2,1,0:T(8,128)S(1)}, u32[]{:S(2)}, u32[]{:S(2)}) %collective-permute-start.15) | collective-permute-done | bytes 155680 | tf_op jit(solution)/shard_map/ppermute | solution.py:360
  36.9 1.7 %collective-permute-done.14.refs_2_ = f32[2,152,128]{2,1,0:T(8,128)S(1)} collective-permute-done((f32[2,152,128]{2,1,0:T(8,128)S(1)}, f32[2,152,128]{2,1,0:T(8,128)S(1)}, u32[]{:S(2)}, u32[]{:S(2)}) %collective-permute-start.14) | collective-permute-done | bytes 155680 | tf_op jit(solution)/shard_map/ppermute | solution.py:360
  38.6 0.3 collective-permute-done.13.refs_1_
  38.9 3.3 %last3.1 = f32[4,8,8,512]{3,2,1,0:T(8,128)} custom-call(s32[4,128]{1,0:T(4,128)S(4)} %get-tuple-element.34.names, s32[6]{0:T(128)S(4)} %get-tuple-element.35.scalars, f32[512,128]{1,0:T(8,128)S(1)} %get-tuple-element.54.field_a, f32[512,128]{1,0:T(8,128)S(1)} %get-tuple-element.57.field_b, f32[2,192,128]{2,1,0:T(8,128)S(1)} %get-tuple-element.58.faces_a, ...), custom_call_target="tpu_custom_call" | custom-call | flops 600000000 | bytes 4194304 | tf_op jit(solution)/shard_map/last3/pallas_call | solution.py:371
  (15 shorter events, 0.1 us)
Async XLA Ops:
  1.8 6.3 %collective-permute-start.3 = (f32[2,152,128]{2,1,0:T(8,128)S(1)}, f32[2,152,128]{2,1,0:T(8,128)S(1)}, u32[]{:S(2)}, u32[]{:S(2)}) collective-permute-start(f32[2,152,128]{2,1,0:T(8,128)S(1)} %get-tuple-element.33.after), channel_id=1, source_target_pairs={{0,1},{1,0},{2,3},{3,2},{4,8},{5,9},{6,10},{7,11},{8,4},{9,5},{10,... | collective-permute-start | bytes 466952 | tf_op jit(solution)/shard_map/ppermute | solution.py:360
  3.1 7.4 %collective-permute-start.2 = (f32[2,152,128]{2,1,0:T(8,128)S(1)}, f32[2,152,128]{2,1,0:T(8,128)S(1)}, u32[]{:S(2)}, u32[]{:S(2)}) collective-permute-start(f32[2,152,128]{2,1,0:T(8,128)S(1)} %get-tuple-element.33.after), channel_id=1, source_target_pairs={{0,1},{1,0},{2,3},{3,2},{4,5},{5,4},{6,7},{7,6},{8,9},{9,8},{10,11... | collective-permute-start | bytes 466952 | tf_op jit(solution)/shard_map/ppermute | solution.py:360
  3.9 6.5 %collective-permute-start.1 = (f32[2,152,128]{2,1,0:T(8,128)S(1)}, f32[2,152,128]{2,1,0:T(8,128)S(1)}, u32[]{:S(2)}, u32[]{:S(2)}) collective-permute-start(f32[2,152,128]{2,1,0:T(8,128)S(1)} %get-tuple-element.33.after), channel_id=1, source_target_pairs={{0,4},{1,2},{2,1},{3,7},{4,0},{5,6},{6,5},{7,3},{8,12},{9,10},{10,... | collective-permute-start | bytes 466952 | tf_op jit(solution)/shard_map/ppermute | solution.py:360
  4.5 6.0 %collective-permute-start = (f32[2,152,128]{2,1,0:T(8,128)S(1)}, f32[2,152,128]{2,1,0:T(8,128)S(1)}, u32[]{:S(2)}, u32[]{:S(2)}) collective-permute-start(f32[2,152,128]{2,1,0:T(8,128)S(1)} %get-tuple-element.33.after), channel_id=1, source_target_pairs={{0,4},{1,5},{2,6},{3,7},{4,0},{5,1},{6,2},{7,3},{8,12},{9,13},{10,... | collective-permute-start | bytes 466952 | tf_op jit(solution)/shard_map/ppermute | solution.py:360
  6.8 3.6 %copy-start = (f32[4,64]{1,0:T(4,128)S(1)}, f32[4,64]{1,0:T(4,128)}, u32[]{:S(2)}) copy-start(f32[4,64]{1,0:T(4,128)} %refs_5_.7) | copy-start | bytes 3076
  12.0 6.9 %collective-permute-start.7 = (f32[2,152,128]{2,1,0:T(8,128)S(1)}, f32[2,152,128]{2,1,0:T(8,128)S(1)}, u32[]{:S(2)}, u32[]{:S(2)}) collective-permute-start(f32[2,152,128]{2,1,0:T(8,128)S(1)} %get-tuple-element.46.after), channel_id=1, source_target_pairs={{0,1},{1,0},{2,3},{3,2},{4,8},{5,9},{6,10},{7,11},{8,4},{9,5},{10,... | collective-permute-start | bytes 466952 | tf_op jit(solution)/shard_map/ppermute | solution.py:360
  13.2 7.4 %collective-permute-start.6 = (f32[2,152,128]{2,1,0:T(8,128)S(1)}, f32[2,152,128]{2,1,0:T(8,128)S(1)}, u32[]{:S(2)}, u32[]{:S(2)}) collective-permute-start(f32[2,152,128]{2,1,0:T(8,128)S(1)} %get-tuple-element.46.after), channel_id=1, source_target_pairs={{0,1},{1,0},{2,3},{3,2},{4,5},{5,4},{6,7},{7,6},{8,9},{9,8},{10,11... | collective-permute-start | bytes 466952 | tf_op jit(solution)/shard_map/ppermute | solution.py:360
  14.1 6.5 %collective-permute-start.5 = (f32[2,152,128]{2,1,0:T(8,128)S(1)}, f32[2,152,128]{2,1,0:T(8,128)S(1)}, u32[]{:S(2)}, u32[]{:S(2)}) collective-permute-start(f32[2,152,128]{2,1,0:T(8,128)S(1)} %get-tuple-element.46.after), channel_id=1, source_target_pairs={{0,4},{1,2},{2,1},{3,7},{4,0},{5,6},{6,5},{7,3},{8,12},{9,10},{10,... | collective-permute-start | bytes 466952 | tf_op jit(solution)/shard_map/ppermute | solution.py:360
  14.6 6.0 %collective-permute-start.4 = (f32[2,152,128]{2,1,0:T(8,128)S(1)}, f32[2,152,128]{2,1,0:T(8,128)S(1)}, u32[]{:S(2)}, u32[]{:S(2)}) collective-permute-start(f32[2,152,128]{2,1,0:T(8,128)S(1)} %get-tuple-element.46.after), channel_id=1, source_target_pairs={{0,4},{1,5},{2,6},{3,7},{4,0},{5,1},{6,2},{7,3},{8,12},{9,13},{10,... | collective-permute-start | bytes 466952 | tf_op jit(solution)/shard_map/ppermute | solution.py:360
  22.1 6.3 %collective-permute-start.11 = (f32[2,152,128]{2,1,0:T(8,128)S(1)}, f32[2,152,128]{2,1,0:T(8,128)S(1)}, u32[]{:S(2)}, u32[]{:S(2)}) collective-permute-start(f32[2,152,128]{2,1,0:T(8,128)S(1)} %get-tuple-element.53.after), channel_id=1, source_target_pairs={{0,1},{1,0},{2,3},{3,2},{4,8},{5,9},{6,10},{7,11},{8,4},{9,5},{10,... | collective-permute-start | bytes 466952 | tf_op jit(solution)/shard_map/ppermute | solution.py:360
  22.5 7.5 %collective-permute-start.10 = (f32[2,152,128]{2,1,0:T(8,128)S(1)}, f32[2,152,128]{2,1,0:T(8,128)S(1)}, u32[]{:S(2)}, u32[]{:S(2)}) collective-permute-start(f32[2,152,128]{2,1,0:T(8,128)S(1)} %get-tuple-element.53.after), channel_id=1, source_target_pairs={{0,1},{1,0},{2,3},{3,2},{4,5},{5,4},{6,7},{7,6},{8,9},{9,8},{10,11... | collective-permute-start | bytes 466952 | tf_op jit(solution)/shard_map/ppermute | solution.py:360
  24.2 5.9 %collective-permute-start.9 = (f32[2,152,128]{2,1,0:T(8,128)S(1)}, f32[2,152,128]{2,1,0:T(8,128)S(1)}, u32[]{:S(2)}, u32[]{:S(2)}) collective-permute-start(f32[2,152,128]{2,1,0:T(8,128)S(1)} %get-tuple-element.53.after), channel_id=1, source_target_pairs={{0,4},{1,2},{2,1},{3,7},{4,0},{5,6},{6,5},{7,3},{8,12},{9,10},{10,... | collective-permute-start | bytes 466952 | tf_op jit(solution)/shard_map/ppermute | solution.py:360
  24.2 5.9 %collective-permute-start.8 = (f32[2,152,128]{2,1,0:T(8,128)S(1)}, f32[2,152,128]{2,1,0:T(8,128)S(1)}, u32[]{:S(2)}, u32[]{:S(2)}) collective-permute-start(f32[2,152,128]{2,1,0:T(8,128)S(1)} %get-tuple-element.53.after), channel_id=1, source_target_pairs={{0,4},{1,5},{2,6},{3,7},{4,0},{5,1},{6,2},{7,3},{8,12},{9,13},{10,... | collective-permute-start | bytes 466952 | tf_op jit(solution)/shard_map/ppermute | solution.py:360
  31.5 5.4 %collective-permute-start.15 = (f32[2,152,128]{2,1,0:T(8,128)S(1)}, f32[2,152,128]{2,1,0:T(8,128)S(1)}, u32[]{:S(2)}, u32[]{:S(2)}) collective-permute-start(f32[2,152,128]{2,1,0:T(8,128)S(1)} %get-tuple-element.60.after), channel_id=1, source_target_pairs={{0,1},{1,0},{2,3},{3,2},{4,8},{5,9},{6,10},{7,11},{8,4},{9,5},{10,... | collective-permute-start | bytes 466952 | tf_op jit(solution)/shard_map/ppermute | solution.py:360
  31.9 6.7 %collective-permute-start.14 = (f32[2,152,128]{2,1,0:T(8,128)S(1)}, f32[2,152,128]{2,1,0:T(8,128)S(1)}, u32[]{:S(2)}, u32[]{:S(2)}) collective-permute-start(f32[2,152,128]{2,1,0:T(8,128)S(1)} %get-tuple-element.60.after), channel_id=1, source_target_pairs={{0,1},{1,0},{2,3},{3,2},{4,5},{5,4},{6,7},{7,6},{8,9},{9,8},{10,11... | collective-permute-start | bytes 466952 | tf_op jit(solution)/shard_map/ppermute | solution.py:360
  33.6 5.2 %collective-permute-start.13 = (f32[2,152,128]{2,1,0:T(8,128)S(1)}, f32[2,152,128]{2,1,0:T(8,128)S(1)}, u32[]{:S(2)}, u32[]{:S(2)}) collective-permute-start(f32[2,152,128]{2,1,0:T(8,128)S(1)} %get-tuple-element.60.after), channel_id=1, source_target_pairs={{0,4},{1,2},{2,1},{3,7},{4,0},{5,6},{6,5},{7,3},{8,12},{9,10},{10,... | collective-permute-start | bytes 466952 | tf_op jit(solution)/shard_map/ppermute | solution.py:360
  33.7 5.2 %collective-permute-start.12 = (f32[2,152,128]{2,1,0:T(8,128)S(1)}, f32[2,152,128]{2,1,0:T(8,128)S(1)}, u32[]{:S(2)}, u32[]{:S(2)}) collective-permute-start(f32[2,152,128]{2,1,0:T(8,128)S(1)} %get-tuple-element.60.after), channel_id=1, source_target_pairs={{0,4},{1,5},{2,6},{3,7},{4,0},{5,1},{6,2},{7,3},{8,12},{9,13},{10,... | collective-permute-start | bytes 466952 | tf_op jit(solution)/shard_map/ppermute | solution.py:360

commit v6 on v5

--- a/solution.py
+++ b/solution.py
@@ -15,7 +15,7 @@
 SM = pl.BlockSpec(memory_space=pltpu.SMEM)
 HB = pl.BlockSpec(memory_space=pltpu.HBM)
 F32, BF16 = jnp.float32, jnp.bfloat16
-ORDER = [0, 3, 2, 1]
+ORDER = [0, 3, 1, 2]
 PLACE, SECOND, LIVE = 0, 4, 5
 
 

time: 42.5 us -> 42.6 us (level)
  the two profiles are of different devices: /device:TPU:4 before, /device:TPU:96 now
where the time goes in v6:
time: 42.6 us; the launch traced here: 42.4 us
  Pallas kernels  16.7 us (39%)
  starting transfers between devices  12.8 us (30%)
  waiting for transfers between devices  12 us (28%)
  between operations  0.92 us (2%)
    pallas_call x13, Pallas kernels, call(): pl.pallas_call(kernel, out_shape=out_shape, in_specs=in_specs, out_specs=...  16.7 us
    ppermute x16, starting transfers between devices, exchange(): lax.ppermute(send, ('space', 'slab'), swaps(at // 2, at % 2))  12.8 us
    ppermute x16, waiting for transfers between devices, exchange(): lax.ppermute(send, ('space', 'slab'), swaps(at // 2, at % 2))  12 us
  transfers between devices with their start and end apart: 16, of which 7 were waited for; matrix products, arithmetic and copies ran while one was open for 0% of the time, Pallas kernels for 18%

profile of v6, /device:TPU:96, one launch (start us, length us, event | category | flops | bytes accessed | tf_op | source)
XLA Modules:
  0.0 42.4 jit_solution(87306647526531024)
XLA Ops:
  0.7 1.2 %entry.1 = (f32[512,128]{1,0:T(8,128)S(1)}, f32[2,192,128]{2,1,0:T(8,128)S(1)}, f32[2,152,128]{2,1,0:T(8,128)S(1)}) custom-call(s32[1]{0:T(128)S(6)} %copy.7.live, s32[1,2]{1,0:T(1,128)} %slots.3, f32[4,8,8,512]{3,2,1,0:T(8,128)} %feat.3), custom_call_target="tpu_custom_call" | custom-call | flops 600000000 | bytes 4194304 | tf_op jit(solution)/shard_map/entry/pallas_call | solution.py:371
  1.8 1.6 %collective-permute-start.3 = (f32[2,152,128]{2,1,0:T(8,128)S(1)}, f32[2,152,128]{2,1,0:T(8,128)S(1)}, u32[]{:S(2)}, u32[]{:S(2)}) collective-permute-start(f32[2,152,128]{2,1,0:T(8,128)S(1)} %get-tuple-element.33.after), channel_id=1, source_target_pairs={{0,1},{1,0},{2,3},{3,2},{4,5},{5,4},{6,7},{7,6},{8,9},{9,8},{10,11... | collective-permute-start | bytes 466952 | tf_op jit(solution)/shard_map/ppermute | solution.py:360
  3.4 2.0 %collective-permute-start.2 = (f32[2,152,128]{2,1,0:T(8,128)S(1)}, f32[2,152,128]{2,1,0:T(8,128)S(1)}, u32[]{:S(2)}, u32[]{:S(2)}) collective-permute-start(f32[2,152,128]{2,1,0:T(8,128)S(1)} %get-tuple-element.33.after), channel_id=1, source_target_pairs={{0,1},{1,0},{2,3},{3,2},{4,8},{5,9},{6,10},{7,11},{8,4},{9,5},{10,... | collective-permute-start | bytes 466952 | tf_op jit(solution)/shard_map/ppermute | solution.py:360
  5.4 0.5 %collective-permute-start = (f32[2,152,128]{2,1,0:T(8,128)S(1)}, f32[2,152,128]{2,1,0:T(8,128)S(1)}, u32[]{:S(2)}, u32[]{:S(2)}) collective-permute-start(f32[2,152,128]{2,1,0:T(8,128)S(1)} %get-tuple-element.33.after), channel_id=1, source_target_pairs={{0,4},{1,5},{2,6},{3,7},{4,0},{5,1},{6,2},{7,3},{8,12},{9,13},{10,... | collective-permute-start | bytes 466952 | tf_op jit(solution)/shard_map/ppermute | solution.py:360
  5.9 2.3 %second_entry.1 = (f32[512,128]{1,0:T(8,128)S(1)}, f32[2,192,128]{2,1,0:T(8,128)S(1)}, f32[27,4,4096]{2,1,0:T(4,128)S(1)}, s32[4,128]{1,0:T(4,128)S(4)}, s32[6]{0:T(128)S(4)}) custom-call(f32[2,152,128]{2,1,0:T(8,128)S(1)} %get-tuple-element.33.after, s32[1]{0:T(128)S(6)} %copy.7.live, s32[1,2]{1,0:T(1,128)} %slots.3, f32[4,8,8,512]{3,2,1,0:T(8,128)} %feat.3, ...), custom_call_target="tpu_custom_call" | custom-call | flops 600000000 | bytes 4194304 | tf_op jit(solution)/shard_map/second_entry/pallas_call | solution.py:371
  8.2 0.4 %taps0.1 = (f32[3456,128]{1,0:T(8,128)S(1)}, bf16[9,256,256]{2,1,0:T(8,128)(2,1)S(1)}) custom-call(f32[27,4,4096]{2,1,0:T(4,128)S(1)} %get-tuple-element.39.weights), custom_call_target="tpu_custom_call" | custom-call | flops 600000000 | bytes 4194304 | tf_op jit(solution)/shard_map/taps0/pallas_call | solution.py:371
  8.7 1.5 %collective-permute-done.2.refs_2_ = f32[2,152,128]{2,1,0:T(8,128)S(1)} collective-permute-done((f32[2,152,128]{2,1,0:T(8,128)S(1)}, f32[2,152,128]{2,1,0:T(8,128)S(1)}, u32[]{:S(2)}, u32[]{:S(2)}) %collective-permute-start.2) | collective-permute-done | bytes 155680 | tf_op jit(solution)/shard_map/ppermute | solution.py:360
  10.2 1.5 %near0.1 = (f32[512,128]{1,0:T(8,128)S(1)}, f32[2,192,128]{2,1,0:T(8,128)S(1)}, f32[2,152,128]{2,1,0:T(8,128)S(1)}, f32[13,192,128]{2,1,0:T(8,128)S(1)}) custom-call(s32[4,128]{1,0:T(4,128)S(4)} %get-tuple-element.34.names, s32[6]{0:T(128)S(4)} %get-tuple-element.35.scalars, f32[512,128]{1,0:T(8,128)S(1)} %get-tuple-element.36.field.refs_6_, ...), custom_call_target="tpu_custom_call" | custom-call | flops 600000000 | bytes 4194304 | tf_op jit(solution)/shard_map/near0/pallas_call | solution.py:371
  11.6 1.9 %collective-permute-start.7 = (f32[2,152,128]{2,1,0:T(8,128)S(1)}, f32[2,152,128]{2,1,0:T(8,128)S(1)}, u32[]{:S(2)}, u32[]{:S(2)}) collective-permute-start(f32[2,152,128]{2,1,0:T(8,128)S(1)} %get-tuple-element.46.after), channel_id=1, source_target_pairs={{0,1},{1,0},{2,3},{3,2},{4,5},{5,4},{6,7},{7,6},{8,9},{9,8},{10,11... | collective-permute-start | bytes 466952 | tf_op jit(solution)/shard_map/ppermute | solution.py:360
  13.5 1.0 %collective-permute-start.6 = (f32[2,152,128]{2,1,0:T(8,128)S(1)}, f32[2,152,128]{2,1,0:T(8,128)S(1)}, u32[]{:S(2)}, u32[]{:S(2)}) collective-permute-start(f32[2,152,128]{2,1,0:T(8,128)S(1)} %get-tuple-element.46.after), channel_id=1, source_target_pairs={{0,1},{1,0},{2,3},{3,2},{4,8},{5,9},{6,10},{7,11},{8,4},{9,5},{10,... | collective-permute-start | bytes 466952 | tf_op jit(solution)/shard_map/ppermute | solution.py:360
  14.5 0.5 %collective-permute-start.4 = (f32[2,152,128]{2,1,0:T(8,128)S(1)}, f32[2,152,128]{2,1,0:T(8,128)S(1)}, u32[]{:S(2)}, u32[]{:S(2)}) collective-permute-start(f32[2,152,128]{2,1,0:T(8,128)S(1)} %get-tuple-element.46.after), channel_id=1, source_target_pairs={{0,4},{1,5},{2,6},{3,7},{4,0},{5,1},{6,2},{7,3},{8,12},{9,13},{10,... | collective-permute-start | bytes 466952 | tf_op jit(solution)/shard_map/ppermute | solution.py:360
  15.0 0.4 taps1.1.refs_4_.taps
  15.4 1.3 %far0.1 = (f32[512,128]{1,0:T(8,128)S(1)}, f32[2,192,128]{2,1,0:T(8,128)S(1)}) custom-call(s32[4,128]{1,0:T(4,128)S(4)} %get-tuple-element.34.names, s32[6]{0:T(128)S(4)} %get-tuple-element.35.scalars, f32[512,128]{1,0:T(8,128)S(1)} %get-tuple-element.43.field.refs_0_, f32[13,192,128]{2,1,0:T(8,128)S(1)} %get-tuple-element.44.table, ...), custom_call_target="tpu_custom_call" | custom-call | flops 600000000 | bytes 4194304 | tf_op jit(solution)/shard_map/far0/pallas_call | solution.py:371
  16.7 0.6 %collective-permute-done.7.refs_3_ = f32[2,152,128]{2,1,0:T(8,128)S(1)} collective-permute-done((f32[2,152,128]{2,1,0:T(8,128)S(1)}, f32[2,152,128]{2,1,0:T(8,128)S(1)}, u32[]{:S(2)}, u32[]{:S(2)}) %collective-permute-start.7) | collective-permute-done | bytes 155680 | tf_op jit(solution)/shard_map/ppermute | solution.py:360
  17.3 2.9 %collective-permute-done.6.refs_2_ = f32[2,152,128]{2,1,0:T(8,128)S(1)} collective-permute-done((f32[2,152,128]{2,1,0:T(8,128)S(1)}, f32[2,152,128]{2,1,0:T(8,128)S(1)}, u32[]{:S(2)}, u32[]{:S(2)}) %collective-permute-start.6) | collective-permute-done | bytes 155680 | tf_op jit(solution)/shard_map/ppermute | solution.py:360
  20.3 1.5 %near1.1 = (f32[512,128]{1,0:T(8,128)S(1)}, f32[2,192,128]{2,1,0:T(8,128)S(1)}, f32[2,152,128]{2,1,0:T(8,128)S(1)}, f32[13,192,128]{2,1,0:T(8,128)S(1)}) custom-call(s32[4,128]{1,0:T(4,128)S(4)} %get-tuple-element.34.names, s32[6]{0:T(128)S(4)} %get-tuple-element.35.scalars, f32[512,128]{1,0:T(8,128)S(1)} %get-tuple-element.41.field, ...), custom_call_target="tpu_custom_call" | custom-call | flops 600000000 | bytes 4194304 | tf_op jit(solution)/shard_map/near1/pallas_call | solution.py:371
  21.8 0.5 %collective-permute-start.11 = (f32[2,152,128]{2,1,0:T(8,128)S(1)}, f32[2,152,128]{2,1,0:T(8,128)S(1)}, u32[]{:S(2)}, u32[]{:S(2)}) collective-permute-start(f32[2,152,128]{2,1,0:T(8,128)S(1)} %get-tuple-element.53.after), channel_id=1, source_target_pairs={{0,1},{1,0},{2,3},{3,2},{4,5},{5,4},{6,7},{7,6},{8,9},{9,8},{10,11... | collective-permute-start | bytes 466952 | tf_op jit(solution)/shard_map/ppermute | solution.py:360
  22.3 1.3 %collective-permute-start.10 = (f32[2,152,128]{2,1,0:T(8,128)S(1)}, f32[2,152,128]{2,1,0:T(8,128)S(1)}, u32[]{:S(2)}, u32[]{:S(2)}) collective-permute-start(f32[2,152,128]{2,1,0:T(8,128)S(1)} %get-tuple-element.53.after), channel_id=1, source_target_pairs={{0,1},{1,0},{2,3},{3,2},{4,8},{5,9},{6,10},{7,11},{8,4},{9,5},{10,... | collective-permute-start | bytes 466952 | tf_op jit(solution)/shard_map/ppermute | solution.py:360
  23.5 0.5 %collective-permute-start.8 = (f32[2,152,128]{2,1,0:T(8,128)S(1)}, f32[2,152,128]{2,1,0:T(8,128)S(1)}, u32[]{:S(2)}, u32[]{:S(2)}) collective-permute-start(f32[2,152,128]{2,1,0:T(8,128)S(1)} %get-tuple-element.53.after), channel_id=1, source_target_pairs={{0,4},{1,5},{2,6},{3,7},{4,0},{5,1},{6,2},{7,3},{8,12},{9,13},{10,... | collective-permute-start | bytes 466952 | tf_op jit(solution)/shard_map/ppermute | solution.py:360
  24.0 0.4 taps2.1.refs_4_.taps
  24.4 1.3 %far1.1 = (f32[512,128]{1,0:T(8,128)S(1)}, f32[2,192,128]{2,1,0:T(8,128)S(1)}) custom-call(s32[4,128]{1,0:T(4,128)S(4)} %get-tuple-element.34.names, s32[6]{0:T(128)S(4)} %get-tuple-element.35.scalars, f32[512,128]{1,0:T(8,128)S(1)} %get-tuple-element.50.field, f32[13,192,128]{2,1,0:T(8,128)S(1)} %get-tuple-element.51.table, ...), custom_call_target="tpu_custom_call" | custom-call | flops 600000000 | bytes 4194304 | tf_op jit(solution)/shard_map/far1/pallas_call | solution.py:371
  25.8 1.3 %collective-permute-done.11.refs_3_ = f32[2,152,128]{2,1,0:T(8,128)S(1)} collective-permute-done((f32[2,152,128]{2,1,0:T(8,128)S(1)}, f32[2,152,128]{2,1,0:T(8,128)S(1)}, u32[]{:S(2)}, u32[]{:S(2)}) %collective-permute-start.11) | collective-permute-done | bytes 155680 | tf_op jit(solution)/shard_map/ppermute | solution.py:360
  27.1 2.0 %collective-permute-done.10.refs_2_ = f32[2,152,128]{2,1,0:T(8,128)S(1)} collective-permute-done((f32[2,152,128]{2,1,0:T(8,128)S(1)}, f32[2,152,128]{2,1,0:T(8,128)S(1)}, u32[]{:S(2)}, u32[]{:S(2)}) %collective-permute-start.10) | collective-permute-done | bytes 155680 | tf_op jit(solution)/shard_map/ppermute | solution.py:360
  29.0 1.5 %near2.1 = (f32[512,128]{1,0:T(8,128)S(1)}, f32[2,192,128]{2,1,0:T(8,128)S(1)}, f32[2,152,128]{2,1,0:T(8,128)S(1)}, f32[13,192,128]{2,1,0:T(8,128)S(1)}) custom-call(s32[4,128]{1,0:T(4,128)S(4)} %get-tuple-element.34.names, s32[6]{0:T(128)S(4)} %get-tuple-element.35.scalars, f32[512,128]{1,0:T(8,128)S(1)} %get-tuple-element.48.field.refs_6_, ...), custom_call_target="tpu_custom_call" | custom-call | flops 600000000 | bytes 4194304 | tf_op jit(solution)/shard_map/near2/pallas_call | solution.py:371
  30.5 1.7 %collective-permute-start.15 = (f32[2,152,128]{2,1,0:T(8,128)S(1)}, f32[2,152,128]{2,1,0:T(8,128)S(1)}, u32[]{:S(2)}, u32[]{:S(2)}) collective-permute-start(f32[2,152,128]{2,1,0:T(8,128)S(1)} %get-tuple-element.60.after), channel_id=1, source_target_pairs={{0,1},{1,0},{2,3},{3,2},{4,5},{5,4},{6,7},{7,6},{8,9},{9,8},{10,11... | collective-permute-start | bytes 466952 | tf_op jit(solution)/shard_map/ppermute | solution.py:360
  32.2 0.9 %collective-permute-start.14 = (f32[2,152,128]{2,1,0:T(8,128)S(1)}, f32[2,152,128]{2,1,0:T(8,128)S(1)}, u32[]{:S(2)}, u32[]{:S(2)}) collective-permute-start(f32[2,152,128]{2,1,0:T(8,128)S(1)} %get-tuple-element.60.after), channel_id=1, source_target_pairs={{0,1},{1,0},{2,3},{3,2},{4,8},{5,9},{6,10},{7,11},{8,4},{9,5},{10,... | collective-permute-start | bytes 466952 | tf_op jit(solution)/shard_map/ppermute | solution.py:360
  33.1 0.5 %collective-permute-start.12 = (f32[2,152,128]{2,1,0:T(8,128)S(1)}, f32[2,152,128]{2,1,0:T(8,128)S(1)}, u32[]{:S(2)}, u32[]{:S(2)}) collective-permute-start(f32[2,152,128]{2,1,0:T(8,128)S(1)} %get-tuple-element.60.after), channel_id=1, source_target_pairs={{0,4},{1,5},{2,6},{3,7},{4,0},{5,1},{6,2},{7,3},{8,12},{9,13},{10,... | collective-permute-start | bytes 466952 | tf_op jit(solution)/shard_map/ppermute | solution.py:360
  33.6 0.4 taps3.1.refs_4_
  34.0 1.3 %far2.1 = (f32[512,128]{1,0:T(8,128)S(1)}, f32[2,192,128]{2,1,0:T(8,128)S(1)}) custom-call(s32[4,128]{1,0:T(4,128)S(4)} %get-tuple-element.34.names, s32[6]{0:T(128)S(4)} %get-tuple-element.35.scalars, f32[512,128]{1,0:T(8,128)S(1)} %get-tuple-element.55.field.refs_7_, f32[13,192,128]{2,1,0:T(8,128)S(1)} %get-tuple-element.56.table, ...), custom_call_target="tpu_custom_call" | custom-call | flops 600000000 | bytes 4194304 | tf_op jit(solution)/shard_map/far2/pallas_call | solution.py:371
  35.3 0.5 %collective-permute-done.15.refs_3_ = f32[2,152,128]{2,1,0:T(8,128)S(1)} collective-permute-done((f32[2,152,128]{2,1,0:T(8,128)S(1)}, f32[2,152,128]{2,1,0:T(8,128)S(1)}, u32[]{:S(2)}, u32[]{:S(2)}) %collective-permute-start.15) | collective-permute-done | bytes 155680 | tf_op jit(solution)/shard_map/ppermute | solution.py:360
  35.8 3.1 %collective-permute-done.14.refs_2_ = f32[2,152,128]{2,1,0:T(8,128)S(1)} collective-permute-done((f32[2,152,128]{2,1,0:T(8,128)S(1)}, f32[2,152,128]{2,1,0:T(8,128)S(1)}, u32[]{:S(2)}, u32[]{:S(2)}) %collective-permute-start.14) | collective-permute-done | bytes 155680 | tf_op jit(solution)/shard_map/ppermute | solution.py:360
  39.0 3.3 %last3.1 = f32[4,8,8,512]{3,2,1,0:T(8,128)} custom-call(s32[4,128]{1,0:T(4,128)S(4)} %get-tuple-element.34.names, s32[6]{0:T(128)S(4)} %get-tuple-element.35.scalars, f32[512,128]{1,0:T(8,128)S(1)} %get-tuple-element.54.field_a, f32[512,128]{1,0:T(8,128)S(1)} %get-tuple-element.57.field_b, f32[2,192,128]{2,1,0:T(8,128)S(1)} %get-tuple-element.58.faces_a, ...), custom_call_target="tpu_custom_call" | custom-call | flops 600000000 | bytes 4194304 | tf_op jit(solution)/shard_map/last3/pallas_call | solution.py:371
  (15 shorter events, 0.0 us)
Async XLA Ops:
  1.8 6.9 %collective-permute-start.3 = (f32[2,152,128]{2,1,0:T(8,128)S(1)}, f32[2,152,128]{2,1,0:T(8,128)S(1)}, u32[]{:S(2)}, u32[]{:S(2)}) collective-permute-start(f32[2,152,128]{2,1,0:T(8,128)S(1)} %get-tuple-element.33.after), channel_id=1, source_target_pairs={{0,1},{1,0},{2,3},{3,2},{4,5},{5,4},{6,7},{7,6},{8,9},{9,8},{10,11... | collective-permute-start | bytes 466952 | tf_op jit(solution)/shard_map/ppermute | solution.py:360
  3.4 6.8 %collective-permute-start.2 = (f32[2,152,128]{2,1,0:T(8,128)S(1)}, f32[2,152,128]{2,1,0:T(8,128)S(1)}, u32[]{:S(2)}, u32[]{:S(2)}) collective-permute-start(f32[2,152,128]{2,1,0:T(8,128)S(1)} %get-tuple-element.33.after), channel_id=1, source_target_pairs={{0,1},{1,0},{2,3},{3,2},{4,8},{5,9},{6,10},{7,11},{8,4},{9,5},{10,... | collective-permute-start | bytes 466952 | tf_op jit(solution)/shard_map/ppermute | solution.py:360
  5.4 4.8 %collective-permute-start.1 = (f32[2,152,128]{2,1,0:T(8,128)S(1)}, f32[2,152,128]{2,1,0:T(8,128)S(1)}, u32[]{:S(2)}, u32[]{:S(2)}) collective-permute-start(f32[2,152,128]{2,1,0:T(8,128)S(1)} %get-tuple-element.33.after), channel_id=1, source_target_pairs={{0,4},{1,2},{2,1},{3,7},{4,0},{5,6},{6,5},{7,3},{8,12},{9,10},{10,... | collective-permute-start | bytes 466952 | tf_op jit(solution)/shard_map/ppermute | solution.py:360
  5.4 4.8 %collective-permute-start = (f32[2,152,128]{2,1,0:T(8,128)S(1)}, f32[2,152,128]{2,1,0:T(8,128)S(1)}, u32[]{:S(2)}, u32[]{:S(2)}) collective-permute-start(f32[2,152,128]{2,1,0:T(8,128)S(1)} %get-tuple-element.33.after), channel_id=1, source_target_pairs={{0,4},{1,5},{2,6},{3,7},{4,0},{5,1},{6,2},{7,3},{8,12},{9,13},{10,... | collective-permute-start | bytes 466952 | tf_op jit(solution)/shard_map/ppermute | solution.py:360
  8.2 1.9 %copy-start = (f32[4,64]{1,0:T(4,128)S(1)}, f32[4,64]{1,0:T(4,128)}, u32[]{:S(2)}) copy-start(f32[4,64]{1,0:T(4,128)} %refs_5_.7) | copy-start | bytes 3076
  11.6 5.7 %collective-permute-start.7 = (f32[2,152,128]{2,1,0:T(8,128)S(1)}, f32[2,152,128]{2,1,0:T(8,128)S(1)}, u32[]{:S(2)}, u32[]{:S(2)}) collective-permute-start(f32[2,152,128]{2,1,0:T(8,128)S(1)} %get-tuple-element.46.after), channel_id=1, source_target_pairs={{0,1},{1,0},{2,3},{3,2},{4,5},{5,4},{6,7},{7,6},{8,9},{9,8},{10,11... | collective-permute-start | bytes 466952 | tf_op jit(solution)/shard_map/ppermute | solution.py:360
  13.5 6.8 %collective-permute-start.6 = (f32[2,152,128]{2,1,0:T(8,128)S(1)}, f32[2,152,128]{2,1,0:T(8,128)S(1)}, u32[]{:S(2)}, u32[]{:S(2)}) collective-permute-start(f32[2,152,128]{2,1,0:T(8,128)S(1)} %get-tuple-element.46.after), channel_id=1, source_target_pairs={{0,1},{1,0},{2,3},{3,2},{4,8},{5,9},{6,10},{7,11},{8,4},{9,5},{10,... | collective-permute-start | bytes 466952 | tf_op jit(solution)/shard_map/ppermute | solution.py:360
  14.5 5.8 %collective-permute-start.5 = (f32[2,152,128]{2,1,0:T(8,128)S(1)}, f32[2,152,128]{2,1,0:T(8,128)S(1)}, u32[]{:S(2)}, u32[]{:S(2)}) collective-permute-start(f32[2,152,128]{2,1,0:T(8,128)S(1)} %get-tuple-element.46.after), channel_id=1, source_target_pairs={{0,4},{1,2},{2,1},{3,7},{4,0},{5,6},{6,5},{7,3},{8,12},{9,10},{10,... | collective-permute-start | bytes 466952 | tf_op jit(solution)/shard_map/ppermute | solution.py:360
  14.5 5.8 %collective-permute-start.4 = (f32[2,152,128]{2,1,0:T(8,128)S(1)}, f32[2,152,128]{2,1,0:T(8,128)S(1)}, u32[]{:S(2)}, u32[]{:S(2)}) collective-permute-start(f32[2,152,128]{2,1,0:T(8,128)S(1)} %get-tuple-element.46.after), channel_id=1, source_target_pairs={{0,4},{1,5},{2,6},{3,7},{4,0},{5,1},{6,2},{7,3},{8,12},{9,13},{10,... | collective-permute-start | bytes 466952 | tf_op jit(solution)/shard_map/ppermute | solution.py:360
  21.8 5.3 %collective-permute-start.11 = (f32[2,152,128]{2,1,0:T(8,128)S(1)}, f32[2,152,128]{2,1,0:T(8,128)S(1)}, u32[]{:S(2)}, u32[]{:S(2)}) collective-permute-start(f32[2,152,128]{2,1,0:T(8,128)S(1)} %get-tuple-element.53.after), channel_id=1, source_target_pairs={{0,1},{1,0},{2,3},{3,2},{4,5},{5,4},{6,7},{7,6},{8,9},{9,8},{10,11... | collective-permute-start | bytes 466952 | tf_op jit(solution)/shard_map/ppermute | solution.py:360
  22.3 6.8 %collective-permute-start.10 = (f32[2,152,128]{2,1,0:T(8,128)S(1)}, f32[2,152,128]{2,1,0:T(8,128)S(1)}, u32[]{:S(2)}, u32[]{:S(2)}) collective-permute-start(f32[2,152,128]{2,1,0:T(8,128)S(1)} %get-tuple-element.53.after), channel_id=1, source_target_pairs={{0,1},{1,0},{2,3},{3,2},{4,8},{5,9},{6,10},{7,11},{8,4},{9,5},{10,... | collective-permute-start | bytes 466952 | tf_op jit(solution)/shard_map/ppermute | solution.py:360
  23.5 5.5 %collective-permute-start.9 = (f32[2,152,128]{2,1,0:T(8,128)S(1)}, f32[2,152,128]{2,1,0:T(8,128)S(1)}, u32[]{:S(2)}, u32[]{:S(2)}) collective-permute-start(f32[2,152,128]{2,1,0:T(8,128)S(1)} %get-tuple-element.53.after), channel_id=1, source_target_pairs={{0,4},{1,2},{2,1},{3,7},{4,0},{5,6},{6,5},{7,3},{8,12},{9,10},{10,... | collective-permute-start | bytes 466952 | tf_op jit(solution)/shard_map/ppermute | solution.py:360
  23.5 5.5 %collective-permute-start.8 = (f32[2,152,128]{2,1,0:T(8,128)S(1)}, f32[2,152,128]{2,1,0:T(8,128)S(1)}, u32[]{:S(2)}, u32[]{:S(2)}) collective-permute-start(f32[2,152,128]{2,1,0:T(8,128)S(1)} %get-tuple-element.53.after), channel_id=1, source_target_pairs={{0,4},{1,5},{2,6},{3,7},{4,0},{5,1},{6,2},{7,3},{8,12},{9,13},{10,... | collective-permute-start | bytes 466952 | tf_op jit(solution)/shard_map/ppermute | solution.py:360
  30.5 5.3 %collective-permute-start.15 = (f32[2,152,128]{2,1,0:T(8,128)S(1)}, f32[2,152,128]{2,1,0:T(8,128)S(1)}, u32[]{:S(2)}, u32[]{:S(2)}) collective-permute-start(f32[2,152,128]{2,1,0:T(8,128)S(1)} %get-tuple-element.60.after), channel_id=1, source_target_pairs={{0,1},{1,0},{2,3},{3,2},{4,5},{5,4},{6,7},{7,6},{8,9},{9,8},{10,11... | collective-permute-start | bytes 466952 | tf_op jit(solution)/shard_map/ppermute | solution.py:360
  32.2 6.8 %collective-permute-start.14 = (f32[2,152,128]{2,1,0:T(8,128)S(1)}, f32[2,152,128]{2,1,0:T(8,128)S(1)}, u32[]{:S(2)}, u32[]{:S(2)}) collective-permute-start(f32[2,152,128]{2,1,0:T(8,128)S(1)} %get-tuple-element.60.after), channel_id=1, source_target_pairs={{0,1},{1,0},{2,3},{3,2},{4,8},{5,9},{6,10},{7,11},{8,4},{9,5},{10,... | collective-permute-start | bytes 466952 | tf_op jit(solution)/shard_map/ppermute | solution.py:360
  33.1 5.9 %collective-permute-start.13 = (f32[2,152,128]{2,1,0:T(8,128)S(1)}, f32[2,152,128]{2,1,0:T(8,128)S(1)}, u32[]{:S(2)}, u32[]{:S(2)}) collective-permute-start(f32[2,152,128]{2,1,0:T(8,128)S(1)} %get-tuple-element.60.after), channel_id=1, source_target_pairs={{0,4},{1,2},{2,1},{3,7},{4,0},{5,6},{6,5},{7,3},{8,12},{9,10},{10,... | collective-permute-start | bytes 466952 | tf_op jit(solution)/shard_map/ppermute | solution.py:360
  33.1 5.9 %collective-permute-start.12 = (f32[2,152,128]{2,1,0:T(8,128)S(1)}, f32[2,152,128]{2,1,0:T(8,128)S(1)}, u32[]{:S(2)}, u32[]{:S(2)}) collective-permute-start(f32[2,152,128]{2,1,0:T(8,128)S(1)} %get-tuple-element.60.after), channel_id=1, source_target_pairs={{0,4},{1,5},{2,6},{3,7},{4,0},{5,1},{6,2},{7,3},{8,12},{9,13},{10,... | collective-permute-start | bytes 466952 | tf_op jit(solution)/shard_map/ppermute | solution.py:360

commit v7 on v6

--- a/solution.py
+++ b/solution.py
@@ -15,7 +15,7 @@
 SM = pl.BlockSpec(memory_space=pltpu.SMEM)
 HB = pl.BlockSpec(memory_space=pltpu.HBM)
 F32, BF16 = jnp.float32, jnp.bfloat16
-ORDER = [0, 3, 1, 2]
+ORDER = [3, 0, 2, 1]
 PLACE, SECOND, LIVE = 0, 4, 5
 
 

time: 42.6 us -> 44.3 us (1.040)
  the two profiles are of different devices: /device:TPU:96 before, /device:TPU:4 now
where the time goes in v7:
time: 44.3 us; the launch traced here: 44.1 us
  Pallas kernels  16.7 us (38%)
  waiting for transfers between devices  15.9 us (36%)
  starting transfers between devices  10.6 us (24%)
  between operations  0.92 us (2%)
    pallas_call x13, Pallas kernels, call(): pl.pallas_call(kernel, out_shape=out_shape, in_specs=in_specs, out_specs=...  16.7 us
    ppermute x16, waiting for transfers between devices, exchange(): lax.ppermute(send, ('space', 'slab'), swaps(at // 2, at % 2))  15.9 us
    ppermute x16, starting transfers between devices, exchange(): lax.ppermute(send, ('space', 'slab'), swaps(at // 2, at % 2))  10.6 us
  transfers between devices with their start and end apart: 16, of which 10 were waited for; matrix products, arithmetic and copies ran while one was open for 0% of the time, Pallas kernels for 18%

profile of v7, /device:TPU:4, one launch (start us, length us, event | category | flops | bytes accessed | tf_op | source)
XLA Modules:
  0.0 44.1 jit_solution(12573412044513938982)
XLA Ops:
  0.7 1.2 %entry.1 = (f32[512,128]{1,0:T(8,128)S(1)}, f32[2,192,128]{2,1,0:T(8,128)S(1)}, f32[2,152,128]{2,1,0:T(8,128)S(1)}) custom-call(s32[1]{0:T(128)S(6)} %copy.7.live, s32[1,2]{1,0:T(1,128)} %slots.3, f32[4,8,8,512]{3,2,1,0:T(8,128)} %feat.3), custom_call_target="tpu_custom_call" | custom-call | flops 600000000 | bytes 4194304 | tf_op jit(solution)/shard_map/entry/pallas_call | solution.py:371
  1.8 1.3 %collective-permute-start.3 = (f32[2,152,128]{2,1,0:T(8,128)S(1)}, f32[2,152,128]{2,1,0:T(8,128)S(1)}, u32[]{:S(2)}, u32[]{:S(2)}) collective-permute-start(f32[2,152,128]{2,1,0:T(8,128)S(1)} %get-tuple-element.33.after), channel_id=1, source_target_pairs={{0,1},{1,0},{2,3},{3,2},{4,8},{5,9},{6,10},{7,11},{8,4},{9,5},{10,... | collective-permute-start | bytes 466952 | tf_op jit(solution)/shard_map/ppermute | solution.py:360
  3.1 0.8 %collective-permute-start.2 = (f32[2,152,128]{2,1,0:T(8,128)S(1)}, f32[2,152,128]{2,1,0:T(8,128)S(1)}, u32[]{:S(2)}, u32[]{:S(2)}) collective-permute-start(f32[2,152,128]{2,1,0:T(8,128)S(1)} %get-tuple-element.33.after), channel_id=1, source_target_pairs={{0,1},{1,0},{2,3},{3,2},{4,5},{5,4},{6,7},{7,6},{8,9},{9,8},{10,11... | collective-permute-start | bytes 466952 | tf_op jit(solution)/shard_map/ppermute | solution.py:360
  3.9 0.6 %collective-permute-start.1 = (f32[2,152,128]{2,1,0:T(8,128)S(1)}, f32[2,152,128]{2,1,0:T(8,128)S(1)}, u32[]{:S(2)}, u32[]{:S(2)}) collective-permute-start(f32[2,152,128]{2,1,0:T(8,128)S(1)} %get-tuple-element.33.after), channel_id=1, source_target_pairs={{0,4},{1,5},{2,6},{3,7},{4,0},{5,1},{6,2},{7,3},{8,12},{9,13},{10,... | collective-permute-start | bytes 466952 | tf_op jit(solution)/shard_map/ppermute | solution.py:360
  4.5 2.3 %second_entry.1 = (f32[512,128]{1,0:T(8,128)S(1)}, f32[2,192,128]{2,1,0:T(8,128)S(1)}, f32[27,4,4096]{2,1,0:T(4,128)S(1)}, s32[4,128]{1,0:T(4,128)S(4)}, s32[6]{0:T(128)S(4)}) custom-call(f32[2,152,128]{2,1,0:T(8,128)S(1)} %get-tuple-element.33.after, s32[1]{0:T(128)S(6)} %copy.7.live, s32[1,2]{1,0:T(1,128)} %slots.3, f32[4,8,8,512]{3,2,1,0:T(8,128)} %feat.3, ...), custom_call_target="tpu_custom_call" | custom-call | flops 600000000 | bytes 4194304 | tf_op jit(solution)/shard_map/second_entry/pallas_call | solution.py:371
  6.8 0.4 taps0.1
  7.3 0.8 %collective-permute-done.3.refs_3_ = f32[2,152,128]{2,1,0:T(8,128)S(1)} collective-permute-done((f32[2,152,128]{2,1,0:T(8,128)S(1)}, f32[2,152,128]{2,1,0:T(8,128)S(1)}, u32[]{:S(2)}, u32[]{:S(2)}) %collective-permute-start.3) | collective-permute-done | bytes 155680 | tf_op jit(solution)/shard_map/ppermute | solution.py:360
  8.1 2.3 %collective-permute-done.2.refs_2_ = f32[2,152,128]{2,1,0:T(8,128)S(1)} collective-permute-done((f32[2,152,128]{2,1,0:T(8,128)S(1)}, f32[2,152,128]{2,1,0:T(8,128)S(1)}, u32[]{:S(2)}, u32[]{:S(2)}) %collective-permute-start.2) | collective-permute-done | bytes 155680 | tf_op jit(solution)/shard_map/ppermute | solution.py:360
  10.5 1.5 %near0.1 = (f32[512,128]{1,0:T(8,128)S(1)}, f32[2,192,128]{2,1,0:T(8,128)S(1)}, f32[2,152,128]{2,1,0:T(8,128)S(1)}, f32[13,192,128]{2,1,0:T(8,128)S(1)}) custom-call(s32[4,128]{1,0:T(4,128)S(4)} %get-tuple-element.34.names, s32[6]{0:T(128)S(4)} %get-tuple-element.35.scalars, f32[512,128]{1,0:T(8,128)S(1)} %get-tuple-element.36.field.refs_6_, ...), custom_call_target="tpu_custom_call" | custom-call | flops 600000000 | bytes 4194304 | tf_op jit(solution)/shard_map/near0/pallas_call | solution.py:371
  12.0 1.3 %collective-permute-start.7 = (f32[2,152,128]{2,1,0:T(8,128)S(1)}, f32[2,152,128]{2,1,0:T(8,128)S(1)}, u32[]{:S(2)}, u32[]{:S(2)}) collective-permute-start(f32[2,152,128]{2,1,0:T(8,128)S(1)} %get-tuple-element.46.after), channel_id=1, source_target_pairs={{0,1},{1,0},{2,3},{3,2},{4,8},{5,9},{6,10},{7,11},{8,4},{9,5},{10,... | collective-permute-start | bytes 466952 | tf_op jit(solution)/shard_map/ppermute | solution.py:360
  13.2 0.8 %collective-permute-start.6 = (f32[2,152,128]{2,1,0:T(8,128)S(1)}, f32[2,152,128]{2,1,0:T(8,128)S(1)}, u32[]{:S(2)}, u32[]{:S(2)}) collective-permute-start(f32[2,152,128]{2,1,0:T(8,128)S(1)} %get-tuple-element.46.after), channel_id=1, source_target_pairs={{0,1},{1,0},{2,3},{3,2},{4,5},{5,4},{6,7},{7,6},{8,9},{9,8},{10,11... | collective-permute-start | bytes 466952 | tf_op jit(solution)/shard_map/ppermute | solution.py:360
  14.1 0.5 %collective-permute-start.4 = (f32[2,152,128]{2,1,0:T(8,128)S(1)}, f32[2,152,128]{2,1,0:T(8,128)S(1)}, u32[]{:S(2)}, u32[]{:S(2)}) collective-permute-start(f32[2,152,128]{2,1,0:T(8,128)S(1)} %get-tuple-element.46.after), channel_id=1, source_target_pairs={{0,4},{1,2},{2,1},{3,7},{4,0},{5,6},{6,5},{7,3},{8,12},{9,10},{10,... | collective-permute-start | bytes 466952 | tf_op jit(solution)/shard_map/ppermute | solution.py:360
  14.6 0.4 taps1.1.refs_4_.taps
  15.0 1.3 %far0.1 = (f32[512,128]{1,0:T(8,128)S(1)}, f32[2,192,128]{2,1,0:T(8,128)S(1)}) custom-call(s32[4,128]{1,0:T(4,128)S(4)} %get-tuple-element.34.names, s32[6]{0:T(128)S(4)} %get-tuple-element.35.scalars, f32[512,128]{1,0:T(8,128)S(1)} %get-tuple-element.43.field.refs_0_, f32[13,192,128]{2,1,0:T(8,128)S(1)} %get-tuple-element.44.table, ...), custom_call_target="tpu_custom_call" | custom-call | flops 600000000 | bytes 4194304 | tf_op jit(solution)/shard_map/far0/pallas_call | solution.py:371
  16.3 2.0 %collective-permute-done.7.refs_3_ = f32[2,152,128]{2,1,0:T(8,128)S(1)} collective-permute-done((f32[2,152,128]{2,1,0:T(8,128)S(1)}, f32[2,152,128]{2,1,0:T(8,128)S(1)}, u32[]{:S(2)}, u32[]{:S(2)}) %collective-permute-start.7) | collective-permute-done | bytes 155680 | tf_op jit(solution)/shard_map/ppermute | solution.py:360
  18.3 2.3 %collective-permute-done.6.refs_2_ = f32[2,152,128]{2,1,0:T(8,128)S(1)} collective-permute-done((f32[2,152,128]{2,1,0:T(8,128)S(1)}, f32[2,152,128]{2,1,0:T(8,128)S(1)}, u32[]{:S(2)}, u32[]{:S(2)}) %collective-permute-start.6) | collective-permute-done | bytes 155680 | tf_op jit(solution)/shard_map/ppermute | solution.py:360
  20.6 1.5 %near1.1 = (f32[512,128]{1,0:T(8,128)S(1)}, f32[2,192,128]{2,1,0:T(8,128)S(1)}, f32[2,152,128]{2,1,0:T(8,128)S(1)}, f32[13,192,128]{2,1,0:T(8,128)S(1)}) custom-call(s32[4,128]{1,0:T(4,128)S(4)} %get-tuple-element.34.names, s32[6]{0:T(128)S(4)} %get-tuple-element.35.scalars, f32[512,128]{1,0:T(8,128)S(1)} %get-tuple-element.41.field, ...), custom_call_target="tpu_custom_call" | custom-call | flops 600000000 | bytes 4194304 | tf_op jit(solution)/shard_map/near1/pallas_call | solution.py:371
  22.1 1.0 %collective-permute-start.11 = (f32[2,152,128]{2,1,0:T(8,128)S(1)}, f32[2,152,128]{2,1,0:T(8,128)S(1)}, u32[]{:S(2)}, u32[]{:S(2)}) collective-permute-start(f32[2,152,128]{2,1,0:T(8,128)S(1)} %get-tuple-element.53.after), channel_id=1, source_target_pairs={{0,1},{1,0},{2,3},{3,2},{4,8},{5,9},{6,10},{7,11},{8,4},{9,5},{10,... | collective-permute-start | bytes 466952 | tf_op jit(solution)/shard_map/ppermute | solution.py:360
  23.1 1.1 %collective-permute-start.10 = (f32[2,152,128]{2,1,0:T(8,128)S(1)}, f32[2,152,128]{2,1,0:T(8,128)S(1)}, u32[]{:S(2)}, u32[]{:S(2)}) collective-permute-start(f32[2,152,128]{2,1,0:T(8,128)S(1)} %get-tuple-element.53.after), channel_id=1, source_target_pairs={{0,1},{1,0},{2,3},{3,2},{4,5},{5,4},{6,7},{7,6},{8,9},{9,8},{10,11... | collective-permute-start | bytes 466952 | tf_op jit(solution)/shard_map/ppermute | solution.py:360
  24.2 0.5 %collective-permute-start.8 = (f32[2,152,128]{2,1,0:T(8,128)S(1)}, f32[2,152,128]{2,1,0:T(8,128)S(1)}, u32[]{:S(2)}, u32[]{:S(2)}) collective-permute-start(f32[2,152,128]{2,1,0:T(8,128)S(1)} %get-tuple-element.53.after), channel_id=1, source_target_pairs={{0,4},{1,2},{2,1},{3,7},{4,0},{5,6},{6,5},{7,3},{8,12},{9,10},{10,... | collective-permute-start | bytes 466952 | tf_op jit(solution)/shard_map/ppermute | solution.py:360
  25.1 1.3 %far1.1 = (f32[512,128]{1,0:T(8,128)S(1)}, f32[2,192,128]{2,1,0:T(8,128)S(1)}) custom-call(s32[4,128]{1,0:T(4,128)S(4)} %get-tuple-element.34.names, s32[6]{0:T(128)S(4)} %get-tuple-element.35.scalars, f32[512,128]{1,0:T(8,128)S(1)} %get-tuple-element.50.field, f32[13,192,128]{2,1,0:T(8,128)S(1)} %get-tuple-element.51.table, ...), custom_call_target="tpu_custom_call" | custom-call | flops 600000000 | bytes 4194304 | tf_op jit(solution)/shard_map/far1/pallas_call | solution.py:371
  26.4 2.1 %collective-permute-done.11.refs_3_ = f32[2,152,128]{2,1,0:T(8,128)S(1)} collective-permute-done((f32[2,152,128]{2,1,0:T(8,128)S(1)}, f32[2,152,128]{2,1,0:T(8,128)S(1)}, u32[]{:S(2)}, u32[]{:S(2)}) %collective-permute-start.11) | collective-permute-done | bytes 155680 | tf_op jit(solution)/shard_map/ppermute | solution.py:360
  28.5 1.7 %collective-permute-done.10.refs_2_ = f32[2,152,128]{2,1,0:T(8,128)S(1)} collective-permute-done((f32[2,152,128]{2,1,0:T(8,128)S(1)}, f32[2,152,128]{2,1,0:T(8,128)S(1)}, u32[]{:S(2)}, u32[]{:S(2)}) %collective-permute-start.10) | collective-permute-done | bytes 155680 | tf_op jit(solution)/shard_map/ppermute | solution.py:360
  30.2 0.4 collective-permute-done.8.refs_0_
  30.6 1.5 %near2.1 = (f32[512,128]{1,0:T(8,128)S(1)}, f32[2,192,128]{2,1,0:T(8,128)S(1)}, f32[2,152,128]{2,1,0:T(8,128)S(1)}, f32[13,192,128]{2,1,0:T(8,128)S(1)}) custom-call(s32[4,128]{1,0:T(4,128)S(4)} %get-tuple-element.34.names, s32[6]{0:T(128)S(4)} %get-tuple-element.35.scalars, f32[512,128]{1,0:T(8,128)S(1)} %get-tuple-element.48.field.refs_6_, ...), custom_call_target="tpu_custom_call" | custom-call | flops 600000000 | bytes 4194304 | tf_op jit(solution)/shard_map/near2/pallas_call | solution.py:371
  32.2 2.0 %collective-permute-start.14 = (f32[2,152,128]{2,1,0:T(8,128)S(1)}, f32[2,152,128]{2,1,0:T(8,128)S(1)}, u32[]{:S(2)}, u32[]{:S(2)}) collective-permute-start(f32[2,152,128]{2,1,0:T(8,128)S(1)} %get-tuple-element.60.after), channel_id=1, source_target_pairs={{0,1},{1,0},{2,3},{3,2},{4,5},{5,4},{6,7},{7,6},{8,9},{9,8},{10,11... | collective-permute-start | bytes 466952 | tf_op jit(solution)/shard_map/ppermute | solution.py:360
  34.2 0.5 %collective-permute-start.12 = (f32[2,152,128]{2,1,0:T(8,128)S(1)}, f32[2,152,128]{2,1,0:T(8,128)S(1)}, u32[]{:S(2)}, u32[]{:S(2)}) collective-permute-start(f32[2,152,128]{2,1,0:T(8,128)S(1)} %get-tuple-element.60.after), channel_id=1, source_target_pairs={{0,4},{1,2},{2,1},{3,7},{4,0},{5,6},{6,5},{7,3},{8,12},{9,10},{10,... | collective-permute-start | bytes 466952 | tf_op jit(solution)/shard_map/ppermute | solution.py:360
  35.1 1.3 %far2.1 = (f32[512,128]{1,0:T(8,128)S(1)}, f32[2,192,128]{2,1,0:T(8,128)S(1)}) custom-call(s32[4,128]{1,0:T(4,128)S(4)} %get-tuple-element.34.names, s32[6]{0:T(128)S(4)} %get-tuple-element.35.scalars, f32[512,128]{1,0:T(8,128)S(1)} %get-tuple-element.55.field.refs_7_, f32[13,192,128]{2,1,0:T(8,128)S(1)} %get-tuple-element.56.table, ...), custom_call_target="tpu_custom_call" | custom-call | flops 600000000 | bytes 4194304 | tf_op jit(solution)/shard_map/far2/pallas_call | solution.py:371
  36.5 1.7 %collective-permute-done.15.refs_3_ = f32[2,152,128]{2,1,0:T(8,128)S(1)} collective-permute-done((f32[2,152,128]{2,1,0:T(8,128)S(1)}, f32[2,152,128]{2,1,0:T(8,128)S(1)}, u32[]{:S(2)}, u32[]{:S(2)}) %collective-permute-start.15) | collective-permute-done | bytes 155680 | tf_op jit(solution)/shard_map/ppermute | solution.py:360
  38.1 1.7 %collective-permute-done.14.refs_2_ = f32[2,152,128]{2,1,0:T(8,128)S(1)} collective-permute-done((f32[2,152,128]{2,1,0:T(8,128)S(1)}, f32[2,152,128]{2,1,0:T(8,128)S(1)}, u32[]{:S(2)}, u32[]{:S(2)}) %collective-permute-start.14) | collective-permute-done | bytes 155680 | tf_op jit(solution)/shard_map/ppermute | solution.py:360
  39.8 0.9 %collective-permute-done.12.refs_0_ = f32[2,152,128]{2,1,0:T(8,128)S(1)} collective-permute-done((f32[2,152,128]{2,1,0:T(8,128)S(1)}, f32[2,152,128]{2,1,0:T(8,128)S(1)}, u32[]{:S(2)}, u32[]{:S(2)}) %collective-permute-start.12) | collective-permute-done | bytes 155680 | tf_op jit(solution)/shard_map/ppermute | solution.py:360
  40.7 3.3 %last3.1 = f32[4,8,8,512]{3,2,1,0:T(8,128)} custom-call(s32[4,128]{1,0:T(4,128)S(4)} %get-tuple-element.34.names, s32[6]{0:T(128)S(4)} %get-tuple-element.35.scalars, f32[512,128]{1,0:T(8,128)S(1)} %get-tuple-element.54.field_a, f32[512,128]{1,0:T(8,128)S(1)} %get-tuple-element.57.field_b, f32[2,192,128]{2,1,0:T(8,128)S(1)} %get-tuple-element.58.faces_a, ...), custom_call_target="tpu_custom_call" | custom-call | flops 600000000 | bytes 4194304 | tf_op jit(solution)/shard_map/last3/pallas_call | solution.py:371
  (15 shorter events, 0.8 us)
Async XLA Ops:
  1.8 6.3 %collective-permute-start.3 = (f32[2,152,128]{2,1,0:T(8,128)S(1)}, f32[2,152,128]{2,1,0:T(8,128)S(1)}, u32[]{:S(2)}, u32[]{:S(2)}) collective-permute-start(f32[2,152,128]{2,1,0:T(8,128)S(1)} %get-tuple-element.33.after), channel_id=1, source_target_pairs={{0,1},{1,0},{2,3},{3,2},{4,8},{5,9},{6,10},{7,11},{8,4},{9,5},{10,... | collective-permute-start | bytes 466952 | tf_op jit(solution)/shard_map/ppermute | solution.py:360
  3.1 7.4 %collective-permute-start.2 = (f32[2,152,128]{2,1,0:T(8,128)S(1)}, f32[2,152,128]{2,1,0:T(8,128)S(1)}, u32[]{:S(2)}, u32[]{:S(2)}) collective-permute-start(f32[2,152,128]{2,1,0:T(8,128)S(1)} %get-tuple-element.33.after), channel_id=1, source_target_pairs={{0,1},{1,0},{2,3},{3,2},{4,5},{5,4},{6,7},{7,6},{8,9},{9,8},{10,11... | collective-permute-start | bytes 466952 | tf_op jit(solution)/shard_map/ppermute | solution.py:360
  3.9 6.5 %collective-permute-start.1 = (f32[2,152,128]{2,1,0:T(8,128)S(1)}, f32[2,152,128]{2,1,0:T(8,128)S(1)}, u32[]{:S(2)}, u32[]{:S(2)}) collective-permute-start(f32[2,152,128]{2,1,0:T(8,128)S(1)} %get-tuple-element.33.after), channel_id=1, source_target_pairs={{0,4},{1,5},{2,6},{3,7},{4,0},{5,1},{6,2},{7,3},{8,12},{9,13},{10,... | collective-permute-start | bytes 466952 | tf_op jit(solution)/shard_map/ppermute | solution.py:360
  4.5 6.0 %collective-permute-start = (f32[2,152,128]{2,1,0:T(8,128)S(1)}, f32[2,152,128]{2,1,0:T(8,128)S(1)}, u32[]{:S(2)}, u32[]{:S(2)}) collective-permute-start(f32[2,152,128]{2,1,0:T(8,128)S(1)} %get-tuple-element.33.after), channel_id=1, source_target_pairs={{0,4},{1,2},{2,1},{3,7},{4,0},{5,6},{6,5},{7,3},{8,12},{9,10},{10,... | collective-permute-start | bytes 466952 | tf_op jit(solution)/shard_map/ppermute | solution.py:360
  6.8 3.6 %copy-start = (f32[4,64]{1,0:T(4,128)S(1)}, f32[4,64]{1,0:T(4,128)}, u32[]{:S(2)}) copy-start(f32[4,64]{1,0:T(4,128)} %refs_5_.7) | copy-start | bytes 3076
  12.0 6.3 %collective-permute-start.7 = (f32[2,152,128]{2,1,0:T(8,128)S(1)}, f32[2,152,128]{2,1,0:T(8,128)S(1)}, u32[]{:S(2)}, u32[]{:S(2)}) collective-permute-start(f32[2,152,128]{2,1,0:T(8,128)S(1)} %get-tuple-element.46.after), channel_id=1, source_target_pairs={{0,1},{1,0},{2,3},{3,2},{4,8},{5,9},{6,10},{7,11},{8,4},{9,5},{10,... | collective-permute-start | bytes 466952 | tf_op jit(solution)/shard_map/ppermute | solution.py:360
  13.2 7.4 %collective-permute-start.6 = (f32[2,152,128]{2,1,0:T(8,128)S(1)}, f32[2,152,128]{2,1,0:T(8,128)S(1)}, u32[]{:S(2)}, u32[]{:S(2)}) collective-permute-start(f32[2,152,128]{2,1,0:T(8,128)S(1)} %get-tuple-element.46.after), channel_id=1, source_target_pairs={{0,1},{1,0},{2,3},{3,2},{4,5},{5,4},{6,7},{7,6},{8,9},{9,8},{10,11... | collective-permute-start | bytes 466952 | tf_op jit(solution)/shard_map/ppermute | solution.py:360
  14.1 6.5 %collective-permute-start.5 = (f32[2,152,128]{2,1,0:T(8,128)S(1)}, f32[2,152,128]{2,1,0:T(8,128)S(1)}, u32[]{:S(2)}, u32[]{:S(2)}) collective-permute-start(f32[2,152,128]{2,1,0:T(8,128)S(1)} %get-tuple-element.46.after), channel_id=1, source_target_pairs={{0,4},{1,5},{2,6},{3,7},{4,0},{5,1},{6,2},{7,3},{8,12},{9,13},{10,... | collective-permute-start | bytes 466952 | tf_op jit(solution)/shard_map/ppermute | solution.py:360
  14.1 6.5 %collective-permute-start.4 = (f32[2,152,128]{2,1,0:T(8,128)S(1)}, f32[2,152,128]{2,1,0:T(8,128)S(1)}, u32[]{:S(2)}, u32[]{:S(2)}) collective-permute-start(f32[2,152,128]{2,1,0:T(8,128)S(1)} %get-tuple-element.46.after), channel_id=1, source_target_pairs={{0,4},{1,2},{2,1},{3,7},{4,0},{5,6},{6,5},{7,3},{8,12},{9,10},{10,... | collective-permute-start | bytes 466952 | tf_op jit(solution)/shard_map/ppermute | solution.py:360
  22.1 6.4 %collective-permute-start.11 = (f32[2,152,128]{2,1,0:T(8,128)S(1)}, f32[2,152,128]{2,1,0:T(8,128)S(1)}, u32[]{:S(2)}, u32[]{:S(2)}) collective-permute-start(f32[2,152,128]{2,1,0:T(8,128)S(1)} %get-tuple-element.53.after), channel_id=1, source_target_pairs={{0,1},{1,0},{2,3},{3,2},{4,8},{5,9},{6,10},{7,11},{8,4},{9,5},{10,... | collective-permute-start | bytes 466952 | tf_op jit(solution)/shard_map/ppermute | solution.py:360
  23.1 7.1 %collective-permute-start.10 = (f32[2,152,128]{2,1,0:T(8,128)S(1)}, f32[2,152,128]{2,1,0:T(8,128)S(1)}, u32[]{:S(2)}, u32[]{:S(2)}) collective-permute-start(f32[2,152,128]{2,1,0:T(8,128)S(1)} %get-tuple-element.53.after), channel_id=1, source_target_pairs={{0,1},{1,0},{2,3},{3,2},{4,5},{5,4},{6,7},{7,6},{8,9},{9,8},{10,11... | collective-permute-start | bytes 466952 | tf_op jit(solution)/shard_map/ppermute | solution.py:360
  24.2 6.0 %collective-permute-start.9 = (f32[2,152,128]{2,1,0:T(8,128)S(1)}, f32[2,152,128]{2,1,0:T(8,128)S(1)}, u32[]{:S(2)}, u32[]{:S(2)}) collective-permute-start(f32[2,152,128]{2,1,0:T(8,128)S(1)} %get-tuple-element.53.after), channel_id=1, source_target_pairs={{0,4},{1,5},{2,6},{3,7},{4,0},{5,1},{6,2},{7,3},{8,12},{9,13},{10,... | collective-permute-start | bytes 466952 | tf_op jit(solution)/shard_map/ppermute | solution.py:360
  24.2 6.4 %collective-permute-start.8 = (f32[2,152,128]{2,1,0:T(8,128)S(1)}, f32[2,152,128]{2,1,0:T(8,128)S(1)}, u32[]{:S(2)}, u32[]{:S(2)}) collective-permute-start(f32[2,152,128]{2,1,0:T(8,128)S(1)} %get-tuple-element.53.after), channel_id=1, source_target_pairs={{0,4},{1,2},{2,1},{3,7},{4,0},{5,6},{6,5},{7,3},{8,12},{9,10},{10,... | collective-permute-start | bytes 466952 | tf_op jit(solution)/shard_map/ppermute | solution.py:360
  32.1 6.0 %collective-permute-start.15 = (f32[2,152,128]{2,1,0:T(8,128)S(1)}, f32[2,152,128]{2,1,0:T(8,128)S(1)}, u32[]{:S(2)}, u32[]{:S(2)}) collective-permute-start(f32[2,152,128]{2,1,0:T(8,128)S(1)} %get-tuple-element.60.after), channel_id=1, source_target_pairs={{0,1},{1,0},{2,3},{3,2},{4,8},{5,9},{6,10},{7,11},{8,4},{9,5},{10,... | collective-permute-start | bytes 466952 | tf_op jit(solution)/shard_map/ppermute | solution.py:360
  32.2 7.6 %collective-permute-start.14 = (f32[2,152,128]{2,1,0:T(8,128)S(1)}, f32[2,152,128]{2,1,0:T(8,128)S(1)}, u32[]{:S(2)}, u32[]{:S(2)}) collective-permute-start(f32[2,152,128]{2,1,0:T(8,128)S(1)} %get-tuple-element.60.after), channel_id=1, source_target_pairs={{0,1},{1,0},{2,3},{3,2},{4,5},{5,4},{6,7},{7,6},{8,9},{9,8},{10,11... | collective-permute-start | bytes 466952 | tf_op jit(solution)/shard_map/ppermute | solution.py:360
  34.2 5.6 %collective-permute-start.13 = (f32[2,152,128]{2,1,0:T(8,128)S(1)}, f32[2,152,128]{2,1,0:T(8,128)S(1)}, u32[]{:S(2)}, u32[]{:S(2)}) collective-permute-start(f32[2,152,128]{2,1,0:T(8,128)S(1)} %get-tuple-element.60.after), channel_id=1, source_target_pairs={{0,4},{1,5},{2,6},{3,7},{4,0},{5,1},{6,2},{7,3},{8,12},{9,13},{10,... | collective-permute-start | bytes 466952 | tf_op jit(solution)/shard_map/ppermute | solution.py:360
  34.2 6.4 %collective-permute-start.12 = (f32[2,152,128]{2,1,0:T(8,128)S(1)}, f32[2,152,128]{2,1,0:T(8,128)S(1)}, u32[]{:S(2)}, u32[]{:S(2)}) collective-permute-start(f32[2,152,128]{2,1,0:T(8,128)S(1)} %get-tuple-element.60.after), channel_id=1, source_target_pairs={{0,4},{1,2},{2,1},{3,7},{4,0},{5,6},{6,5},{7,3},{8,12},{9,10},{10,... | collective-permute-start | bytes 466952 | tf_op jit(solution)/shard_map/ppermute | solution.py:360
